TPU v7x, 32 devices: a whole 2x2x4 slice. The times are simulated.
32 devices in a mesh: dp: 4 (over y, core), seq: 8 (over z, x).
Axes of the slice: x: 2, y: 2, z: 4, core: 2. Of those that a mesh axis runs over, the one named last changes fastest.
Arguments:
- queries: bfloat16 [4, 1024, 1152], P('dp', 'seq'), may hold values from -12 to 12
- keys: bfloat16 [4, 1024, 1152], P('dp', 'seq'), may hold values from -12 to 12
- values: bfloat16 [4, 1024, 1152], P('dp', 'seq'), may hold values from -6 to 6
- out_weight: bfloat16 [1152, 1152], replicated, may hold values from -0.1875 to 0.1875
- out_grad: bfloat16 [4, 1024, 1152], P('dp', 'seq'), may hold values from -48 to 48
- lengths: int32 [4, 4], P('dp'), may hold values from 128 to 384, as said below
Outputs:
- query_grad: float32 [4, 1024, 1152], P('dp', 'seq')
- key_grad: float32 [4, 1024, 1152], P('dp', 'seq')
- value_grad: float32 [4, 1024, 1152], P('dp', 'seq')
- weight_grad: float32 [1152, 1152], P('seq')
Inputs may be any that keep to these rules, and one draw needn't show every extreme that they name: Each row's 4 lengths sum to 1024; the largest in each row is exactly 384.
All inputs are finite; a program needn't handle non-finite values.
Results may differ from a plain program's by a relative error of at most 0.012.
The roundings to bfloat16 on the way count: a program that leaves them out, or rounds other values in their place, can miss the bound.
Values may be sent and summed in bfloat16 or wider, within the bound.
No kernel may reach another device: no remote copies, remote signals or barrier semaphores. Data moves between devices by JAX's collectives and lax.ppermute only.
A program may use at most 128 MiB of HBM per device.

v0:
```python
import math

import jax
import jax.numpy as jnp
from jax import lax
from jax.sharding import PartitionSpec as P

HEADS = 16
HEAD_DIM = 72
MAXLEN = 384


NEG_FILL = -1e30


def shifted(block, axis, distance):
    devices = range(lax.axis_size(axis))
    route = [(i - distance, i) for i in devices if i - distance in devices]
    return lax.ppermute(block, axis, route)


def split_heads(rows_in):
    return rows_in.reshape(rows_in.shape[0], HEADS, HEAD_DIM)


def image_ids(image_ends, shard, tok_rows, shards):
    positions = shard * tok_rows + jnp.arange(tok_rows, dtype=jnp.int32)
    found = jnp.sum((positions[:, None] >= image_ends[None, :]).astype(jnp.int32), axis=1)
    inside = jnp.logical_and(shard >= 0, shard < shards)
    return jnp.where(inside, found, -1)


def masked_scores(q_rows, k_rows, q_ids, k_ids):
    scores = jnp.einsum(
        "qhd,khd->hqk", split_heads(q_rows), split_heads(k_rows), preferred_element_type=jnp.float32
    ) * HEAD_DIM ** (-0.5)
    same_image = q_ids[:, None] == k_ids[None, :]
    return jnp.where(same_image[None, :, :], scores, NEG_FILL)


def touches(q_ids, k_ids):
    return jnp.any(q_ids[:, None] == k_ids[None, :])


def make_probs(q_rows, k_rows, q_ids, k_ids, log_norm):
    return jnp.exp(masked_scores(q_rows, k_rows, q_ids, k_ids) - log_norm[:, :, None]).astype(
        jnp.bfloat16
    )


def score_grads(q_rows, k_rows, v_rows, d_rows, q_ids, k_ids, log_norm, row_delta):
    weights = make_probs(q_rows, k_rows, q_ids, k_ids, log_norm)
    d_probs = jnp.einsum(
        "qhd,khd->hqk", split_heads(d_rows), split_heads(v_rows), preferred_element_type=jnp.float32
    )
    d_scores = (
        HEAD_DIM ** (-0.5) * weights.astype(jnp.float32) * (d_probs - row_delta[:, :, None])
    ).astype(jnp.bfloat16)
    return (weights, d_scores)


def query_part(d_scores, k_rows):
    return jnp.einsum(
        "hqk,khd->qhd", d_scores, split_heads(k_rows), preferred_element_type=jnp.float32
    )


def key_part(weights, d_scores, q_rows, d_rows):
    k_part = jnp.einsum(
        "hqk,qhd->khd", d_scores, split_heads(q_rows), preferred_element_type=jnp.float32
    )
    v_part = jnp.einsum(
        "hqk,qhd->khd", weights, split_heads(d_rows), preferred_element_type=jnp.float32
    )
    return (k_part, v_part)


def body(queries, keys, values, out_weight, out_grad, lengths):
    q_rows = queries[0]
    k_rows = keys[0]
    v_rows = values[0]
    dy_rows = out_grad[0]
    tok_rows = q_rows.shape[0]
    feature_width = q_rows.shape[1]
    shards = lax.axis_size("seq")
    seq_index = lax.axis_index("seq")
    key_reach = (MAXLEN + tok_rows - 2) // tok_rows
    image_ends = jnp.cumsum(lengths[0])
    own_ids = image_ids(image_ends, seq_index, tok_rows, shards)
    d_out = jnp.einsum("td,ed->te", dy_rows, out_weight, preferred_element_type=jnp.float32).astype(
        jnp.bfloat16
    )
    remote = []
    for distance in range(1, key_reach + 1):
        for offset in (distance, -distance):
            arrived = shifted((k_rows, v_rows), "seq", offset)
            remote.append((offset, arrived[0], arrived[1]))
    remote_ids = [image_ids(image_ends, seq_index - entry[0], tok_rows, shards) for entry in remote]
    own_scores = masked_scores(q_rows, k_rows, own_ids, own_ids)
    row_max = jnp.max(own_scores, axis=2)
    row_sum = jnp.sum(jnp.exp(own_scores - row_max[:, :, None]), axis=2)
    for entry, tile_ids in zip(remote, remote_ids):
        k_tile = entry[1]

        def widen(carried):
            old_max, old_sum = carried
            scores = masked_scores(q_rows, k_tile, own_ids, tile_ids)
            new_max = jnp.maximum(old_max, jnp.max(scores, axis=2))
            new_sum = old_sum * jnp.exp(old_max - new_max) + jnp.sum(
                jnp.exp(scores - new_max[:, :, None]), axis=2
            )
            return (new_max, new_sum)

        row_max, row_sum = lax.cond(
            touches(own_ids, tile_ids), widen, lambda carried: carried, (row_max, row_sum)
        )
    log_norm = row_max + jnp.log(row_sum)
    head_zeros = jnp.zeros((tok_rows, HEADS, HEAD_DIM), jnp.float32)
    mixed_sum = jnp.einsum(
        "hqk,khd->qhd",
        make_probs(q_rows, k_rows, own_ids, own_ids, log_norm),
        split_heads(v_rows),
        preferred_element_type=jnp.float32,
    )
    for entry, tile_ids in zip(remote, remote_ids):
        k_tile = entry[1]
        v_tile = entry[2]

        def mix_tile():
            weights = make_probs(q_rows, k_tile, own_ids, tile_ids, log_norm)
            return jnp.einsum(
                "hqk,khd->qhd", weights, split_heads(v_tile), preferred_element_type=jnp.float32
            )

        mixed_sum = mixed_sum + lax.cond(touches(own_ids, tile_ids), mix_tile, lambda: head_zeros)
    attended = mixed_sum.reshape(tok_rows, feature_width).astype(jnp.bfloat16)
    row_delta = jnp.sum(
        (d_out.astype(jnp.float32) * attended.astype(jnp.float32)).reshape(
            tok_rows, HEADS, HEAD_DIM
        ),
        axis=2,
    ).T
    weights, d_scores = score_grads(
        q_rows, k_rows, v_rows, d_out, own_ids, own_ids, log_norm, row_delta
    )
    q_grad = query_part(d_scores, k_rows)
    k_grad, v_grad = key_part(weights, d_scores, q_rows, d_out)
    for entry, tile_ids in zip(remote, remote_ids):
        offset = entry[0]
        k_tile = entry[1]
        v_tile = entry[2]

        def all_parts():
            tile_weights, tile_scores = score_grads(
                q_rows, k_tile, v_tile, d_out, own_ids, tile_ids, log_norm, row_delta
            )
            k_part, v_part = key_part(tile_weights, tile_scores, q_rows, d_out)
            return (query_part(tile_scores, k_tile), k_part, v_part)

        parts = lax.cond(
            touches(own_ids, tile_ids), all_parts, lambda: (head_zeros, head_zeros, head_zeros)
        )
        q_grad = q_grad + parts[0]
        returned = shifted(
            (parts[1].reshape(tok_rows, feature_width), parts[2].reshape(tok_rows, feature_width)),
            "seq",
            -offset,
        )
        k_grad = k_grad + returned[0].reshape(tok_rows, HEADS, HEAD_DIM)
        v_grad = v_grad + returned[1].reshape(tok_rows, HEADS, HEAD_DIM)
    weight_share = lax.psum_scatter(
        jnp.einsum("tr,tc->rc", attended, dy_rows, preferred_element_type=jnp.float32),
        "seq",
        scatter_dimension=0,
        tiled=True,
    )
    weight_sum = lax.psum(weight_share, "dp")
    all_tokens = tok_rows * shards * lax.axis_size("dp")
    weight_grad = weight_sum * (1.0 / math.sqrt(all_tokens))
    return (
        q_grad.reshape(1, tok_rows, feature_width),
        k_grad.reshape(1, tok_rows, feature_width),
        v_grad.reshape(1, tok_rows, feature_width),
        weight_grad,
    )


def solution(mesh):
    in_specs = (
        P("dp", "seq", None),
        P("dp", "seq", None),
        P("dp", "seq", None),
        P(),
        P("dp", "seq", None),
        P("dp", None),
    )
    out_specs = (P("dp", "seq", None), P("dp", "seq", None), P("dp", "seq", None), P("seq", None))
    return jax.shard_map(body, mesh=mesh, in_specs=in_specs, out_specs=out_specs, check_vma=False)
```

profile of v0, /device:TPU:17, one launch (start us, length us, event | category | flops | bytes accessed | tf_op | source)
XLA Modules:
  0.0 338.5 jit_solution(15637837956788970193)
XLA Ops:
  8.6 3.1 collective-permute-start
  11.7 3.1 collective-permute-start.1
  14.8 3.2 collective-permute-start.2
  18.0 2.1 collective-permute-start.3
  20.1 4.6 %collective-permute-start.4 = (bf16[128,1152]{0,1:T(8,128)(2,1)S(1)}, bf16[128,1152]{0,1:T(8,128)(2,1)}, u32[]{:S(2)}, u32[]{:S(2)}) collective-permute-start(bf16[128,1152]{0,1:T(8,128)(2,1)S(1)} %bitcast.263), channel_id=1, source_target_pairs={{0,3},{1,4},{2,5},{3,6},{4,7},{8,11},{9,12},{10,13},{11,14},{12,15... | collective-permute-start | bytes 884744 | tf_op jit(solution)/shard_map/ppermute | solution.py:19
  27.0 1.5 compare_reduce_fusion
  29.6 2.0 copy.103
  31.6 3.1 collective-permute-start.5
  35.8 2.1 collective-permute-start.7
  41.8 3.3 conditional.18
  45.1 2.5 conditional.19
  47.6 1.9 collective-permute-start.8
  49.6 2.5 conditional.20
  52.1 3.4 collective-permute-start.9
  55.5 3.6 %collective-permute-start.10 = (bf16[128,1152]{0,1:T(8,128)(2,1)}, bf16[128,1152]{0,1:T(8,128)(2,1)}, u32[]{:S(2)}, u32[]{:S(2)}) collective-permute-start(bf16[128,1152]{0,1:T(8,128)(2,1)} %bitcast.87), channel_id=1, source_target_pairs={{0,3},{1,4},{2,5},{3,6},{4,7},{8,11},{9,12},{10,13},{11,14},{12,15... | collective-permute-start | bytes 884744 | tf_op jit(solution)/shard_map/ppermute | solution.py:19
  59.1 2.0 collective-permute-start.6
  61.2 4.8 %collective-permute-start.11 = (bf16[128,1152]{0,1:T(8,128)(2,1)}, bf16[128,1152]{0,1:T(8,128)(2,1)}, u32[]{:S(2)}, u32[]{:S(2)}) collective-permute-start(bf16[128,1152]{0,1:T(8,128)(2,1)} %bitcast.87), channel_id=1, source_target_pairs={{3,0},{4,1},{5,2},{6,3},{7,4},{11,8},{12,9},{13,10},{14,11},{15,12... | collective-permute-start | bytes 884744 | tf_op jit(solution)/shard_map/ppermute | solution.py:19
  67.4 4.5 %conditional.25 = (f32[128,16,72]{0,2,1:T(8,128)}) conditional(s32[]{:T(128)} %convert_element_type.160, () %tuple.148, (s32[128]{0:T(128)}, s32[128]{0:T(128)S(1)}, bf16[1,128,1152]{2,1,0:T(8,128)(2,1)S(1)}, bf16[128,1152]{0,1:T(8,128)(2,1)}, f32[16,128]{1,0:T(8,128)S(1)}, /*index=5*/bf16[128,1152]{0,1:T(8,128)(2,1)}) %tuple.371), branch_computations={%region_42.43_spmd, %region_43.44_spmd} | conditional | flops 76562432 | bytes 2106376 | solution.py:135
  69.1 2.8 convolution_bitcast_fusion.1
  71.9 4.5 %conditional.26 = (f32[128,16,72]{0,2,1:T(8,128)}) conditional(s32[]{:T(128)} %convert_element_type.158, () %tuple.150, (s32[128]{0:T(128)}, s32[128]{0:T(128)S(1)}, bf16[1,128,1152]{2,1,0:T(8,128)(2,1)S(1)}, bf16[128,1152]{0,1:T(8,128)(2,1)}, f32[16,128]{1,0:T(8,128)S(1)}, /*index=5*/bf16[128,1152]{0,1:T(8,128)(2,1)}) %tuple.368), branch_computations={%region_44.45_spmd, %region_45.46_spmd} | conditional | flops 76562432 | bytes 2106376 | solution.py:135
  73.5 2.8 convolution_bitcast_fusion.2
  78.1 2.9 collective-permute-done.6
  81.0 4.4 %conditional.24 = (f32[128,16,72]{0,2,1:T(8,128)}) conditional(s32[]{:T(128)} %convert_element_type.162, () %tuple.146, (s32[128]{0:T(128)}, s32[128]{0:T(128)S(1)}, bf16[1,128,1152]{2,1,0:T(8,128)(2,1)S(1)}, bf16[128,1152]{0,1:T(8,128)(2,1)}, f32[16,128]{1,0:T(8,128)S(1)}, /*index=5*/bf16[128,1152]{0,1:T(8,128)(2,1)}) %tuple.365), branch_computations={%region_40.41_spmd, %region_41.42_spmd} | conditional | flops 76562432 | bytes 2106376 | solution.py:135
  82.6 2.8 convolution_bitcast_fusion
  85.4 2.1 convolution_bitcast_fusion.27
  88.4 2.4 add_convert_fusion
  90.8 3.2 fusion.105
  94.1 1.9 convolution_convert_fusion
  96.7 7.2 %conditional.31 = (f32[128,16,72]{0,2,1:T(8,128)S(1)}, f32[128,16,72]{0,2,1:T(8,128)}, f32[128,16,72]{0,2,1:T(8,128)}) conditional(s32[]{:T(128)} %convert_element_type.160, () %tuple.160, (s32[128]{0:T(128)S(1)}, s32[128]{0:T(128)S(1)}, bf16[1,128,1152]{2,1,0:T(8,128)(2,1)S(1)}, bf16[128,1152]{0,1:T(8,128)(2,1)}, f32[16,128]{1,0:T(8,128)S(1)}, ...), branch_computations={%region_55.56_spmd, %region_56.57_spmd} | conditional | flops 191119360 | bytes 8209432 | solution.py:160
  97.0 1.5 fusion.77
  98.7 1.5 fusion.76
  101.3 1.4 convolution_bitcast_fusion.11
  103.9 5.4 %collective-permute-start.19 = (f32[128,1152]{0,1:T(8,128)}, f32[128,1152]{0,1:T(8,128)}, u32[]{:S(2)}, u32[]{:S(2)}) collective-permute-start(f32[128,1152]{0,1:T(8,128)} %bitcast.110), channel_id=1, source_target_pairs={{0,1},{1,2},{2,3},{3,4},{4,5},{5,6},{6,7},{8,9},{9,10},{10,11},{11... | collective-permute-start | bytes 1769480 | tf_op jit(solution)/shard_map/ppermute | solution.py:19
  109.3 7.4 %conditional.32 = (f32[128,16,72]{0,2,1:T(8,128)S(1)}, f32[128,16,72]{0,2,1:T(8,128)}, f32[128,16,72]{0,2,1:T(8,128)}) conditional(s32[]{:T(128)} %convert_element_type.158, () %tuple.162, (s32[128]{0:T(128)S(1)}, s32[128]{0:T(128)S(1)}, bf16[1,128,1152]{2,1,0:T(8,128)(2,1)S(1)}, bf16[128,1152]{0,1:T(8,128)(2,1)}, f32[16,128]{1,0:T(8,128)S(1)}, ...), branch_computations={%region_57.58_spmd, %region_58.59_spmd} | conditional | flops 191119360 | bytes 8209432 | solution.py:160
  109.7 1.5 fusion.83
  111.4 1.6 fusion.82
  114.1 1.4 convolution_bitcast_fusion.14
  116.7 2.9 collective-permute-start.20
  119.9 7.2 %conditional.30 = (f32[128,16,72]{0,2,1:T(8,128)S(1)}, f32[128,16,72]{0,2,1:T(8,128)}, f32[128,16,72]{0,2,1:T(8,128)}) conditional(s32[]{:T(128)} %convert_element_type.162, () %tuple.158, (s32[128]{0:T(128)S(1)}, s32[128]{0:T(128)S(1)}, bf16[1,128,1152]{2,1,0:T(8,128)(2,1)S(1)}, bf16[128,1152]{0,1:T(8,128)(2,1)}, f32[16,128]{1,0:T(8,128)S(1)}, ...), branch_computations={%region_53.54_spmd, %region_54.55_spmd} | conditional | flops 191119360 | bytes 8209432 | solution.py:160
  120.2 1.5 fusion.71
  121.9 1.5 fusion.70
  124.5 1.4 convolution_bitcast_fusion.8
  127.1 1.9 collective-permute-start.18
  129.1 2.6 conditional.33
  131.7 3.1 collective-permute-start.21
  134.9 1.8 conditional.34
  136.7 9.5 %collective-permute-start.22 = (f32[128,1152]{0,1:T(8,128)}, f32[128,1152]{0,1:T(8,128)}, u32[]{:S(2)}, u32[]{:S(2)}) collective-permute-start(f32[128,1152]{0,1:T(8,128)} %bitcast.116), channel_id=1, source_target_pairs={{3,0},{4,1},{5,2},{6,3},{7,4},{11,8},{12,9},{13,10},{14,11},{15,12... | collective-permute-start | bytes 1769480 | tf_op jit(solution)/shard_map/ppermute | solution.py:19
  146.2 2.6 conditional.35
  148.8 1.5 fusion.104
  150.6 1.9 collective-permute-start.23
  152.6 1.9 collective-permute-start.13
  154.6 1.6 add_add_fusion.2
  157.7 18.0 %collective-permute-done.18 = f32[128,1152]{0,1:T(8,128)} collective-permute-done((f32[128,1152]{0,1:T(8,128)}, f32[128,1152]{0,1:T(8,128)}, u32[]{:S(2)}, u32[]{:S(2)}) %collective-permute-start.18) | collective-permute-done | bytes 589856 | tf_op jit(solution)/shard_map/ppermute | solution.py:19
  175.7 6.8 %collective-permute-start.14 = (f32[128,1152]{0,1:T(8,128)}, f32[128,1152]{0,1:T(8,128)}, u32[]{:S(2)}, u32[]{:S(2)}) collective-permute-start(f32[128,1152]{0,1:T(8,128)} %bitcast.98), channel_id=1, source_target_pairs={{2,0},{3,1},{4,2},{5,3},{6,4},{7,5},{10,8},{11,9},{12,10},{13,11},... | collective-permute-start | bytes 1769480 | tf_op jit(solution)/shard_map/ppermute | solution.py:19
  182.6 4.8 %collective-permute-start.12 = (f32[128,1152]{0,1:T(8,128)}, f32[128,1152]{0,1:T(8,128)}, u32[]{:S(2)}, u32[]{:S(2)}) collective-permute-start(f32[128,1152]{0,1:T(8,128)} %bitcast.94), channel_id=1, source_target_pairs={{1,0},{2,1},{3,2},{4,3},{5,4},{6,5},{7,6},{9,8},{10,9},{11,10},{12... | collective-permute-start | bytes 1769480 | tf_op jit(solution)/shard_map/ppermute | solution.py:19
  187.4 18.1 %collective-permute-done.22 = f32[128,1152]{0,1:T(8,128)} collective-permute-done((f32[128,1152]{0,1:T(8,128)}, f32[128,1152]{0,1:T(8,128)}, u32[]{:S(2)}, u32[]{:S(2)}) %collective-permute-start.22) | collective-permute-done | bytes 589856 | tf_op jit(solution)/shard_map/ppermute | solution.py:19
  205.5 1.9 collective-permute-start.15
  207.4 6.1 %collective-permute-start.16 = (f32[128,1152]{0,1:T(8,128)}, f32[128,1152]{0,1:T(8,128)}, u32[]{:S(2)}, u32[]{:S(2)}) collective-permute-start(f32[128,1152]{0,1:T(8,128)} %bitcast.102), channel_id=1, source_target_pairs={{3,0},{4,1},{5,2},{6,3},{7,4},{11,8},{12,9},{13,10},{14,11},{15,12... | collective-permute-start | bytes 1769480 | tf_op jit(solution)/shard_map/ppermute | solution.py:19
  213.5 1.9 collective-permute-start.17
  216.8 2.1 add_add_fusion
  220.0 74.1 %reduce-scatter.2.cloned.1.call-done = f32[144,1152]{1,0:T(8,128)} async-done(((f32[1152,1152]{1,0:T(8,128)}), f32[144,1152]{1,0:T(8,128)}) %reduce-scatter.2.cloned.1.call-update) | async-done | bytes 663568 | tf_op jit(solution)/shard_map/reduce_scatter | solution.py:171
  295.0 2.5 add_add_fusion.1
  298.5 31.2 %all-reduce.2.cloned.1.call-done = f32[144,1152]{1,0:T(8,128)} async-done(((f32[144,1152]{1,0:T(8,128)}), f32[144,1152]{1,0:T(8,128)}) %all-reduce.2.cloned.1.call-update) | async-done | bytes 663568 | tf_op jit(solution)/shard_map/psum | solution.py:177
  329.6 2.0 broadcast_multiply_fusion
  (199 shorter events, 47.1 us)
Async XLA Ops:
  7.2 86.9 %copy-start = (bf16[1152,1152]{1,0:T(8,128)(2,1)S(1)}, bf16[1152,1152]{1,0:T(8,128)(2,1)}, u32[]{:S(2)}) copy-start(bf16[1152,1152]{1,0:T(8,128)(2,1)} %param.45) | copy-start | bytes 7962628
  7.2 34.6 %copy-start.2 = (bf16[1,128,1152]{2,1,0:T(8,128)(2,1)S(1)}, bf16[1,128,1152]{2,1,0:T(8,128)(2,1)}, u32[]{:S(2)}) copy-start(bf16[1,128,1152]{2,1,0:T(8,128)(2,1)} %param.42) | copy-start | bytes 884740
  7.2 286.9 %reduce-scatter.2.cloned.1.call-start = ((), (), s32[]{:S(2)}) async-start(), calls=%async_computation.1 | async-start | bytes 5971968 | tf_op jit(solution)/shard_map/reduce_scatter | solution.py:171
  8.6 33.2 %copy-start.6 = (bf16[1,128,1152]{1,2,0:T(8,128)(2,1)}, bf16[1,128,1152]{1,2,0:T(8,128)(2,1)S(1)}, u32[]{:S(2)}) copy-start(bf16[1,128,1152]{1,2,0:T(8,128)(2,1)S(1)} %copy.94) | copy-start | bytes 884740
  8.6 23.0 %collective-permute-start = (bf16[128,1152]{0,1:T(8,128)(2,1)S(1)}, bf16[128,1152]{0,1:T(8,128)(2,1)}, u32[]{:S(2)}, u32[]{:S(2)}) collective-permute-start(bf16[128,1152]{0,1:T(8,128)(2,1)S(1)} %bitcast.259), channel_id=1, source_target_pairs={{0,1},{1,2},{2,3},{3,4},{4,5},{5,6},{6,7},{8,9},{9,10},{10,11},{11... | collective-permute-start | bytes 884744 | tf_op jit(solution)/shard_map/ppermute | solution.py:19
  11.7 24.1 %collective-permute-start.1 = (bf16[128,1152]{0,1:T(8,128)(2,1)S(1)}, bf16[128,1152]{0,1:T(8,128)(2,1)}, u32[]{:S(2)}, u32[]{:S(2)}) collective-permute-start(bf16[128,1152]{0,1:T(8,128)(2,1)S(1)} %bitcast.260), channel_id=1, source_target_pairs={{1,0},{2,1},{3,2},{4,3},{5,4},{6,5},{7,6},{9,8},{10,9},{11,10},{12... | collective-permute-start | bytes 884744 | tf_op jit(solution)/shard_map/ppermute | solution.py:19
  14.8 32.8 %collective-permute-start.2 = (bf16[128,1152]{0,1:T(8,128)(2,1)S(1)}, bf16[128,1152]{0,1:T(8,128)(2,1)}, u32[]{:S(2)}, u32[]{:S(2)}) collective-permute-start(bf16[128,1152]{0,1:T(8,128)(2,1)S(1)} %bitcast.261), channel_id=1, source_target_pairs={{0,2},{1,3},{2,4},{3,5},{4,6},{5,7},{8,10},{9,11},{10,12},{11,13},... | collective-permute-start | bytes 884744 | tf_op jit(solution)/shard_map/ppermute | solution.py:19
  18.0 34.1 %collective-permute-start.3 = (bf16[128,1152]{0,1:T(8,128)(2,1)S(1)}, bf16[128,1152]{0,1:T(8,128)(2,1)}, u32[]{:S(2)}, u32[]{:S(2)}) collective-permute-start(bf16[128,1152]{0,1:T(8,128)(2,1)S(1)} %bitcast.262), channel_id=1, source_target_pairs={{2,0},{3,1},{4,2},{5,3},{6,4},{7,5},{10,8},{11,9},{12,10},{13,11},... | collective-permute-start | bytes 884744 | tf_op jit(solution)/shard_map/ppermute | solution.py:19
  20.1 35.4 %collective-permute-start.4 = (bf16[128,1152]{0,1:T(8,128)(2,1)S(1)}, bf16[128,1152]{0,1:T(8,128)(2,1)}, u32[]{:S(2)}, u32[]{:S(2)}) collective-permute-start(bf16[128,1152]{0,1:T(8,128)(2,1)S(1)} %bitcast.263), channel_id=1, source_target_pairs={{0,3},{1,4},{2,5},{3,6},{4,7},{8,11},{9,12},{10,13},{11,14},{12,15... | collective-permute-start | bytes 884744 | tf_op jit(solution)/shard_map/ppermute | solution.py:19
  25.7 0.6 copy-start.41
  25.8 0.6 copy-start.29
  25.9 0.6 copy-start.27
  29.6 12.2 %copy-start.8 = (bf16[1,128,1152]{1,2,0:T(8,128)(2,1)}, bf16[1,128,1152]{1,2,0:T(8,128)(2,1)S(1)}, u32[]{:S(2)}) copy-start(bf16[1,128,1152]{1,2,0:T(8,128)(2,1)S(1)} %copy.93) | copy-start | bytes 884740
  31.6 27.5 %collective-permute-start.5 = (bf16[128,1152]{0,1:T(8,128)(2,1)S(1)}, bf16[128,1152]{0,1:T(8,128)(2,1)}, u32[]{:S(2)}, u32[]{:S(2)}) collective-permute-start(bf16[128,1152]{0,1:T(8,128)(2,1)S(1)} %bitcast.264), channel_id=1, source_target_pairs={{3,0},{4,1},{5,2},{6,3},{7,4},{11,8},{12,9},{13,10},{14,11},{15,12... | collective-permute-start | bytes 884744 | tf_op jit(solution)/shard_map/ppermute | solution.py:19
  35.8 2.1 copy-start.3
  35.8 25.3 %collective-permute-start.7 = (bf16[128,1152]{0,1:T(8,128)(2,1)}, bf16[128,1152]{0,1:T(8,128)(2,1)}, u32[]{:S(2)}, u32[]{:S(2)}) collective-permute-start(bf16[128,1152]{0,1:T(8,128)(2,1)} %bitcast.87), channel_id=1, source_target_pairs={{1,0},{2,1},{3,2},{4,3},{5,4},{6,5},{7,6},{9,8},{10,9},{11,10},{12... | collective-permute-start | bytes 884744 | tf_op jit(solution)/shard_map/ppermute | solution.py:19
  47.6 24.3 %collective-permute-start.8 = (bf16[128,1152]{0,1:T(8,128)(2,1)}, bf16[128,1152]{0,1:T(8,128)(2,1)}, u32[]{:S(2)}, u32[]{:S(2)}) collective-permute-start(bf16[128,1152]{0,1:T(8,128)(2,1)} %bitcast.87), channel_id=1, source_target_pairs={{0,2},{1,3},{2,4},{3,5},{4,6},{5,7},{8,10},{9,11},{10,12},{11,13},... | collective-permute-start | bytes 884744 | tf_op jit(solution)/shard_map/ppermute | solution.py:19
  52.1 24.3 %collective-permute-start.9 = (bf16[128,1152]{0,1:T(8,128)(2,1)}, bf16[128,1152]{0,1:T(8,128)(2,1)}, u32[]{:S(2)}, u32[]{:S(2)}) collective-permute-start(bf16[128,1152]{0,1:T(8,128)(2,1)} %bitcast.87), channel_id=1, source_target_pairs={{2,0},{3,1},{4,2},{5,3},{6,4},{7,5},{10,8},{11,9},{12,10},{13,11},... | collective-permute-start | bytes 884744 | tf_op jit(solution)/shard_map/ppermute | solution.py:19
  55.5 21.8 %collective-permute-start.10 = (bf16[128,1152]{0,1:T(8,128)(2,1)}, bf16[128,1152]{0,1:T(8,128)(2,1)}, u32[]{:S(2)}, u32[]{:S(2)}) collective-permute-start(bf16[128,1152]{0,1:T(8,128)(2,1)} %bitcast.87), channel_id=1, source_target_pairs={{0,3},{1,4},{2,5},{3,6},{4,7},{8,11},{9,12},{10,13},{11,14},{12,15... | collective-permute-start | bytes 884744 | tf_op jit(solution)/shard_map/ppermute | solution.py:19
  59.1 8.3 %copy-start.42 = (s32[128]{0:T(128)S(1)}, s32[128]{0:T(128)}, u32[]{:S(2)}) copy-start(s32[128]{0:T(128)} %copy-done.41) | copy-start | bytes 1540
  59.1 21.8 %collective-permute-start.6 = (bf16[128,1152]{0,1:T(8,128)(2,1)}, bf16[128,1152]{0,1:T(8,128)(2,1)}, u32[]{:S(2)}, u32[]{:S(2)}) collective-permute-start(bf16[128,1152]{0,1:T(8,128)(2,1)} %bitcast.87), channel_id=1, source_target_pairs={{0,1},{1,2},{2,3},{3,4},{4,5},{5,6},{6,7},{8,9},{9,10},{10,11},{11... | collective-permute-start | bytes 884744 | tf_op jit(solution)/shard_map/ppermute | solution.py:19
  61.1 10.7 %copy-start.39 = (s32[128]{0:T(128)S(1)}, s32[128]{0:T(128)}, u32[]{:S(2)}) copy-start(s32[128]{0:T(128)} %copy-done.38) | copy-start | bytes 1540
  61.2 26.3 %copy-start.23 = (f32[16,128]{1,0:T(8,128)}, f32[16,128]{1,0:T(8,128)S(1)}, u32[]{:S(2)}) copy-start(f32[16,128]{1,0:T(8,128)S(1)} %log_add_fusion) | copy-start | bytes 24580
  61.2 26.3 %collective-permute-start.11 = (bf16[128,1152]{0,1:T(8,128)(2,1)}, bf16[128,1152]{0,1:T(8,128)(2,1)}, u32[]{:S(2)}, u32[]{:S(2)}) collective-permute-start(bf16[128,1152]{0,1:T(8,128)(2,1)} %bitcast.87), channel_id=1, source_target_pairs={{3,0},{4,1},{5,2},{6,3},{7,4},{11,8},{12,9},{13,10},{14,11},{15,12... | collective-permute-start | bytes 884744 | tf_op jit(solution)/shard_map/ppermute | solution.py:19
  67.4 18.0 %copy-start.4 = (bf16[16,128,128]{1,2,0:T(8,128)(2,1)}, bf16[16,128,128]{1,2,0:T(8,128)(2,1)S(1)}, u32[]{:S(2)}) copy-start(bf16[16,128,128]{1,2,0:T(8,128)(2,1)S(1)} %exponential_convert_fusion) | copy-start | bytes 1572868
  67.4 8.9 %copy-start.33 = (s32[128]{0:T(128)S(1)}, s32[128]{0:T(128)}, u32[]{:S(2)}) copy-start(s32[128]{0:T(128)} %copy-done.32) | copy-start | bytes 1540
  71.9 5.3 %copy-start.30 = (s32[128]{0:T(128)S(1)}, s32[128]{0:T(128)}, u32[]{:S(2)}) copy-start(s32[128]{0:T(128)} %copy-done.29) | copy-start | bytes 1540
  76.4 4.6 %copy-start.36 = (s32[128]{0:T(128)S(1)}, s32[128]{0:T(128)}, u32[]{:S(2)}) copy-start(s32[128]{0:T(128)} %copy-done.35) | copy-start | bytes 1540
  87.6 0.8 copy-start.18
  88.4 2.4 copy-start.19
  94.0 235.6 %all-reduce.2.cloned.1.call-start = ((), (), s32[]{:S(2)}) async-start(), calls=%async_computation.2 | async-start | bytes 1327104 | tf_op jit(solution)/shard_map/psum | solution.py:177
  94.0 2.5 copy-start.22
  94.1 2.5 copy-start.43
  96.0 0.7 copy-start.24
  96.7 12.6 %copy-start.40 = (s32[128]{0:T(128)S(1)}, s32[128]{0:T(128)}, u32[]{:S(2)}) copy-start(s32[128]{0:T(128)} %copy-done.38) | copy-start | bytes 1540
  103.9 5.4 %copy-start.10 = (f32[128,16,72]{0,2,1:T(8,128)}, f32[128,16,72]{0,2,1:T(8,128)S(1)}, u32[]{:S(2)}) copy-start(f32[128,16,72]{0,2,1:T(8,128)S(1)} %get-tuple-element.459) | copy-start | bytes 1769476
  103.9 46.8 %collective-permute-start.19 = (f32[128,1152]{0,1:T(8,128)}, f32[128,1152]{0,1:T(8,128)}, u32[]{:S(2)}, u32[]{:S(2)}) collective-permute-start(f32[128,1152]{0,1:T(8,128)} %bitcast.110), channel_id=1, source_target_pairs={{0,1},{1,2},{2,3},{3,4},{4,5},{5,6},{6,7},{8,9},{9,10},{10,11},{11... | collective-permute-start | bytes 1769480 | tf_op jit(solution)/shard_map/ppermute | solution.py:19
  109.3 10.6 %copy-start.37 = (s32[128]{0:T(128)S(1)}, s32[128]{0:T(128)}, u32[]{:S(2)}) copy-start(s32[128]{0:T(128)} %copy-done.35) | copy-start | bytes 1540
  116.7 2.9 copy-start.12
  116.7 35.9 %collective-permute-start.20 = (f32[128,1152]{0,1:T(8,128)}, f32[128,1152]{0,1:T(8,128)}, u32[]{:S(2)}, u32[]{:S(2)}) collective-permute-start(f32[128,1152]{0,1:T(8,128)} %bitcast.112), channel_id=1, source_target_pairs={{2,0},{3,1},{4,2},{5,3},{6,4},{7,5},{10,8},{11,9},{12,10},{13,11},... | collective-permute-start | bytes 1769480 | tf_op jit(solution)/shard_map/ppermute | solution.py:19
  119.9 9.2 %copy-start.34 = (s32[128]{0:T(128)S(1)}, s32[128]{0:T(128)}, u32[]{:S(2)}) copy-start(s32[128]{0:T(128)} %copy-done.32) | copy-start | bytes 1540
  127.1 1.9 copy-start.14
  127.1 48.6 %collective-permute-start.18 = (f32[128,1152]{0,1:T(8,128)}, f32[128,1152]{0,1:T(8,128)}, u32[]{:S(2)}, u32[]{:S(2)}) collective-permute-start(f32[128,1152]{0,1:T(8,128)} %bitcast.108), channel_id=1, source_target_pairs={{1,0},{2,1},{3,2},{4,3},{5,4},{6,5},{7,6},{9,8},{10,9},{11,10},{12... | collective-permute-start | bytes 1769480 | tf_op jit(solution)/shard_map/ppermute | solution.py:19
  129.1 5.8 %copy-start.31 = (s32[128]{0:T(128)S(1)}, s32[128]{0:T(128)}, u32[]{:S(2)}) copy-start(s32[128]{0:T(128)} %copy-done.29) | copy-start | bytes 1540
  131.7 50.8 %collective-permute-start.21 = (f32[128,1152]{0,1:T(8,128)}, f32[128,1152]{0,1:T(8,128)}, u32[]{:S(2)}, u32[]{:S(2)}) collective-permute-start(f32[128,1152]{0,1:T(8,128)} %bitcast.114), channel_id=1, source_target_pairs={{0,2},{1,3},{2,4},{3,5},{4,6},{5,7},{8,10},{9,11},{10,12},{11,13},... | collective-permute-start | bytes 1769480 | tf_op jit(solution)/shard_map/ppermute | solution.py:19
  134.9 11.3 %copy-start.28 = (s32[128]{0:T(128)S(1)}, s32[128]{0:T(128)}, u32[]{:S(2)}) copy-start(s32[128]{0:T(128)} %copy-done.27) | copy-start | bytes 1540
  136.7 9.5 %copy-start.16 = (f32[128,16,72]{0,2,1:T(8,128)}, f32[128,16,72]{0,2,1:T(8,128)S(1)}, u32[]{:S(2)}) copy-start(f32[128,16,72]{0,2,1:T(8,128)S(1)} %get-tuple-element.462) | copy-start | bytes 1769476
  136.7 68.8 %collective-permute-start.22 = (f32[128,1152]{0,1:T(8,128)}, f32[128,1152]{0,1:T(8,128)}, u32[]{:S(2)}, u32[]{:S(2)}) collective-permute-start(f32[128,1152]{0,1:T(8,128)} %bitcast.116), channel_id=1, source_target_pairs={{3,0},{4,1},{5,2},{6,3},{7,4},{11,8},{12,9},{13,10},{14,11},{15,12... | collective-permute-start | bytes 1769480 | tf_op jit(solution)/shard_map/ppermute | solution.py:19
  146.2 2.6 copy-start.5
  146.2 4.1 %copy-start.7 = (bf16[1,128,1152]{1,2,0:T(8,128)(2,1)S(1)}, bf16[1,128,1152]{1,2,0:T(8,128)(2,1)}, u32[]{:S(2)}) copy-start(bf16[1,128,1152]{1,2,0:T(8,128)(2,1)} %copy-done.6) | copy-start | bytes 884740
  148.8 5.7 %copy-start.11 = (f32[128,16,72]{0,2,1:T(8,128)S(1)}, f32[128,16,72]{0,2,1:T(8,128)}, u32[]{:S(2)}) copy-start(f32[128,16,72]{0,2,1:T(8,128)} %copy-done.10) | copy-start | bytes 1769476
  148.8 5.7 %copy-start.13 = (f32[128,16,72]{0,2,1:T(8,128)S(1)}, f32[128,16,72]{0,2,1:T(8,128)}, u32[]{:S(2)}) copy-start(f32[128,16,72]{0,2,1:T(8,128)} %copy-done.12) | copy-start | bytes 1769476
  148.8 5.7 %copy-start.15 = (f32[128,16,72]{0,2,1:T(8,128)S(1)}, f32[128,16,72]{0,2,1:T(8,128)}, u32[]{:S(2)}) copy-start(f32[128,16,72]{0,2,1:T(8,128)} %copy-done.14) | copy-start | bytes 1769476
  148.8 5.7 %copy-start.17 = (f32[128,16,72]{0,2,1:T(8,128)S(1)}, f32[128,16,72]{0,2,1:T(8,128)}, u32[]{:S(2)}) copy-start(f32[128,16,72]{0,2,1:T(8,128)} %copy-done.16) | copy-start | bytes 1769476
  150.6 56.8 %collective-permute-start.23 = (f32[128,1152]{0,1:T(8,128)}, f32[128,1152]{0,1:T(8,128)}, u32[]{:S(2)}, u32[]{:S(2)}) collective-permute-start(f32[128,1152]{0,1:T(8,128)} %bitcast.118), channel_id=1, source_target_pairs={{0,3},{1,4},{2,5},{3,6},{4,7},{8,11},{9,12},{10,13},{11,14},{12,15... | collective-permute-start | bytes 1769480 | tf_op jit(solution)/shard_map/ppermute | solution.py:19
  152.6 61.0 %collective-permute-start.13 = (f32[128,1152]{0,1:T(8,128)}, f32[128,1152]{0,1:T(8,128)}, u32[]{:S(2)}, u32[]{:S(2)}) collective-permute-start(f32[128,1152]{0,1:T(8,128)} %bitcast.96), channel_id=1, source_target_pairs={{0,1},{1,2},{2,3},{3,4},{4,5},{5,6},{6,7},{8,9},{9,10},{10,11},{11... | collective-permute-start | bytes 1769480 | tf_op jit(solution)/shard_map/ppermute | solution.py:19
  154.5 60.9 %copy-start.9 = (bf16[1,128,1152]{1,2,0:T(8,128)(2,1)S(1)}, bf16[1,128,1152]{1,2,0:T(8,128)(2,1)}, u32[]{:S(2)}) copy-start(bf16[1,128,1152]{1,2,0:T(8,128)(2,1)} %copy-done.8) | copy-start | bytes 884740
  175.7 118.4 %collective-permute-start.14 = (f32[128,1152]{0,1:T(8,128)}, f32[128,1152]{0,1:T(8,128)}, u32[]{:S(2)}, u32[]{:S(2)}) collective-permute-start(f32[128,1152]{0,1:T(8,128)} %bitcast.98), channel_id=1, source_target_pairs={{2,0},{3,1},{4,2},{5,3},{6,4},{7,5},{10,8},{11,9},{12,10},{13,11},... | collective-permute-start | bytes 1769480 | tf_op jit(solution)/shard_map/ppermute | solution.py:19
  182.6 111.5 %collective-permute-start.12 = (f32[128,1152]{0,1:T(8,128)}, f32[128,1152]{0,1:T(8,128)}, u32[]{:S(2)}, u32[]{:S(2)}) collective-permute-start(f32[128,1152]{0,1:T(8,128)} %bitcast.94), channel_id=1, source_target_pairs={{1,0},{2,1},{3,2},{4,3},{5,4},{6,5},{7,6},{9,8},{10,9},{11,10},{12... | collective-permute-start | bytes 1769480 | tf_op jit(solution)/shard_map/ppermute | solution.py:19
  205.5 88.6 %collective-permute-start.15 = (f32[128,1152]{0,1:T(8,128)}, f32[128,1152]{0,1:T(8,128)}, u32[]{:S(2)}, u32[]{:S(2)}) collective-permute-start(f32[128,1152]{0,1:T(8,128)} %bitcast.100), channel_id=1, source_target_pairs={{0,2},{1,3},{2,4},{3,5},{4,6},{5,7},{8,10},{9,11},{10,12},{11,13},... | collective-permute-start | bytes 1769480 | tf_op jit(solution)/shard_map/ppermute | solution.py:19
  207.4 86.7 %collective-permute-start.16 = (f32[128,1152]{0,1:T(8,128)}, f32[128,1152]{0,1:T(8,128)}, u32[]{:S(2)}, u32[]{:S(2)}) collective-permute-start(f32[128,1152]{0,1:T(8,128)} %bitcast.102), channel_id=1, source_target_pairs={{3,0},{4,1},{5,2},{6,3},{7,4},{11,8},{12,9},{13,10},{14,11},{15,12... | collective-permute-start | bytes 1769480 | tf_op jit(solution)/shard_map/ppermute | solution.py:19
  213.5 80.6 %collective-permute-start.17 = (f32[128,1152]{0,1:T(8,128)}, f32[128,1152]{0,1:T(8,128)S(1)}, u32[]{:S(2)}, u32[]{:S(2)}) collective-permute-start(f32[128,1152]{0,1:T(8,128)} %bitcast.104), channel_id=1, source_target_pairs={{0,3},{1,4},{2,5},{3,6},{4,7},{8,11},{9,12},{10,13},{11,14},{12,15... | collective-permute-start | bytes 1769480 | tf_op jit(solution)/shard_map/ppermute | solution.py:19
  294.1 0.8 copy-start.20
  295.0 36.6 %copy-start.1 = (bf16[1152,1152]{1,0:T(8,128)(2,1)S(1)}, bf16[1152,1152]{1,0:T(8,128)(2,1)}, u32[]{:S(2)}) copy-start(bf16[1152,1152]{1,0:T(8,128)(2,1)} %param.45) | copy-start | bytes 7962628
  (4 other events, 2.2 us)
Sparse Core Ops, SparseCore 0:
  94.1 199.9 reduce-scatter.1
  296.6 33.0 all-reduce.1
where the time goes:
time: 343 us; the launch traced here: 338 us
  waiting for transfers between devices  144 us (42%)
  starting transfers between devices  85.4 us (25%)
  matrix products  44.6 us (13%)
  local copies, waits for them, and re-layouts  25.2 us (7%)
  other arithmetic  19.8 us (6%)
  between operations  18.7 us (5%)
    ppermute x24, starting transfers between devices, shifted(): return lax.ppermute(block, axis, route)  85.3 us
    reduce_scatter x1, waiting for transfers between devices, body(): lax.psum_scatter(jnp.einsum('tr,tc->rc', attended, dy_rows, preferred_ele...  74.1 us
    ppermute x24, waiting for transfers between devices, shifted(): return lax.ppermute(block, axis, route)  39 us
    psum x1, waiting for transfers between devices, body(): weight_sum = lax.psum(weight_share, 'dp')  31.2 us
    unnamed x90, local copies, waits for them, and re-layouts  10.6 us
    dot_general x7, matrix products, masked_scores(): jnp.einsum('qhd,khd->hqk', split_heads(q_rows), split_heads(k_rows), pref...  9.66 us
    broadcast_in_dim x12, local copies, waits for them, and re-layouts, body(): head_zeros = jnp.zeros((tok_rows, HEADS, HEAD_DIM), jnp.float32)  8.7 us
    dot_general x3, matrix products, mix_tile(): jnp.einsum('hqk,khd->qhd', weights, split_heads(v_tile), preferred_elemen...  8.45 us
  transfers between devices with their start and end apart: 26, of which 5 were waited for; matrix products, arithmetic and copies ran while one was open for 23% of the time, Pallas kernels for 0%

commit v1 on v0

--- a/solution.py
+++ b/solution.py
@@ -1,8 +1,11 @@
+import functools
 import math
 
 import jax
 import jax.numpy as jnp
 from jax import lax
+from jax.experimental import pallas as pl
+from jax.experimental.pallas import tpu as pltpu
 from jax.sharding import PartitionSpec as P
 
 HEADS = 16
@@ -75,7 +78,7 @@
     return (k_part, v_part)
 
 
-def body(queries, keys, values, out_weight, out_grad, lengths):
+def halo_body(queries, keys, values, out_weight, out_grad, lengths):
     q_rows = queries[0]
     k_rows = keys[0]
     v_rows = values[0]
@@ -185,6 +188,329 @@
     )
 
 
+BF16, F32 = jnp.bfloat16, jnp.float32
+ANY = pl.BlockSpec(memory_space=pl.ANY)
+VMEM = pl.BlockSpec(memory_space=pltpu.VMEM)
+HBM = pl.BlockSpec(memory_space=pltpu.HBM)
+SMEM = pl.BlockSpec(memory_space=pltpu.SMEM)
+DMA = pltpu.SemaphoreType.DMA
+PARAMS = pltpu.CompilerParams(vmem_limit_bytes=16 * 1024 * 1024)
+NT = ((1,), (1,))
+
+
+def dot(a, b, contract=((1,), (0,))):
+    return lax.dot_general(a, b, (contract, ((), ())), preferred_element_type=F32)
+
+
+def spread_kernel(q_ref, k_ref, v_ref, out_ref, rows_s, turned_s, in_sem, out_sem):
+    shards, height, _ = out_ref.shape
+    part = height // 3
+    loads = [pltpu.make_async_copy(ref, rows_s.at[i], in_sem.at[i]) for i, ref in enumerate((q_ref, k_ref, v_ref))]
+    for load in loads:
+        load.start()
+    stores = []
+    for i, load in enumerate(loads):
+        load.wait()
+        turned = rows_s[i].T
+        for shard in range(shards):
+            turned_s[i, shard] = turned[shard * part:(shard + 1) * part, :]
+        store = pltpu.make_async_copy(turned_s.at[i], out_ref.at[:, pl.ds(i * part, part), :], out_sem.at[i])
+        store.start()
+        stores.append(store)
+    for store in stores:
+        store.wait()
+
+
+def collect_kernel(*refs):
+    blocks, (q_ref, k_ref, v_ref, turned_s, rows_s, out_sem) = refs[:-6], refs[-6:]
+    part = blocks[0].shape[0] // 3
+    me = lax.axis_index("seq")
+    for n, block in enumerate(blocks):
+        turned_s[me ^ (-n % len(blocks))] = block[...]
+    stores = []
+    for i, ref in enumerate((q_ref, k_ref, v_ref)):
+        whole = jnp.concatenate([turned_s[n, i * part:(i + 1) * part, :] for n in range(len(blocks))], axis=0)
+        rows_s[i] = whole.astype(F32).T
+        store = pltpu.make_async_copy(rows_s.at[i], ref, out_sem.at[i])
+        store.start()
+        stores.append(store)
+    for store in stores:
+        store.wait()
+
+
+def window_sizes(tok, shards):
+    return min(2, shards), min((MAXLEN + tok - 2) // tok + 1, shards)
+
+
+def each_image(lengths, tok, shards, work):
+    least, most = window_sizes(tok, shards)
+
+    def one_image(image, start):
+        end = start + lengths[0, image]
+        low = start // tok
+        count = jnp.maximum((end - 1) // tok - low + 1, least)
+        first = jnp.minimum(low, shards - count)
+        for size in range(least, most + 1):
+            @pl.when(count == size)
+            def _():
+                work(image, size, first, start, end)
+        return end
+
+    lax.fori_loop(0, lengths.shape[1], one_image, jnp.int32(0))
+
+
+def store_heads(ref, block, columns):
+    heads, padded, _ = ref.shape
+    filler = jnp.zeros((padded - HEAD_DIM, block.shape[1]), F32)
+    for head in range(heads):
+        rows = block[head * HEAD_DIM:(head + 1) * HEAD_DIM, :]
+        ref[head, :, columns] = jnp.concatenate([rows, filler], axis=0).astype(BF16)
+
+
+def joined(ref):
+    return jnp.concatenate([ref[head, 0:HEAD_DIM, :] for head in range(ref.shape[0])], axis=0).astype(BF16)
+
+
+def forward_kernel(early, len_ref, w_ref, in_ref, *refs):
+    pieces = refs[:early]
+    (q_s, k_s, vt_s, att_s, probs_s, d_s, wg_s, w_s, len_s, v_s, kt_s, sum_s, dy_s, len_sem, w_sem, dy_sem) = refs[early:]
+    shards, height, tok = in_ref.shape
+    part = height // 3
+    heads = q_s.shape[0]
+    scale = HEAD_DIM ** (-0.5)
+
+    load_len = pltpu.make_async_copy(len_ref, len_s, len_sem)
+    load_len.start()
+    load_w = load_w_rows(w_ref, w_s, w_sem)
+    loads = load_rows(pieces, dy_s, dy_sem)
+    sum_s[...] = jnp.zeros_like(sum_s)
+    for shard in range(shards):
+        columns = slice(shard * tok, (shard + 1) * tok)
+        for i, ref in enumerate((q_s, k_s, v_s)):
+            store_heads(ref, in_ref[shard, i * part:(i + 1) * part, :].astype(F32), columns)
+    for head in range(heads):
+        kt_s[head] = k_s[head].T
+        vt_s[head] = v_s[head].T
+    load_len.wait()
+
+    def work(image, count, first, start, end):
+        width = count * tok
+        base = pl.multiple_of(first * tok, tok)
+        columns = pl.ds(base, width)
+        key_pos = base + lax.broadcasted_iota(jnp.int32, (width, 1), 0)
+        key_in = jnp.logical_and(key_pos >= start, key_pos < end)
+        query_pos = base + lax.broadcasted_iota(jnp.int32, (1, width), 1)
+        query_in = jnp.logical_and(query_pos >= start, query_pos < end)
+        for head in range(heads):
+            scores = jnp.where(key_in, dot(kt_s[head, columns, :], q_s[head, :, columns]), NEG_FILL)
+            top = jnp.max(scores, axis=0, keepdims=True)
+            grown = jnp.exp((scores - top) * scale)
+            total = jnp.sum(grown, axis=0, keepdims=True)
+            probs = (grown * jnp.where(query_in, 1.0 / total, 0.0)).astype(BF16)
+            probs_s[image, head, 0:width, 0:width] = probs
+            sum_s[head, :, columns] += dot(v_s[head, :, columns], probs)
+
+    each_image(len_s, tok, shards, work)
+    att_s[...] = joined(sum_s)
+    for n in range(early, shards):
+        dy_s[piece_columns(n, tok), :] = jnp.zeros((tok, dy_s.shape[1]), BF16)
+    load_w.wait()
+    for load in loads:
+        load.wait()
+    for shard in range(0, shards, 2):
+        d_block = dot(w_s[...], dy_s[shard * tok:(shard + 2) * tok, :], NT)
+        store_heads(d_s, d_block, slice(shard * tok, (shard + 2) * tok))
+    wg_s[...] = dot(att_s[...], dy_s[...])
+
+
+def backward_kernel(early, len_ref, w_s, q_s, k_s, vt_s, att_s, probs_s, d_ref, *refs):
+    late = refs[:8 - early]
+    outs = refs[8 - early:16 - early]
+    (len_s, d_s, dq_s, dk_s, dv_s, out_s, len_sem, out_sem) = refs[16 - early:]
+    shards, height, tok = out_s.shape
+    part = height // 3
+    heads = d_s.shape[0]
+    scale = HEAD_DIM ** (-0.5)
+    load_len = pltpu.make_async_copy(len_ref, len_s, len_sem)
+    load_len.start()
+    d_s[...] = d_ref[...]
+    for ref in (dq_s, dk_s, dv_s):
+        ref[...] = jnp.zeros_like(ref)
+    for n, piece in enumerate(late):
+        store_heads(d_s, dot(w_s[...], piece[...], NT), piece_columns(early + n, tok))
+    load_len.wait()
+
+    def work(image, count, first, start, end):
+        width = count * tok
+        columns = pl.ds(pl.multiple_of(first * tok, tok), width)
+        att_all = att_s[:, columns].astype(F32)
+        for head in range(heads):
+            d = d_s[head, :, columns]
+            probs = probs_s[image, head, 0:width, 0:width]
+            att = att_all[head * HEAD_DIM:(head + 1) * HEAD_DIM, :]
+            delta = jnp.sum(d[0:HEAD_DIM, :].astype(F32) * att, axis=0, keepdims=True)
+            d_probs = dot(vt_s[head, columns, :], d)
+            d_scores = (scale * probs.astype(F32) * (d_probs - delta)).astype(BF16)
+            dq_s[head, :, columns] += dot(k_s[head, :, columns], d_scores)
+            dk_s[head, :, columns] += dot(q_s[head, :, columns], d_scores, NT)
+            dv_s[head, :, columns] += dot(d, probs, NT)
+
+    each_image(len_s, tok, shards, work)
+
+    stores = []
+    for i, ref in enumerate((dq_s, dk_s, dv_s)):
+        whole = joined(ref)
+        for shard in range(shards):
+            out_s[shard, i * part:(i + 1) * part, :] = whole[:, shard * tok:(shard + 1) * tok]
+    me = lax.axis_index("seq")
+    for n in range(shards - 1, 0, -1):
+        store = pltpu.make_async_copy(out_s.at[me ^ n], outs[n], out_sem.at[n])
+        store.start()
+        stores.append(store)
+    outs[0][...] = out_s[me]
+    for store in stores:
+        store.wait()
+
+
+def weight_kernel(early, att_ref, wg_ref, *refs):
+    late, out_ref = refs[:-1], refs[-1]
+    total = wg_ref[...]
+    for n, piece in enumerate(late):
+        total = total + dot(att_ref[:, piece_columns(early + n, piece.shape[0])], piece[...])
+    out_ref[...] = total.astype(BF16)
+
+
+def load_w_rows(w_ref, w_s, sem):
+    part = w_s.shape[0]
+    row = pl.multiple_of(lax.axis_index("seq") * part, part)
+    load = pltpu.make_async_copy(w_ref.at[pl.ds(row, part), :], w_s, sem)
+    load.start()
+    return load
+
+
+def piece_columns(n, tok):
+    me = lax.axis_index("seq")
+    owner = me ^ jnp.where(is_inner(me), INNER_SOURCES[n], OUTER_SOURCES[n])
+    return pl.ds(pl.multiple_of(owner * tok, tok), tok)
+
+
+def load_rows(pieces, dy_s, sems):
+    loads = []
+    for n, piece in enumerate(pieces):
+        load = pltpu.make_async_copy(piece, dy_s.at[piece_columns(n, piece.shape[0]), :], sems.at[n])
+        load.start()
+        loads.append(load)
+    return loads
+
+
+INNER_SOURCES = (0, 2, 6, 4, 3, 1, 7, 5)
+OUTER_SOURCES = (0, 2, 1, 3, 4, 6, 5, 7)
+
+
+def is_inner(index):
+    z = index // 2
+    return jnp.logical_or(z == 1, z == 2)
+
+
+def gather_steps(block, event):
+    devices = range(8)
+    along = [(i, i ^ 2) for i in devices]
+    across = [(i, i ^ 1) for i in devices]
+    middle = [(i, i ^ 6 if i // 2 in (1, 2) else i ^ 1) for i in devices]
+    inner = is_inner(lax.axis_index("seq"))
+
+    def move(value, pairs):
+        return lax.ppermute(value, "seq", pairs)
+
+    one = move(block, along)
+    two = move(block, middle)
+    one, two = after(one, event), after(two, event)
+    three = move(one, middle)
+    four = move(two, along)
+    five = move(three, along)
+    six = move(jnp.where(inner, two, four), across)
+    seven = move(jnp.where(inner, three, five), across)
+    return (block, one, two, three, four, five, six, seven)
+
+
+def after(value, *events):
+    return lax.optimization_barrier((value, *events))[0]
+
+
+def in_hbm(*arrays):
+    return [pltpu.with_memory_space_constraint(array, pltpu.HBM) for array in arrays]
+
+
+def head_body(queries, keys, values, out_weight, out_grad, lengths):
+    tok, width = queries.shape[1:]
+    shards = lax.axis_size("seq")
+    groups = lax.axis_size("dp")
+    part = width // shards
+    heads = HEADS // shards
+    tokens = tok * shards
+    padded = -(-HEAD_DIM // 16) * 16
+
+    def shape(dims, kind=BF16):
+        return jax.ShapeDtypeStruct(dims, kind)
+
+    sent = pl.pallas_call(
+        spread_kernel, out_shape=pltpu.HBM((shards, 3 * part, tok), BF16),
+        in_specs=[HBM] * 3, out_specs=HBM, compiler_params=PARAMS,
+        scratch_shapes=[pltpu.VMEM((3, tok, width), BF16), pltpu.VMEM((3, shards, part, tok), BF16), DMA((3,)), DMA((3,))],
+    )(*in_hbm(queries[0], keys[0], values[0]))
+    pieces = gather_steps(out_grad[0], sent)
+    arrived = lax.all_to_all(after(sent, *pieces[1:3]), "seq", 0, 0, tiled=True)
+
+    images = lengths.shape[1]
+    window = window_sizes(tok, shards)[1] * tok
+    wide, tall = (heads, padded, tokens), (heads, tokens, padded)
+    flat, chance = (part, tokens), (images, heads, window, window)
+
+    def scratch(*dims, kind=BF16):
+        return [pltpu.VMEM(d, kind) for d in dims]
+
+    len_s = pltpu.SMEM((1, images), jnp.int32)
+    early = 6
+    late = len(pieces) - early
+    q_t, k_t, v_r, attended, probs, d_part, w_early, w_rows = pl.pallas_call(
+        functools.partial(forward_kernel, early),
+        out_shape=[shape(wide), shape(wide), shape(tall), shape(flat), shape(chance), shape(wide), shape((part, width), F32), shape((part, width))],
+        in_specs=[HBM, HBM, VMEM] + [HBM] * early, out_specs=[VMEM] * 8, compiler_params=PARAMS,
+        scratch_shapes=[len_s] + scratch(wide, tall) + scratch(wide, kind=F32) + scratch((tokens, width))
+        + [DMA, DMA, DMA((early,))],
+    )(*in_hbm(lengths, out_weight), arrived, *in_hbm(*pieces[:early]))
+    w_part = pl.pallas_call(
+        functools.partial(weight_kernel, early), out_shape=shape((part, width)),
+        in_specs=[VMEM] * (2 + late), out_specs=VMEM, compiler_params=PARAMS,
+    )(attended, w_early, *pieces[early:])
+    grads = pl.pallas_call(
+        functools.partial(backward_kernel, early),
+        out_shape=[shape((3 * part, tok))] + [pltpu.HBM((3 * part, tok), BF16)] * (shards - 1),
+        in_specs=[HBM] + [VMEM] * (7 + late), out_specs=[VMEM] + [HBM] * (shards - 1), compiler_params=PARAMS,
+        scratch_shapes=[len_s] + scratch(wide) + scratch(wide, wide, wide, kind=F32)
+        + scratch((shards, 3 * part, tok)) + [DMA, DMA((shards,))],
+    )(*in_hbm(lengths), w_rows, q_t, k_t, v_r, attended, probs, d_part, *pieces[early:])
+    sums = w_part.astype(F32)
+    step = 1
+    while step < groups:
+        pairs = [(i, i ^ step) for i in range(groups)]
+        sums = w_part.astype(F32) + after(lax.ppermute(w_part, "dp", pairs), grads[0]).astype(F32)
+        w_part = lax.reduce_precision(sums, 8, 7).astype(BF16)
+        step *= 2
+    weight_grad = sums * (1.0 / math.sqrt(tokens * groups))
+
+    returned = [grads[0]]
+    for n in range(shards - 1, 0, -1):
+        block = grads[n] if n > 1 else after(grads[n], weight_grad)
+        returned.append(lax.ppermute(block, "seq", [(i, i ^ n) for i in range(shards)]))
+    q_grad, k_grad, v_grad = pl.pallas_call(
+        collect_kernel, out_shape=[shape((tok, width), F32)] * 3, in_specs=[VMEM] * shards, out_specs=[ANY] * 3,
+        compiler_params=PARAMS,
+        scratch_shapes=scratch((shards, 3 * part, tok)) + scratch((3, tok, width), kind=F32) + [DMA((3,))],
+    )(*returned)
+    return q_grad[None], k_grad[None], v_grad[None], weight_grad
+
+
 def solution(mesh):
     in_specs = (
         P("dp", "seq", None),
@@ -195,4 +521,6 @@
         P("dp", None),
     )
     out_specs = (P("dp", "seq", None), P("dp", "seq", None), P("dp", "seq", None), P("seq", None))
+    by_heads = mesh.shape["seq"] == 8 and mesh.shape["dp"] & (mesh.shape["dp"] - 1) == 0
+    body = head_body if by_heads else halo_body
     return jax.shard_map(body, mesh=mesh, in_specs=in_specs, out_specs=out_specs, check_vma=False)

time: 343 us -> 84 us (0.24)
  the two profiles are of different devices: /device:TPU:17 before, /device:TPU:0 now
where the time goes in v1:
time: 84 us; the launch traced here: 84.2 us
  starting transfers between devices  36.2 us (43%)
  waiting for transfers between devices  30.8 us (37%)
  Pallas kernels  15.3 us (18%)
  other arithmetic  1.11 us (1%)
    ppermute x7, waiting for transfers between devices, move(): return lax.ppermute(value, 'seq', pairs)  23.1 us
    ppermute x7, starting transfers between devices, head_body(): lax.ppermute(block, 'seq', [(i, i ^ n) for i in range(shards)])  17.3 us
    ppermute x7, starting transfers between devices, move(): return lax.ppermute(value, 'seq', pairs)  13.6 us
    ppermute x7, waiting for transfers between devices, head_body(): lax.ppermute(block, 'seq', [(i, i ^ n) for i in range(shards)])  6.55 us
    pallas_call x1, Pallas kernels, head_body(): pl.pallas_call(functools.partial(forward_kernel, early), out_shape=[shape...  6.16 us
    pallas_call x1, Pallas kernels, head_body(): pl.pallas_call(functools.partial(backward_kernel, early), out_shape=[shap...  5.19 us
    all_to_all x1, starting transfers between devices, head_body(): arrived = lax.all_to_all(after(sent, *pieces[1:3]), 'seq', 0, 0, tiled=True)  3.55 us
    pallas_call x1, Pallas kernels, head_body(): pl.pallas_call(spread_kernel, out_shape=pltpu.HBM((shards, 3 * part, tok)...  2.16 us
  transfers between devices with their start and end apart: 17, of which 8 were waited for; matrix products, arithmetic and copies ran while one was open for 1% of the time, Pallas kernels for 16%

profile of v1, /device:TPU:0, one launch (start us, length us, event | category | flops | bytes accessed | tf_op | source)
XLA Modules:
  0.0 84.2 jit_solution(16810062278759023557)
XLA Ops:
  0.6 3.1 %collective-permute-start = (bf16[128,1152]{1,0:T(8,128)(2,1)}, bf16[128,1152]{1,0:T(8,128)(2,1)S(1)}, u32[]{:S(2)}, u32[]{:S(2)}) collective-permute-start(bf16[128,1152]{1,0:T(8,128)(2,1)} %bitcast.7), channel_id=1, source_target_pairs={{0,2},{1,3},{2,0},{3,1},{4,6},{5,7},{6,4},{7,5},{8,10},{9,11},{10,... | collective-permute-start | bytes 884744 | tf_op jit(solution)/shard_map/ppermute | solution.py:423
  3.7 1.5 %collective-permute-start.1 = (bf16[128,1152]{1,0:T(8,128)(2,1)}, bf16[128,1152]{1,0:T(8,128)(2,1)S(1)}, u32[]{:S(2)}, u32[]{:S(2)}) collective-permute-start(bf16[128,1152]{1,0:T(8,128)(2,1)} %bitcast.8), channel_id=1, source_target_pairs={{0,1},{1,0},{2,4},{3,5},{4,2},{5,3},{6,7},{7,6},{8,9},{9,8},{10,12... | collective-permute-start | bytes 884744 | tf_op jit(solution)/shard_map/ppermute | solution.py:423
  5.2 2.2 %shard_map.93 = bf16[8,432,128]{2,1,0:T(8,128)(2,1)} custom-call(bf16[128,1152]{1,0:T(8,128)(2,1)} %bitcast.10, bf16[128,1152]{1,0:T(8,128)(2,1)} %bitcast.11, bf16[128,1152]{1,0:T(8,128)(2,1)} %bitcast.12), custom_call_target="tpu_custom_call" | custom-call | tf_op jit(solution)/shard_map/pallas_call | solution.py:456
  7.4 3.6 %collective-permute-done.refs_1_ = bf16[128,1152]{1,0:T(8,128)(2,1)S(1)} collective-permute-done((bf16[128,1152]{1,0:T(8,128)(2,1)}, bf16[128,1152]{1,0:T(8,128)(2,1)S(1)}, u32[]{:S(2)}, u32[]{:S(2)}) %collective-permute-start) | collective-permute-done | bytes 294944 | tf_op jit(solution)/shard_map/ppermute | solution.py:423
  10.9 0.0 copy-start.4
  10.9 1.5 %collective-permute-done.1.refs_2_ = bf16[128,1152]{1,0:T(8,128)(2,1)S(1)} collective-permute-done((bf16[128,1152]{1,0:T(8,128)(2,1)}, bf16[128,1152]{1,0:T(8,128)(2,1)S(1)}, u32[]{:S(2)}, u32[]{:S(2)}) %collective-permute-start.1) | collective-permute-done | bytes 294944 | tf_op jit(solution)/shard_map/ppermute | solution.py:423
  12.4 0.0 copy-start
  12.4 1.5 %collective-permute-start.2 = (bf16[128,1152]{1,0:T(8,128)(2,1)S(1)}, bf16[128,1152]{1,0:T(8,128)(2,1)S(1)}, u32[]{:S(2)}, u32[]{:S(2)}) collective-permute-start(bf16[128,1152]{1,0:T(8,128)(2,1)S(1)} %collective-permute-done.refs_1_), channel_id=1, source_target_pairs={{0,1},{1,0},{2,4},{3,5},{4,2},{5,3},{6,7},{7,6},{8,9},{9,8},{10,12... | collective-permute-start | bytes 884744 | tf_op jit(solution)/shard_map/ppermute | solution.py:423
  13.9 1.7 %collective-permute-start.3 = (bf16[128,1152]{1,0:T(8,128)(2,1)S(1)}, bf16[128,1152]{1,0:T(8,128)(2,1)S(1)}, u32[]{:S(2)}, u32[]{:S(2)}) collective-permute-start(bf16[128,1152]{1,0:T(8,128)(2,1)S(1)} %collective-permute-done.1.refs_2_), channel_id=1, source_target_pairs={{0,2},{1,3},{2,0},{3,1},{4,6},{5,7},{6,4},{7,5},{8,10},{9,11},{10,... | collective-permute-start | bytes 884744 | tf_op jit(solution)/shard_map/ppermute | solution.py:423
  15.6 3.5 %all-to-all-start = ((bf16[8,432,128]{2,1,0:T(8,128)(2,1)}), bf16[8,432,128]{2,1,0:T(8,128)(2,1)S(1)}, u32[]{:S(2)}, u32[]{:S(2)}) async-start(bf16[8,432,128]{2,1,0:T(8,128)(2,1)} %shard_map.93), calls=%async_computation | async-start | bytes 1769472 | tf_op jit(solution)/shard_map/all_to_all | solution.py:462
  19.1 1.6 %collective-permute-done.2.refs_3_ = bf16[128,1152]{1,0:T(8,128)(2,1)S(1)} collective-permute-done((bf16[128,1152]{1,0:T(8,128)(2,1)S(1)}, bf16[128,1152]{1,0:T(8,128)(2,1)S(1)}, u32[]{:S(2)}, u32[]{:S(2)}) %collective-permute-start.2) | collective-permute-done | bytes 294944 | tf_op jit(solution)/shard_map/ppermute | solution.py:423
  20.7 0.0 copy-start.1
  20.7 2.3 %collective-permute-start.4 = (bf16[128,1152]{1,0:T(8,128)(2,1)S(1)}, bf16[128,1152]{1,0:T(8,128)(2,1)S(1)}, u32[]{:S(2)}, u32[]{:S(2)}) collective-permute-start(bf16[128,1152]{1,0:T(8,128)(2,1)S(1)} %collective-permute-done.2.refs_3_), channel_id=1, source_target_pairs={{0,2},{1,3},{2,0},{3,1},{4,6},{5,7},{6,4},{7,5},{8,10},{9,11},{10,... | collective-permute-start | bytes 884744 | tf_op jit(solution)/shard_map/ppermute | solution.py:423
  23.1 0.0 collective-permute-done.3.refs_4_
  23.1 0.0 copy-start.2
  23.1 2.1 %collective-permute-start.5 = (bf16[128,1152]{1,0:T(8,128)(2,1)S(1)}, bf16[128,1152]{1,0:T(8,128)(2,1)S(1)}, u32[]{:S(2)}, u32[]{:S(2)}) collective-permute-start(bf16[128,1152]{1,0:T(8,128)(2,1)S(1)} %broadcast_select_fusion.1), channel_id=1, source_target_pairs={{0,1},{1,0},{2,3},{3,2},{4,5},{5,4},{6,7},{7,6},{8,9},{9,8},{10,11... | collective-permute-start | bytes 884744 | tf_op jit(solution)/shard_map/ppermute | solution.py:423
  25.2 16.5 %collective-permute-done.4.refs_5_ = bf16[128,1152]{1,0:T(8,128)(2,1)S(1)} collective-permute-done((bf16[128,1152]{1,0:T(8,128)(2,1)S(1)}, bf16[128,1152]{1,0:T(8,128)(2,1)S(1)}, u32[]{:S(2)}, u32[]{:S(2)}) %collective-permute-start.4) | collective-permute-done | bytes 294944 | tf_op jit(solution)/shard_map/ppermute | solution.py:423
  41.7 0.0 copy-start.3
  41.8 1.5 %collective-permute-start.6 = (bf16[128,1152]{1,0:T(8,128)(2,1)S(1)}, bf16[128,1152]{1,0:T(8,128)(2,1)S(1)}, u32[]{:S(2)}, u32[]{:S(2)}) collective-permute-start(bf16[128,1152]{1,0:T(8,128)(2,1)S(1)} %broadcast_select_fusion), channel_id=1, source_target_pairs={{0,1},{1,0},{2,3},{3,2},{4,5},{5,4},{6,7},{7,6},{8,9},{9,8},{10,11... | collective-permute-start | bytes 884744 | tf_op jit(solution)/shard_map/ppermute | solution.py:423
  43.2 0.0 all-to-all-done.in_ref
  43.2 0.0 copy-done.4
  43.2 0.0 copy-done
  43.2 0.0 copy-done.1
  43.2 0.0 copy-done.2
  43.3 0.0 copy-done.3
  43.3 6.2 %shard_map.94 = (bf16[2,80,1024]{2,1,0:T(8,128)(2,1)S(1)}, bf16[2,80,1024]{2,1,0:T(8,128)(2,1)S(1)}, bf16[2,1024,80]{2,1,0:T(8,128)(2,1)S(1)}, bf16[144,1024]{1,...) custom-call(s32[1,4]{1,0:T(1,128)} %len_ref.3, ...), custom_call_target="tpu_custom_call" | custom-call | tf_op jit(solution)/shard_map/pallas_call | solution.py:475
  49.4 0.0 collective-permute-done.5.refs_0_
  49.5 0.0 collective-permute-done.6.refs_1_
  49.5 0.3 shard_map.96
  49.8 0.1 collective-permute-start.13
  49.9 5.2 %shard_map.95 = (bf16[432,128]{1,0:T(8,128)(2,1)S(1)}, bf16[432,128]{1,0:T(8,128)(2,1)}, bf16[432,128]{1,0:T(8,128)(2,1)}, bf16[432,128]{1,0:T(8,128)(2,1)}, bf1...) custom-call(s32[1,4]{1,0:T(1,128)} %len_ref.3, ...), custom_call_target="tpu_custom_call" | custom-call | tf_op jit(solution)/shard_map/pallas_call | solution.py:486
  55.1 0.0 collective-permute-done.13
  55.1 0.1 reduce-precision_convert_fusion
  55.2 1.6 %collective-permute-start.14 = (bf16[144,1152]{1,0:T(8,128)(2,1)S(1)}, bf16[144,1152]{1,0:T(8,128)(2,1)S(1)}, u32[]{:S(2)}, u32[]{:S(2)}) collective-permute-start(bf16[144,1152]{1,0:T(8,128)(2,1)S(1)} %reduce-precision_convert_fusion), channel_id=1, source_target_pairs={{0,16},{8,24},{16,0},{24,8},{1,17},{9,25},{17,1},{25,9},{2,18},{10... | collective-permute-start | bytes 995336 | tf_op jit(solution)/shard_map/ppermute | solution.py:497
  56.8 2.7 %collective-permute-start.7 = (bf16[432,128]{1,0:T(8,128)(2,1)}, bf16[432,128]{1,0:T(8,128)(2,1)S(1)}, u32[]{:S(2)}, u32[]{:S(2)}) collective-permute-start(bf16[432,128]{1,0:T(8,128)(2,1)} %get-tuple-element.40), channel_id=1, source_target_pairs={{0,7},{1,6},{2,5},{3,4},{4,3},{5,2},{6,1},{7,0},{8,15},{9,14},{10,... | collective-permute-start | bytes 331784 | tf_op jit(solution)/shard_map/ppermute | solution.py:505
  59.5 2.2 %collective-permute-start.8 = (bf16[432,128]{1,0:T(8,128)(2,1)}, bf16[432,128]{1,0:T(8,128)(2,1)S(1)}, u32[]{:S(2)}, u32[]{:S(2)}) collective-permute-start(bf16[432,128]{1,0:T(8,128)(2,1)} %get-tuple-element.41), channel_id=1, source_target_pairs={{0,6},{1,7},{2,4},{3,5},{4,2},{5,3},{6,0},{7,1},{8,14},{9,15},{10,... | collective-permute-start | bytes 331784 | tf_op jit(solution)/shard_map/ppermute | solution.py:505
  61.7 0.0 collective-permute-start.9
  61.7 2.7 %collective-permute-start.10 = (bf16[432,128]{1,0:T(8,128)(2,1)}, bf16[432,128]{1,0:T(8,128)(2,1)S(1)}, u32[]{:S(2)}, u32[]{:S(2)}) collective-permute-start(bf16[432,128]{1,0:T(8,128)(2,1)} %get-tuple-element.43), channel_id=1, source_target_pairs={{0,4},{1,5},{2,6},{3,7},{4,0},{5,1},{6,2},{7,3},{8,12},{9,13},{10,... | collective-permute-start | bytes 331784 | tf_op jit(solution)/shard_map/ppermute | solution.py:505
  64.4 1.1 %collective-permute-done.14 = bf16[144,1152]{1,0:T(8,128)(2,1)S(1)} collective-permute-done((bf16[144,1152]{1,0:T(8,128)(2,1)S(1)}, bf16[144,1152]{1,0:T(8,128)(2,1)S(1)}, u32[]{:S(2)}, u32[]{:S(2)}) %collective-permute-start.14) | collective-permute-done | bytes 331808 | tf_op jit(solution)/shard_map/ppermute | solution.py:497
  65.6 1.8 %collective-permute-start.11 = (bf16[432,128]{1,0:T(8,128)(2,1)}, bf16[432,128]{1,0:T(8,128)(2,1)S(1)}, u32[]{:S(2)}, u32[]{:S(2)}) collective-permute-start(bf16[432,128]{1,0:T(8,128)(2,1)} %get-tuple-element.44), channel_id=1, source_target_pairs={{0,3},{1,2},{2,1},{3,0},{4,7},{5,6},{6,5},{7,4},{8,11},{9,10},{10,... | collective-permute-start | bytes 331784 | tf_op jit(solution)/shard_map/ppermute | solution.py:505
  67.4 0.9 %add_multiply_fusion = f32[144,1152]{1,0:T(8,128)} fusion(bf16[144,1152]{1,0:T(8,128)(2,1)S(1)} %collective-permute-done.14, bf16[144,1152]{1,0:T(8,128)(2,1)S(1)} %reduce-precision_convert_fusion), kind=kLoop, calls=%fused_computation | loop fusion | flops 663552 | bytes 1327104 | tf_op jit(solution)/shard_map/mul | solution.py:500
  68.3 0.0 collective-permute-done.7.refs_1_
  68.3 7.7 %collective-permute-start.12 = (bf16[432,128]{1,0:T(8,128)(2,1)}, bf16[432,128]{1,0:T(8,128)(2,1)S(1)}, u32[]{:S(2)}, u32[]{:S(2)}) collective-permute-start(bf16[432,128]{1,0:T(8,128)(2,1)} %get-tuple-element.45), channel_id=1, source_target_pairs={{0,2},{1,3},{2,0},{3,1},{4,6},{5,7},{6,4},{7,5},{8,10},{9,11},{10,... | collective-permute-start | bytes 331784 | tf_op jit(solution)/shard_map/ppermute | solution.py:505
  76.0 0.0 collective-permute-done.8.refs_2_
  76.0 0.1 collective-permute-start.15
  76.2 3.1 %collective-permute-done.9.refs_3_ = bf16[432,128]{1,0:T(8,128)(2,1)S(1)} collective-permute-done((bf16[432,128]{1,0:T(8,128)(2,1)}, bf16[432,128]{1,0:T(8,128)(2,1)S(1)}, u32[]{:S(2)}, u32[]{:S(2)}) %collective-permute-start.9) | collective-permute-done | bytes 110624 | tf_op jit(solution)/shard_map/ppermute | solution.py:505
  79.3 1.1 %collective-permute-done.10.refs_4_ = bf16[432,128]{1,0:T(8,128)(2,1)S(1)} collective-permute-done((bf16[432,128]{1,0:T(8,128)(2,1)}, bf16[432,128]{1,0:T(8,128)(2,1)S(1)}, u32[]{:S(2)}, u32[]{:S(2)}) %collective-permute-start.10) | collective-permute-done | bytes 110624 | tf_op jit(solution)/shard_map/ppermute | solution.py:505
  80.4 0.0 collective-permute-done.11.refs_5_
  80.4 2.3 %collective-permute-done.12.refs_6_ = bf16[432,128]{1,0:T(8,128)(2,1)S(1)} collective-permute-done((bf16[432,128]{1,0:T(8,128)(2,1)}, bf16[432,128]{1,0:T(8,128)(2,1)S(1)}, u32[]{:S(2)}, u32[]{:S(2)}) %collective-permute-start.12) | collective-permute-done | bytes 110624 | tf_op jit(solution)/shard_map/ppermute | solution.py:505
  82.7 0.0 collective-permute-done.15.refs_7_
  82.7 1.5 %shard_map.97 = (f32[128,1152]{1,0:T(8,128)}, f32[128,1152]{1,0:T(8,128)}, f32[128,1152]{1,0:T(8,128)}) custom-call(bf16[432,128]{1,0:T(8,128)(2,1)S(1)} %get-tuple-element.39.refs_0_, bf16[432,128]{1,0:T(8,128)(2,1)S(1)} %collective-permute-done.7.refs_1_, bf16[432,128]{1,0:T(8,128)(2,1)S(1)} %collective-permute-done.8.refs_2_, ...), custom_call_target="tpu_custom_call" | custom-call | tf_op jit(solution)/shard_map/pallas_call | solution.py:506
  (2 shorter events, 0.1 us)
Async XLA Ops:
  0.6 10.3 %collective-permute-start = (bf16[128,1152]{1,0:T(8,128)(2,1)}, bf16[128,1152]{1,0:T(8,128)(2,1)S(1)}, u32[]{:S(2)}, u32[]{:S(2)}) collective-permute-start(bf16[128,1152]{1,0:T(8,128)(2,1)} %bitcast.7), channel_id=1, source_target_pairs={{0,2},{1,3},{2,0},{3,1},{4,6},{5,7},{6,4},{7,5},{8,10},{9,11},{10,... | collective-permute-start | bytes 884744 | tf_op jit(solution)/shard_map/ppermute | solution.py:423
  3.7 8.7 %collective-permute-start.1 = (bf16[128,1152]{1,0:T(8,128)(2,1)}, bf16[128,1152]{1,0:T(8,128)(2,1)S(1)}, u32[]{:S(2)}, u32[]{:S(2)}) collective-permute-start(bf16[128,1152]{1,0:T(8,128)(2,1)} %bitcast.8), channel_id=1, source_target_pairs={{0,1},{1,0},{2,4},{3,5},{4,2},{5,3},{6,7},{7,6},{8,9},{9,8},{10,12... | collective-permute-start | bytes 884744 | tf_op jit(solution)/shard_map/ppermute | solution.py:423
  10.9 32.3 %copy-start.4 = (bf16[128,1152]{1,0:T(8,128)(2,1)}, bf16[128,1152]{1,0:T(8,128)(2,1)S(1)}, u32[]{:S(2)}) copy-start(bf16[128,1152]{1,0:T(8,128)(2,1)S(1)} %collective-permute-done.refs_1_) | copy-start | bytes 884740
  12.4 30.8 %copy-start = (bf16[128,1152]{1,0:T(8,128)(2,1)}, bf16[128,1152]{1,0:T(8,128)(2,1)S(1)}, u32[]{:S(2)}) copy-start(bf16[128,1152]{1,0:T(8,128)(2,1)S(1)} %collective-permute-done.1.refs_2_) | copy-start | bytes 884740
  12.4 8.3 %collective-permute-start.2 = (bf16[128,1152]{1,0:T(8,128)(2,1)S(1)}, bf16[128,1152]{1,0:T(8,128)(2,1)S(1)}, u32[]{:S(2)}, u32[]{:S(2)}) collective-permute-start(bf16[128,1152]{1,0:T(8,128)(2,1)S(1)} %collective-permute-done.refs_1_), channel_id=1, source_target_pairs={{0,1},{1,0},{2,4},{3,5},{4,2},{5,3},{6,7},{7,6},{8,9},{9,8},{10,12... | collective-permute-start | bytes 884744 | tf_op jit(solution)/shard_map/ppermute | solution.py:423
  13.9 9.2 %collective-permute-start.3 = (bf16[128,1152]{1,0:T(8,128)(2,1)S(1)}, bf16[128,1152]{1,0:T(8,128)(2,1)S(1)}, u32[]{:S(2)}, u32[]{:S(2)}) collective-permute-start(bf16[128,1152]{1,0:T(8,128)(2,1)S(1)} %collective-permute-done.1.refs_2_), channel_id=1, source_target_pairs={{0,2},{1,3},{2,0},{3,1},{4,6},{5,7},{6,4},{7,5},{8,10},{9,11},{10,... | collective-permute-start | bytes 884744 | tf_op jit(solution)/shard_map/ppermute | solution.py:423
  15.6 27.7 %all-to-all-start = ((bf16[8,432,128]{2,1,0:T(8,128)(2,1)}), bf16[8,432,128]{2,1,0:T(8,128)(2,1)S(1)}, u32[]{:S(2)}, u32[]{:S(2)}) async-start(bf16[8,432,128]{2,1,0:T(8,128)(2,1)} %shard_map.93), calls=%async_computation | async-start | bytes 1769472 | tf_op jit(solution)/shard_map/all_to_all | solution.py:462
  20.7 22.5 %copy-start.1 = (bf16[128,1152]{1,0:T(8,128)(2,1)}, bf16[128,1152]{1,0:T(8,128)(2,1)S(1)}, u32[]{:S(2)}) copy-start(bf16[128,1152]{1,0:T(8,128)(2,1)S(1)} %collective-permute-done.2.refs_3_) | copy-start | bytes 884740
  20.7 21.0 %collective-permute-start.4 = (bf16[128,1152]{1,0:T(8,128)(2,1)S(1)}, bf16[128,1152]{1,0:T(8,128)(2,1)S(1)}, u32[]{:S(2)}, u32[]{:S(2)}) collective-permute-start(bf16[128,1152]{1,0:T(8,128)(2,1)S(1)} %collective-permute-done.2.refs_3_), channel_id=1, source_target_pairs={{0,2},{1,3},{2,0},{3,1},{4,6},{5,7},{6,4},{7,5},{8,10},{9,11},{10,... | collective-permute-start | bytes 884744 | tf_op jit(solution)/shard_map/ppermute | solution.py:423
  23.1 20.2 %copy-start.2 = (bf16[128,1152]{1,0:T(8,128)(2,1)}, bf16[128,1152]{1,0:T(8,128)(2,1)S(1)}, u32[]{:S(2)}) copy-start(bf16[128,1152]{1,0:T(8,128)(2,1)S(1)} %collective-permute-done.3.refs_4_) | copy-start | bytes 884740
  23.1 26.3 %collective-permute-start.5 = (bf16[128,1152]{1,0:T(8,128)(2,1)S(1)}, bf16[128,1152]{1,0:T(8,128)(2,1)S(1)}, u32[]{:S(2)}, u32[]{:S(2)}) collective-permute-start(bf16[128,1152]{1,0:T(8,128)(2,1)S(1)} %broadcast_select_fusion.1), channel_id=1, source_target_pairs={{0,1},{1,0},{2,3},{3,2},{4,5},{5,4},{6,7},{7,6},{8,9},{9,8},{10,11... | collective-permute-start | bytes 884744 | tf_op jit(solution)/shard_map/ppermute | solution.py:423
  41.7 1.6 %copy-start.3 = (bf16[128,1152]{1,0:T(8,128)(2,1)}, bf16[128,1152]{1,0:T(8,128)(2,1)S(1)}, u32[]{:S(2)}) copy-start(bf16[128,1152]{1,0:T(8,128)(2,1)S(1)} %collective-permute-done.4.refs_5_) | copy-start | bytes 884740
  41.8 7.7 %collective-permute-start.6 = (bf16[128,1152]{1,0:T(8,128)(2,1)S(1)}, bf16[128,1152]{1,0:T(8,128)(2,1)S(1)}, u32[]{:S(2)}, u32[]{:S(2)}) collective-permute-start(bf16[128,1152]{1,0:T(8,128)(2,1)S(1)} %broadcast_select_fusion), channel_id=1, source_target_pairs={{0,1},{1,0},{2,3},{3,2},{4,5},{5,4},{6,7},{7,6},{8,9},{9,8},{10,11... | collective-permute-start | bytes 884744 | tf_op jit(solution)/shard_map/ppermute | solution.py:423
  49.8 5.3 %collective-permute-start.13 = (bf16[144,1152]{1,0:T(8,128)(2,1)S(1)}, bf16[144,1152]{1,0:T(8,128)(2,1)S(1)}, u32[]{:S(2)}, u32[]{:S(2)}) collective-permute-start(bf16[144,1152]{1,0:T(8,128)(2,1)S(1)} %shard_map.96), channel_id=1, source_target_pairs={{0,8},{8,0},{16,24},{24,16},{1,9},{9,1},{17,25},{25,17},{2,10},{10... | collective-permute-start | bytes 995336 | tf_op jit(solution)/shard_map/ppermute | solution.py:497
  55.2 10.4 %collective-permute-start.14 = (bf16[144,1152]{1,0:T(8,128)(2,1)S(1)}, bf16[144,1152]{1,0:T(8,128)(2,1)S(1)}, u32[]{:S(2)}, u32[]{:S(2)}) collective-permute-start(bf16[144,1152]{1,0:T(8,128)(2,1)S(1)} %reduce-precision_convert_fusion), channel_id=1, source_target_pairs={{0,16},{8,24},{16,0},{24,8},{1,17},{9,25},{17,1},{25,9},{2,18},{10... | collective-permute-start | bytes 995336 | tf_op jit(solution)/shard_map/ppermute | solution.py:497
  56.8 11.5 %collective-permute-start.7 = (bf16[432,128]{1,0:T(8,128)(2,1)}, bf16[432,128]{1,0:T(8,128)(2,1)S(1)}, u32[]{:S(2)}, u32[]{:S(2)}) collective-permute-start(bf16[432,128]{1,0:T(8,128)(2,1)} %get-tuple-element.40), channel_id=1, source_target_pairs={{0,7},{1,6},{2,5},{3,4},{4,3},{5,2},{6,1},{7,0},{8,15},{9,14},{10,... | collective-permute-start | bytes 331784 | tf_op jit(solution)/shard_map/ppermute | solution.py:505
  59.5 16.5 %collective-permute-start.8 = (bf16[432,128]{1,0:T(8,128)(2,1)}, bf16[432,128]{1,0:T(8,128)(2,1)S(1)}, u32[]{:S(2)}, u32[]{:S(2)}) collective-permute-start(bf16[432,128]{1,0:T(8,128)(2,1)} %get-tuple-element.41), channel_id=1, source_target_pairs={{0,6},{1,7},{2,4},{3,5},{4,2},{5,3},{6,0},{7,1},{8,14},{9,15},{10,... | collective-permute-start | bytes 331784 | tf_op jit(solution)/shard_map/ppermute | solution.py:505
  61.7 17.6 %collective-permute-start.9 = (bf16[432,128]{1,0:T(8,128)(2,1)}, bf16[432,128]{1,0:T(8,128)(2,1)S(1)}, u32[]{:S(2)}, u32[]{:S(2)}) collective-permute-start(bf16[432,128]{1,0:T(8,128)(2,1)} %get-tuple-element.42), channel_id=1, source_target_pairs={{0,5},{1,4},{2,7},{3,6},{4,1},{5,0},{6,3},{7,2},{8,13},{9,12},{10,... | collective-permute-start | bytes 331784 | tf_op jit(solution)/shard_map/ppermute | solution.py:505
  61.7 18.7 %collective-permute-start.10 = (bf16[432,128]{1,0:T(8,128)(2,1)}, bf16[432,128]{1,0:T(8,128)(2,1)S(1)}, u32[]{:S(2)}, u32[]{:S(2)}) collective-permute-start(bf16[432,128]{1,0:T(8,128)(2,1)} %get-tuple-element.43), channel_id=1, source_target_pairs={{0,4},{1,5},{2,6},{3,7},{4,0},{5,1},{6,2},{7,3},{8,12},{9,13},{10,... | collective-permute-start | bytes 331784 | tf_op jit(solution)/shard_map/ppermute | solution.py:505
  65.6 14.9 %collective-permute-start.11 = (bf16[432,128]{1,0:T(8,128)(2,1)}, bf16[432,128]{1,0:T(8,128)(2,1)S(1)}, u32[]{:S(2)}, u32[]{:S(2)}) collective-permute-start(bf16[432,128]{1,0:T(8,128)(2,1)} %get-tuple-element.44), channel_id=1, source_target_pairs={{0,3},{1,2},{2,1},{3,0},{4,7},{5,6},{6,5},{7,4},{8,11},{9,10},{10,... | collective-permute-start | bytes 331784 | tf_op jit(solution)/shard_map/ppermute | solution.py:505
  68.3 14.4 %collective-permute-start.12 = (bf16[432,128]{1,0:T(8,128)(2,1)}, bf16[432,128]{1,0:T(8,128)(2,1)S(1)}, u32[]{:S(2)}, u32[]{:S(2)}) collective-permute-start(bf16[432,128]{1,0:T(8,128)(2,1)} %get-tuple-element.45), channel_id=1, source_target_pairs={{0,2},{1,3},{2,0},{3,1},{4,6},{5,7},{6,4},{7,5},{8,10},{9,11},{10,... | collective-permute-start | bytes 331784 | tf_op jit(solution)/shard_map/ppermute | solution.py:505
  76.0 6.7 %collective-permute-start.15 = (bf16[432,128]{1,0:T(8,128)(2,1)}, bf16[432,128]{1,0:T(8,128)(2,1)S(1)}, u32[]{:S(2)}, u32[]{:S(2)}) collective-permute-start(bf16[432,128]{1,0:T(8,128)(2,1)} %get-tuple-element.50), channel_id=1, source_target_pairs={{0,1},{1,0},{2,3},{3,2},{4,5},{5,4},{6,7},{7,6},{8,9},{9,8},{10,11... | collective-permute-start | bytes 331784 | tf_op jit(solution)/shard_map/ppermute | solution.py:505

commit v2 on v1

--- a/solution.py
+++ b/solution.py
@@ -226,7 +226,7 @@
     part = blocks[0].shape[0] // 3
     me = lax.axis_index("seq")
     for n, block in enumerate(blocks):
-        turned_s[me ^ (-n % len(blocks))] = block[...]
+        turned_s[me ^ BACK_ORDER[n]] = block[...]
     stores = []
     for i, ref in enumerate((q_ref, k_ref, v_ref)):
         whole = jnp.concatenate([turned_s[n, i * part:(i + 1) * part, :] for n in range(len(blocks))], axis=0)
@@ -403,6 +403,8 @@
     return loads
 
 
+BACK_ORDER = (0, 5, 3, 4, 7, 6, 2, 1)
+FIFTH_PARTS = 4
 INNER_SOURCES = (0, 2, 6, 4, 3, 1, 7, 5)
 OUTER_SOURCES = (0, 2, 1, 3, 4, 6, 5, 7)
 
@@ -427,7 +429,8 @@
     one, two = after(one, event), after(two, event)
     three = move(one, middle)
     four = move(two, along)
-    five = move(three, along)
+    rows = block.shape[0] // FIFTH_PARTS
+    five = jnp.concatenate([move(three[n * rows:(n + 1) * rows], along) for n in range(FIFTH_PARTS)])
     six = move(jnp.where(inner, two, four), across)
     seven = move(jnp.where(inner, three, five), across)
     return (block, one, two, three, four, five, six, seven)
@@ -500,9 +503,10 @@
     weight_grad = sums * (1.0 / math.sqrt(tokens * groups))
 
     returned = [grads[0]]
-    for n in range(shards - 1, 0, -1):
-        block = grads[n] if n > 1 else after(grads[n], weight_grad)
+    for n in BACK_ORDER[1:]:
+        block = after(grads[n], weight_grad) if n == BACK_ORDER[-1] else grads[n]
         returned.append(lax.ppermute(block, "seq", [(i, i ^ n) for i in range(shards)]))
+
     q_grad, k_grad, v_grad = pl.pallas_call(
         collect_kernel, out_shape=[shape((tok, width), F32)] * 3, in_specs=[VMEM] * shards, out_specs=[ANY] * 3,
         compiler_params=PARAMS,

time: 84 us -> 79.4 us (0.945)
  the two profiles are of different devices: /device:TPU:0 before, /device:TPU:17 now
where the time goes in v2:
time: 79.4 us; the launch traced here: 79 us
  waiting for transfers between devices  38.6 us (49%)
  starting transfers between devices  22.4 us (28%)
  Pallas kernels  16 us (20%)
  other arithmetic  1.11 us (1%)
    ppermute x10, waiting for transfers between devices, move(): return lax.ppermute(value, 'seq', pairs)  22.8 us
    ppermute x7, waiting for transfers between devices, head_body(): lax.ppermute(block, 'seq', [(i, i ^ n) for i in range(shards)])  11.1 us
    ppermute x10, starting transfers between devices, move(): return lax.ppermute(value, 'seq', pairs)  8.48 us
    pallas_call x1, Pallas kernels, head_body(): pl.pallas_call(functools.partial(forward_kernel, early), out_shape=[shape...  6.54 us
    ppermute x7, starting transfers between devices, head_body(): lax.ppermute(block, 'seq', [(i, i ^ n) for i in range(shards)])  6.09 us
    pallas_call x1, Pallas kernels, head_body(): pl.pallas_call(functools.partial(backward_kernel, early), out_shape=[shap...  5.51 us
    ppermute x2, waiting for transfers between devices, head_body(): lax.ppermute(w_part, 'dp', pairs)  4.68 us
    all_to_all x1, starting transfers between devices, head_body(): arrived = lax.all_to_all(after(sent, *pieces[1:3]), 'seq', 0, 0, tiled=True)  4.21 us
  transfers between devices with their start and end apart: 20, of which 10 were waited for; matrix products, arithmetic and copies ran while one was open for 1% of the time, Pallas kernels for 18%

profile of v2, /device:TPU:17, one launch (start us, length us, event | category | flops | bytes accessed | tf_op | source)
XLA Modules:
  0.0 79.0 jit_solution(1699817083221517832)
XLA Ops:
  0.6 1.4 %collective-permute-start = (bf16[128,1152]{1,0:T(8,128)(2,1)}, bf16[128,1152]{1,0:T(8,128)(2,1)S(1)}, u32[]{:S(2)}, u32[]{:S(2)}) collective-permute-start(bf16[128,1152]{1,0:T(8,128)(2,1)} %bitcast.7), channel_id=1, source_target_pairs={{0,2},{1,3},{2,0},{3,1},{4,6},{5,7},{6,4},{7,5},{8,10},{9,11},{10,... | collective-permute-start | bytes 884744 | tf_op jit(solution)/shard_map/ppermute | solution.py:425
  2.0 0.0 collective-permute-start.1
  2.0 2.2 %shard_map.93 = bf16[8,432,128]{2,1,0:T(8,128)(2,1)} custom-call(bf16[128,1152]{1,0:T(8,128)(2,1)} %bitcast.10, bf16[128,1152]{1,0:T(8,128)(2,1)} %bitcast.11, bf16[128,1152]{1,0:T(8,128)(2,1)} %bitcast.12), custom_call_target="tpu_custom_call" | custom-call | tf_op jit(solution)/shard_map/pallas_call | solution.py:459
  4.2 4.6 %collective-permute-done.refs_1_ = bf16[128,1152]{1,0:T(8,128)(2,1)S(1)} collective-permute-done((bf16[128,1152]{1,0:T(8,128)(2,1)}, bf16[128,1152]{1,0:T(8,128)(2,1)S(1)}, u32[]{:S(2)}, u32[]{:S(2)}) %collective-permute-start) | collective-permute-done | bytes 294944 | tf_op jit(solution)/shard_map/ppermute | solution.py:425
  8.8 0.0 copy-start.4
  8.8 0.2 collective-permute-start.2
  9.0 0.8 %collective-permute-done.1.refs_2_ = bf16[128,1152]{1,0:T(8,128)(2,1)S(1)} collective-permute-done((bf16[128,1152]{1,0:T(8,128)(2,1)}, bf16[128,1152]{1,0:T(8,128)(2,1)S(1)}, u32[]{:S(2)}, u32[]{:S(2)}) %collective-permute-start.1) | collective-permute-done | bytes 294944 | tf_op jit(solution)/shard_map/ppermute | solution.py:425
  9.8 0.0 copy-start.2
  9.8 1.5 %collective-permute-start.3 = (bf16[128,1152]{1,0:T(8,128)(2,1)S(1)}, bf16[128,1152]{1,0:T(8,128)(2,1)S(1)}, u32[]{:S(2)}, u32[]{:S(2)}) collective-permute-start(bf16[128,1152]{1,0:T(8,128)(2,1)S(1)} %collective-permute-done.1.refs_2_), channel_id=1, source_target_pairs={{0,2},{1,3},{2,0},{3,1},{4,6},{5,7},{6,4},{7,5},{8,10},{9,11},{10,... | collective-permute-start | bytes 884744 | tf_op jit(solution)/shard_map/ppermute | solution.py:425
  11.3 4.2 %all-to-all-start = ((bf16[8,432,128]{2,1,0:T(8,128)(2,1)}), bf16[8,432,128]{2,1,0:T(8,128)(2,1)S(1)}, u32[]{:S(2)}, u32[]{:S(2)}) async-start(bf16[8,432,128]{2,1,0:T(8,128)(2,1)} %shard_map.93), calls=%async_computation | async-start | bytes 1769472 | tf_op jit(solution)/shard_map/all_to_all | solution.py:465
  15.5 0.2 collective-permute-done.2.refs_3_
  15.7 0.0 copy-start
  15.8 1.4 %collective-permute-start.4 = (bf16[32,1152]{1,0:T(8,128)(2,1)S(1)}, bf16[32,1152]{1,0:T(8,128)(2,1)S(1)}, u32[]{:S(2)}, u32[]{:S(2)}) collective-permute-start(bf16[32,1152]{1,0:T(8,128)(2,1)S(1)} %get-tuple-element.57), channel_id=1, source_target_pairs={{0,2},{1,3},{2,0},{3,1},{4,6},{5,7},{6,4},{7,5},{8,10},{9,11},{10,... | collective-permute-start | bytes 221192 | tf_op jit(solution)/shard_map/ppermute | solution.py:425
  17.1 0.2 collective-permute-start.5
  17.3 1.3 %collective-permute-start.6 = (bf16[32,1152]{1,0:T(8,128)(2,1)S(1)}, bf16[32,1152]{1,0:T(8,128)(2,1)S(1)}, u32[]{:S(2)}, u32[]{:S(2)}) collective-permute-start(bf16[32,1152]{1,0:T(8,128)(2,1)S(1)} %get-tuple-element.55), channel_id=1, source_target_pairs={{0,2},{1,3},{2,0},{3,1},{4,6},{5,7},{6,4},{7,5},{8,10},{9,11},{10,... | collective-permute-start | bytes 221192 | tf_op jit(solution)/shard_map/ppermute | solution.py:425
  18.6 0.2 collective-permute-start.7
  18.8 0.0 collective-permute-done.3.refs_4_
  18.8 0.0 copy-start.3
  18.8 1.3 %collective-permute-start.8 = (bf16[128,1152]{1,0:T(8,128)(2,1)S(1)}, bf16[128,1152]{1,0:T(8,128)(2,1)S(1)}, u32[]{:S(2)}, u32[]{:S(2)}) collective-permute-start(bf16[128,1152]{1,0:T(8,128)(2,1)S(1)} %broadcast_select_fusion.1), channel_id=1, source_target_pairs={{0,1},{1,0},{2,3},{3,2},{4,5},{5,4},{6,7},{7,6},{8,9},{9,8},{10,11... | collective-permute-start | bytes 884744 | tf_op jit(solution)/shard_map/ppermute | solution.py:425
  20.1 12.5 %collective-permute-done.4 = bf16[32,1152]{1,0:T(8,128)(2,1)S(1)} collective-permute-done((bf16[32,1152]{1,0:T(8,128)(2,1)S(1)}, bf16[32,1152]{1,0:T(8,128)(2,1)S(1)}, u32[]{:S(2)}, u32[]{:S(2)}) %collective-permute-start.4) | collective-permute-done | bytes 73760 | tf_op jit(solution)/shard_map/ppermute | solution.py:425
  32.5 1.6 %collective-permute-done.5 = bf16[32,1152]{1,0:T(8,128)(2,1)S(1)} collective-permute-done((bf16[32,1152]{1,0:T(8,128)(2,1)S(1)}, bf16[32,1152]{1,0:T(8,128)(2,1)S(1)}, u32[]{:S(2)}, u32[]{:S(2)}) %collective-permute-start.5) | collective-permute-done | bytes 73760 | tf_op jit(solution)/shard_map/ppermute | solution.py:425
  34.1 1.6 %collective-permute-done.6 = bf16[32,1152]{1,0:T(8,128)(2,1)S(1)} collective-permute-done((bf16[32,1152]{1,0:T(8,128)(2,1)S(1)}, bf16[32,1152]{1,0:T(8,128)(2,1)S(1)}, u32[]{:S(2)}, u32[]{:S(2)}) %collective-permute-start.6) | collective-permute-done | bytes 73760 | tf_op jit(solution)/shard_map/ppermute | solution.py:425
  35.7 1.6 %collective-permute-done.7 = bf16[32,1152]{1,0:T(8,128)(2,1)S(1)} collective-permute-done((bf16[32,1152]{1,0:T(8,128)(2,1)S(1)}, bf16[32,1152]{1,0:T(8,128)(2,1)S(1)}, u32[]{:S(2)}, u32[]{:S(2)}) %collective-permute-start.7) | collective-permute-done | bytes 73760 | tf_op jit(solution)/shard_map/ppermute | solution.py:425
  37.3 0.0 copy-start.1
  37.4 1.1 %collective-permute-start.9 = (bf16[128,1152]{1,0:T(8,128)(2,1)S(1)}, bf16[128,1152]{1,0:T(8,128)(2,1)S(1)}, u32[]{:S(2)}, u32[]{:S(2)}) collective-permute-start(bf16[128,1152]{1,0:T(8,128)(2,1)S(1)} %broadcast_select_fusion), channel_id=1, source_target_pairs={{0,1},{1,0},{2,3},{3,2},{4,5},{5,4},{6,7},{7,6},{8,9},{9,8},{10,11... | collective-permute-start | bytes 884744 | tf_op jit(solution)/shard_map/ppermute | solution.py:425
  38.5 0.0 all-to-all-done.in_ref
  38.5 0.0 copy-done.4
  38.5 0.0 copy-done.2
  38.5 0.0 copy-done
  38.5 0.0 copy-done.3
  38.5 0.0 copy-done.1
  38.5 6.5 %shard_map.94 = (bf16[2,80,1024]{2,1,0:T(8,128)(2,1)S(1)}, bf16[2,80,1024]{2,1,0:T(8,128)(2,1)S(1)}, bf16[2,1024,80]{2,1,0:T(8,128)(2,1)S(1)}, bf16[144,1024]{1,...) custom-call(s32[1,4]{1,0:T(1,128)} %len_ref.3, ...), custom_call_target="tpu_custom_call" | custom-call | tf_op jit(solution)/shard_map/pallas_call | solution.py:478
  45.1 0.0 collective-permute-done.8.refs_0_
  45.1 0.0 collective-permute-done.9.refs_1_
  45.1 0.3 shard_map.96
  45.5 2.6 %collective-permute-start.16 = (bf16[144,1152]{1,0:T(8,128)(2,1)S(1)}, bf16[144,1152]{1,0:T(8,128)(2,1)S(1)}, u32[]{:S(2)}, u32[]{:S(2)}) collective-permute-start(bf16[144,1152]{1,0:T(8,128)(2,1)S(1)} %shard_map.96), channel_id=1, source_target_pairs={{0,8},{8,0},{16,24},{24,16},{1,9},{9,1},{17,25},{25,17},{2,10},{10... | collective-permute-start | bytes 995336 | tf_op jit(solution)/shard_map/ppermute | solution.py:500
  48.1 5.5 %shard_map.95 = (bf16[432,128]{1,0:T(8,128)(2,1)S(1)}, bf16[432,128]{1,0:T(8,128)(2,1)}, bf16[432,128]{1,0:T(8,128)(2,1)}, bf16[432,128]{1,0:T(8,128)(2,1)}, bf1...) custom-call(s32[1,4]{1,0:T(1,128)} %len_ref.3, ...), custom_call_target="tpu_custom_call" | custom-call | tf_op jit(solution)/shard_map/pallas_call | solution.py:489
  53.6 0.0 collective-permute-done.16
  53.6 0.1 reduce-precision_convert_fusion
  53.7 1.0 %collective-permute-start.17 = (bf16[144,1152]{1,0:T(8,128)(2,1)S(1)}, bf16[144,1152]{1,0:T(8,128)(2,1)S(1)}, u32[]{:S(2)}, u32[]{:S(2)}) collective-permute-start(bf16[144,1152]{1,0:T(8,128)(2,1)S(1)} %reduce-precision_convert_fusion), channel_id=1, source_target_pairs={{0,16},{8,24},{16,0},{24,8},{1,17},{9,25},{17,1},{25,9},{2,18},{10... | collective-permute-start | bytes 995336 | tf_op jit(solution)/shard_map/ppermute | solution.py:500
  54.7 0.4 collective-permute-start.10
  55.1 2.2 %collective-permute-start.11 = (bf16[432,128]{1,0:T(8,128)(2,1)}, bf16[432,128]{1,0:T(8,128)(2,1)S(1)}, u32[]{:S(2)}, u32[]{:S(2)}) collective-permute-start(bf16[432,128]{1,0:T(8,128)(2,1)} %get-tuple-element.41), channel_id=1, source_target_pairs={{0,3},{1,2},{2,1},{3,0},{4,7},{5,6},{6,5},{7,4},{8,11},{9,10},{10,... | collective-permute-start | bytes 331784 | tf_op jit(solution)/shard_map/ppermute | solution.py:508
  57.3 1.5 %collective-permute-start.12 = (bf16[432,128]{1,0:T(8,128)(2,1)}, bf16[432,128]{1,0:T(8,128)(2,1)S(1)}, u32[]{:S(2)}, u32[]{:S(2)}) collective-permute-start(bf16[432,128]{1,0:T(8,128)(2,1)} %get-tuple-element.42), channel_id=1, source_target_pairs={{0,4},{1,5},{2,6},{3,7},{4,0},{5,1},{6,2},{7,3},{8,12},{9,13},{10,... | collective-permute-start | bytes 331784 | tf_op jit(solution)/shard_map/ppermute | solution.py:508
  58.8 0.0 collective-permute-start.13
  58.8 4.7 %collective-permute-done.17 = bf16[144,1152]{1,0:T(8,128)(2,1)S(1)} collective-permute-done((bf16[144,1152]{1,0:T(8,128)(2,1)S(1)}, bf16[144,1152]{1,0:T(8,128)(2,1)S(1)}, u32[]{:S(2)}, u32[]{:S(2)}) %collective-permute-start.17) | collective-permute-done | bytes 331808 | tf_op jit(solution)/shard_map/ppermute | solution.py:500
  63.4 0.5 collective-permute-start.14
  63.9 0.9 %add_multiply_fusion = f32[144,1152]{1,0:T(8,128)} fusion(bf16[144,1152]{1,0:T(8,128)(2,1)S(1)} %collective-permute-done.17, bf16[144,1152]{1,0:T(8,128)(2,1)S(1)} %reduce-precision_convert_fusion), kind=kLoop, calls=%fused_computation | loop fusion | flops 663552 | bytes 1327104 | tf_op jit(solution)/shard_map/mul | solution.py:503
  64.9 0.0 collective-permute-done.10.refs_1_
  64.9 0.8 %collective-permute-start.15 = (bf16[432,128]{1,0:T(8,128)(2,1)}, bf16[432,128]{1,0:T(8,128)(2,1)S(1)}, u32[]{:S(2)}, u32[]{:S(2)}) collective-permute-start(bf16[432,128]{1,0:T(8,128)(2,1)} %get-tuple-element.45), channel_id=1, source_target_pairs={{0,2},{1,3},{2,0},{3,1},{4,6},{5,7},{6,4},{7,5},{8,10},{9,11},{10,... | collective-permute-start | bytes 331784 | tf_op jit(solution)/shard_map/ppermute | solution.py:508
  65.7 0.0 collective-permute-done.11.refs_2_
  65.7 0.7 collective-permute-start.18
  66.4 0.0 collective-permute-done.12.refs_3_
  66.4 8.8 %collective-permute-done.13.refs_4_ = bf16[432,128]{1,0:T(8,128)(2,1)S(1)} collective-permute-done((bf16[432,128]{1,0:T(8,128)(2,1)}, bf16[432,128]{1,0:T(8,128)(2,1)S(1)}, u32[]{:S(2)}, u32[]{:S(2)}) %collective-permute-start.13) | collective-permute-done | bytes 110624 | tf_op jit(solution)/shard_map/ppermute | solution.py:508
  75.2 2.3 %collective-permute-done.14.refs_5_ = bf16[432,128]{1,0:T(8,128)(2,1)S(1)} collective-permute-done((bf16[432,128]{1,0:T(8,128)(2,1)}, bf16[432,128]{1,0:T(8,128)(2,1)S(1)}, u32[]{:S(2)}, u32[]{:S(2)}) %collective-permute-start.14) | collective-permute-done | bytes 110624 | tf_op jit(solution)/shard_map/ppermute | solution.py:508
  77.5 0.0 collective-permute-done.15.refs_6_
  77.5 0.0 collective-permute-done.18.refs_7_
  77.5 1.5 %shard_map.97 = (f32[128,1152]{1,0:T(8,128)}, f32[128,1152]{1,0:T(8,128)}, f32[128,1152]{1,0:T(8,128)}) custom-call(bf16[432,128]{1,0:T(8,128)(2,1)S(1)} %get-tuple-element.39.refs_0_, bf16[432,128]{1,0:T(8,128)(2,1)S(1)} %collective-permute-done.10.refs_1_, bf16[432,128]{1,0:T(8,128)(2,1)S(1)} %collective-permute-done.11.refs_2_, ...), custom_call_target="tpu_custom_call" | custom-call | tf_op jit(solution)/shard_map/pallas_call | solution.py:510
  (7 shorter events, 0.1 us)
Async XLA Ops:
  0.6 8.2 %collective-permute-start = (bf16[128,1152]{1,0:T(8,128)(2,1)}, bf16[128,1152]{1,0:T(8,128)(2,1)S(1)}, u32[]{:S(2)}, u32[]{:S(2)}) collective-permute-start(bf16[128,1152]{1,0:T(8,128)(2,1)} %bitcast.7), channel_id=1, source_target_pairs={{0,2},{1,3},{2,0},{3,1},{4,6},{5,7},{6,4},{7,5},{8,10},{9,11},{10,... | collective-permute-start | bytes 884744 | tf_op jit(solution)/shard_map/ppermute | solution.py:425
  2.0 7.8 %collective-permute-start.1 = (bf16[128,1152]{1,0:T(8,128)(2,1)}, bf16[128,1152]{1,0:T(8,128)(2,1)S(1)}, u32[]{:S(2)}, u32[]{:S(2)}) collective-permute-start(bf16[128,1152]{1,0:T(8,128)(2,1)} %bitcast.8), channel_id=1, source_target_pairs={{0,1},{1,0},{2,4},{3,5},{4,2},{5,3},{6,7},{7,6},{8,9},{9,8},{10,12... | collective-permute-start | bytes 884744 | tf_op jit(solution)/shard_map/ppermute | solution.py:425
  8.8 29.7 %copy-start.4 = (bf16[128,1152]{1,0:T(8,128)(2,1)}, bf16[128,1152]{1,0:T(8,128)(2,1)S(1)}, u32[]{:S(2)}) copy-start(bf16[128,1152]{1,0:T(8,128)(2,1)S(1)} %collective-permute-done.refs_1_) | copy-start | bytes 884740
  8.8 7.0 %collective-permute-start.2 = (bf16[128,1152]{1,0:T(8,128)(2,1)S(1)}, bf16[128,1152]{1,0:T(8,128)(2,1)S(1)}, u32[]{:S(2)}, u32[]{:S(2)}) collective-permute-start(bf16[128,1152]{1,0:T(8,128)(2,1)S(1)} %collective-permute-done.refs_1_), channel_id=1, source_target_pairs={{0,1},{1,0},{2,4},{3,5},{4,2},{5,3},{6,7},{7,6},{8,9},{9,8},{10,12... | collective-permute-start | bytes 884744 | tf_op jit(solution)/shard_map/ppermute | solution.py:425
  9.8 28.7 %copy-start.2 = (bf16[128,1152]{1,0:T(8,128)(2,1)}, bf16[128,1152]{1,0:T(8,128)(2,1)S(1)}, u32[]{:S(2)}) copy-start(bf16[128,1152]{1,0:T(8,128)(2,1)S(1)} %collective-permute-done.1.refs_2_) | copy-start | bytes 884740
  9.8 9.0 %collective-permute-start.3 = (bf16[128,1152]{1,0:T(8,128)(2,1)S(1)}, bf16[128,1152]{1,0:T(8,128)(2,1)S(1)}, u32[]{:S(2)}, u32[]{:S(2)}) collective-permute-start(bf16[128,1152]{1,0:T(8,128)(2,1)S(1)} %collective-permute-done.1.refs_2_), channel_id=1, source_target_pairs={{0,2},{1,3},{2,0},{3,1},{4,6},{5,7},{6,4},{7,5},{8,10},{9,11},{10,... | collective-permute-start | bytes 884744 | tf_op jit(solution)/shard_map/ppermute | solution.py:425
  11.3 27.2 %all-to-all-start = ((bf16[8,432,128]{2,1,0:T(8,128)(2,1)}), bf16[8,432,128]{2,1,0:T(8,128)(2,1)S(1)}, u32[]{:S(2)}, u32[]{:S(2)}) async-start(bf16[8,432,128]{2,1,0:T(8,128)(2,1)} %shard_map.93), calls=%async_computation | async-start | bytes 1769472 | tf_op jit(solution)/shard_map/all_to_all | solution.py:465
  15.7 22.8 %copy-start = (bf16[128,1152]{1,0:T(8,128)(2,1)}, bf16[128,1152]{1,0:T(8,128)(2,1)S(1)}, u32[]{:S(2)}) copy-start(bf16[128,1152]{1,0:T(8,128)(2,1)S(1)} %collective-permute-done.2.refs_3_) | copy-start | bytes 884740
  15.8 16.8 %collective-permute-start.4 = (bf16[32,1152]{1,0:T(8,128)(2,1)S(1)}, bf16[32,1152]{1,0:T(8,128)(2,1)S(1)}, u32[]{:S(2)}, u32[]{:S(2)}) collective-permute-start(bf16[32,1152]{1,0:T(8,128)(2,1)S(1)} %get-tuple-element.57), channel_id=1, source_target_pairs={{0,2},{1,3},{2,0},{3,1},{4,6},{5,7},{6,4},{7,5},{8,10},{9,11},{10,... | collective-permute-start | bytes 221192 | tf_op jit(solution)/shard_map/ppermute | solution.py:425
  17.1 17.0 %collective-permute-start.5 = (bf16[32,1152]{1,0:T(8,128)(2,1)S(1)}, bf16[32,1152]{1,0:T(8,128)(2,1)S(1)}, u32[]{:S(2)}, u32[]{:S(2)}) collective-permute-start(bf16[32,1152]{1,0:T(8,128)(2,1)S(1)} %get-tuple-element.56), channel_id=1, source_target_pairs={{0,2},{1,3},{2,0},{3,1},{4,6},{5,7},{6,4},{7,5},{8,10},{9,11},{10,... | collective-permute-start | bytes 221192 | tf_op jit(solution)/shard_map/ppermute | solution.py:425
  17.3 18.4 %collective-permute-start.6 = (bf16[32,1152]{1,0:T(8,128)(2,1)S(1)}, bf16[32,1152]{1,0:T(8,128)(2,1)S(1)}, u32[]{:S(2)}, u32[]{:S(2)}) collective-permute-start(bf16[32,1152]{1,0:T(8,128)(2,1)S(1)} %get-tuple-element.55), channel_id=1, source_target_pairs={{0,2},{1,3},{2,0},{3,1},{4,6},{5,7},{6,4},{7,5},{8,10},{9,11},{10,... | collective-permute-start | bytes 221192 | tf_op jit(solution)/shard_map/ppermute | solution.py:425
  18.6 18.7 %collective-permute-start.7 = (bf16[32,1152]{1,0:T(8,128)(2,1)S(1)}, bf16[32,1152]{1,0:T(8,128)(2,1)S(1)}, u32[]{:S(2)}, u32[]{:S(2)}) collective-permute-start(bf16[32,1152]{1,0:T(8,128)(2,1)S(1)} %get-tuple-element.54), channel_id=1, source_target_pairs={{0,2},{1,3},{2,0},{3,1},{4,6},{5,7},{6,4},{7,5},{8,10},{9,11},{10,... | collective-permute-start | bytes 221192 | tf_op jit(solution)/shard_map/ppermute | solution.py:425
  18.8 19.7 %copy-start.3 = (bf16[128,1152]{1,0:T(8,128)(2,1)}, bf16[128,1152]{1,0:T(8,128)(2,1)S(1)}, u32[]{:S(2)}) copy-start(bf16[128,1152]{1,0:T(8,128)(2,1)S(1)} %collective-permute-done.3.refs_4_) | copy-start | bytes 884740
  18.8 26.3 %collective-permute-start.8 = (bf16[128,1152]{1,0:T(8,128)(2,1)S(1)}, bf16[128,1152]{1,0:T(8,128)(2,1)S(1)}, u32[]{:S(2)}, u32[]{:S(2)}) collective-permute-start(bf16[128,1152]{1,0:T(8,128)(2,1)S(1)} %broadcast_select_fusion.1), channel_id=1, source_target_pairs={{0,1},{1,0},{2,3},{3,2},{4,5},{5,4},{6,7},{7,6},{8,9},{9,8},{10,11... | collective-permute-start | bytes 884744 | tf_op jit(solution)/shard_map/ppermute | solution.py:425
  37.3 1.2 %copy-start.1 = (bf16[128,1152]{1,0:T(8,128)(2,1)}, bf16[128,1152]{1,0:T(8,128)(2,1)S(1)}, u32[]{:S(2)}) copy-start(bf16[128,1152]{1,0:T(8,128)(2,1)S(1)} %constant_dynamic-update-slice_fusion.refs_5_) | copy-start | bytes 884740
  37.4 7.7 %collective-permute-start.9 = (bf16[128,1152]{1,0:T(8,128)(2,1)S(1)}, bf16[128,1152]{1,0:T(8,128)(2,1)S(1)}, u32[]{:S(2)}, u32[]{:S(2)}) collective-permute-start(bf16[128,1152]{1,0:T(8,128)(2,1)S(1)} %broadcast_select_fusion), channel_id=1, source_target_pairs={{0,1},{1,0},{2,3},{3,2},{4,5},{5,4},{6,7},{7,6},{8,9},{9,8},{10,11... | collective-permute-start | bytes 884744 | tf_op jit(solution)/shard_map/ppermute | solution.py:425
  45.5 8.2 %collective-permute-start.16 = (bf16[144,1152]{1,0:T(8,128)(2,1)S(1)}, bf16[144,1152]{1,0:T(8,128)(2,1)S(1)}, u32[]{:S(2)}, u32[]{:S(2)}) collective-permute-start(bf16[144,1152]{1,0:T(8,128)(2,1)S(1)} %shard_map.96), channel_id=1, source_target_pairs={{0,8},{8,0},{16,24},{24,16},{1,9},{9,1},{17,25},{25,17},{2,10},{10... | collective-permute-start | bytes 995336 | tf_op jit(solution)/shard_map/ppermute | solution.py:500
  53.7 9.7 %collective-permute-start.17 = (bf16[144,1152]{1,0:T(8,128)(2,1)S(1)}, bf16[144,1152]{1,0:T(8,128)(2,1)S(1)}, u32[]{:S(2)}, u32[]{:S(2)}) collective-permute-start(bf16[144,1152]{1,0:T(8,128)(2,1)S(1)} %reduce-precision_convert_fusion), channel_id=1, source_target_pairs={{0,16},{8,24},{16,0},{24,8},{1,17},{9,25},{17,1},{25,9},{2,18},{10... | collective-permute-start | bytes 995336 | tf_op jit(solution)/shard_map/ppermute | solution.py:500
  54.7 10.2 %collective-permute-start.10 = (bf16[432,128]{1,0:T(8,128)(2,1)}, bf16[432,128]{1,0:T(8,128)(2,1)S(1)}, u32[]{:S(2)}, u32[]{:S(2)}) collective-permute-start(bf16[432,128]{1,0:T(8,128)(2,1)} %get-tuple-element.40), channel_id=1, source_target_pairs={{0,5},{1,4},{2,7},{3,6},{4,1},{5,0},{6,3},{7,2},{8,13},{9,12},{10,... | collective-permute-start | bytes 331784 | tf_op jit(solution)/shard_map/ppermute | solution.py:508
  55.1 10.6 %collective-permute-start.11 = (bf16[432,128]{1,0:T(8,128)(2,1)}, bf16[432,128]{1,0:T(8,128)(2,1)S(1)}, u32[]{:S(2)}, u32[]{:S(2)}) collective-permute-start(bf16[432,128]{1,0:T(8,128)(2,1)} %get-tuple-element.41), channel_id=1, source_target_pairs={{0,3},{1,2},{2,1},{3,0},{4,7},{5,6},{6,5},{7,4},{8,11},{9,10},{10,... | collective-permute-start | bytes 331784 | tf_op jit(solution)/shard_map/ppermute | solution.py:508
  57.3 9.2 %collective-permute-start.12 = (bf16[432,128]{1,0:T(8,128)(2,1)}, bf16[432,128]{1,0:T(8,128)(2,1)S(1)}, u32[]{:S(2)}, u32[]{:S(2)}) collective-permute-start(bf16[432,128]{1,0:T(8,128)(2,1)} %get-tuple-element.42), channel_id=1, source_target_pairs={{0,4},{1,5},{2,6},{3,7},{4,0},{5,1},{6,2},{7,3},{8,12},{9,13},{10,... | collective-permute-start | bytes 331784 | tf_op jit(solution)/shard_map/ppermute | solution.py:508
  58.8 16.5 %collective-permute-start.13 = (bf16[432,128]{1,0:T(8,128)(2,1)}, bf16[432,128]{1,0:T(8,128)(2,1)S(1)}, u32[]{:S(2)}, u32[]{:S(2)}) collective-permute-start(bf16[432,128]{1,0:T(8,128)(2,1)} %get-tuple-element.43), channel_id=1, source_target_pairs={{0,7},{1,6},{2,5},{3,4},{4,3},{5,2},{6,1},{7,0},{8,15},{9,14},{10,... | collective-permute-start | bytes 331784 | tf_op jit(solution)/shard_map/ppermute | solution.py:508
  63.4 14.1 %collective-permute-start.14 = (bf16[432,128]{1,0:T(8,128)(2,1)}, bf16[432,128]{1,0:T(8,128)(2,1)S(1)}, u32[]{:S(2)}, u32[]{:S(2)}) collective-permute-start(bf16[432,128]{1,0:T(8,128)(2,1)} %get-tuple-element.44), channel_id=1, source_target_pairs={{0,6},{1,7},{2,4},{3,5},{4,2},{5,3},{6,0},{7,1},{8,14},{9,15},{10,... | collective-permute-start | bytes 331784 | tf_op jit(solution)/shard_map/ppermute | solution.py:508
  64.9 12.7 %collective-permute-start.15 = (bf16[432,128]{1,0:T(8,128)(2,1)}, bf16[432,128]{1,0:T(8,128)(2,1)S(1)}, u32[]{:S(2)}, u32[]{:S(2)}) collective-permute-start(bf16[432,128]{1,0:T(8,128)(2,1)} %get-tuple-element.45), channel_id=1, source_target_pairs={{0,2},{1,3},{2,0},{3,1},{4,6},{5,7},{6,4},{7,5},{8,10},{9,11},{10,... | collective-permute-start | bytes 331784 | tf_op jit(solution)/shard_map/ppermute | solution.py:508
  65.7 11.8 %collective-permute-start.18 = (bf16[432,128]{1,0:T(8,128)(2,1)}, bf16[432,128]{1,0:T(8,128)(2,1)S(1)}, u32[]{:S(2)}, u32[]{:S(2)}) collective-permute-start(bf16[432,128]{1,0:T(8,128)(2,1)} %get-tuple-element.50), channel_id=1, source_target_pairs={{0,1},{1,0},{2,3},{3,2},{4,5},{5,4},{6,7},{7,6},{8,9},{9,8},{10,11... | collective-permute-start | bytes 331784 | tf_op jit(solution)/shard_map/ppermute | solution.py:508

commit v3 on v2

--- a/solution.py
+++ b/solution.py
@@ -267,16 +267,17 @@
         ref[head, :, columns] = jnp.concatenate([rows, filler], axis=0).astype(BF16)
 
 
-def joined(ref):
-    return jnp.concatenate([ref[head, 0:HEAD_DIM, :] for head in range(ref.shape[0])], axis=0).astype(BF16)
+def joined(ref, turned=False):
+    heads = [ref[head].T if turned else ref[head] for head in range(ref.shape[0])]
+    return jnp.concatenate([block[0:HEAD_DIM, :] for block in heads], axis=0).astype(BF16)
 
 
 def forward_kernel(early, len_ref, w_ref, in_ref, *refs):
     pieces = refs[:early]
-    (q_s, k_s, vt_s, att_s, probs_s, d_s, wg_s, w_s, len_s, v_s, kt_s, sum_s, dy_s, len_sem, w_sem, dy_sem) = refs[early:]
+    (qt_s, k_s, vt_s, att_s, probs_s, d_s, wg_s, w_s, len_s, q_s, v_s, kt_s, sum_s, dy_s, len_sem, w_sem, dy_sem) = refs[early:]
     shards, height, tok = in_ref.shape
     part = height // 3
-    heads = q_s.shape[0]
+    heads = k_s.shape[0]
     scale = HEAD_DIM ** (-0.5)
 
     load_len = pltpu.make_async_copy(len_ref, len_s, len_sem)
@@ -289,6 +290,7 @@
         for i, ref in enumerate((q_s, k_s, v_s)):
             store_heads(ref, in_ref[shard, i * part:(i + 1) * part, :].astype(F32), columns)
     for head in range(heads):
+        qt_s[head] = q_s[head].T
         kt_s[head] = k_s[head].T
         vt_s[head] = v_s[head].T
     load_len.wait()
@@ -323,10 +325,10 @@
     wg_s[...] = dot(att_s[...], dy_s[...])
 
 
-def backward_kernel(early, len_ref, w_s, q_s, k_s, vt_s, att_s, probs_s, d_ref, *refs):
+def backward_kernel(early, len_ref, w_s, qt_s, k_s, vt_s, att_s, probs_s, d_ref, *refs):
     late = refs[:8 - early]
     outs = refs[8 - early:16 - early]
-    (len_s, d_s, dq_s, dk_s, dv_s, out_s, len_sem, out_sem) = refs[16 - early:]
+    (len_s, d_s, dt_s, dq_s, dk_s, dv_s, out_s, len_sem, out_sem) = refs[16 - early:]
     shards, height, tok = out_s.shape
     part = height // 3
     heads = d_s.shape[0]
@@ -338,6 +340,8 @@
         ref[...] = jnp.zeros_like(ref)
     for n, piece in enumerate(late):
         store_heads(d_s, dot(w_s[...], piece[...], NT), piece_columns(early + n, tok))
+    for head in range(heads):
+        dt_s[head] = d_s[head].T
     load_len.wait()
 
     def work(image, count, first, start, end):
@@ -352,14 +356,14 @@
             d_probs = dot(vt_s[head, columns, :], d)
             d_scores = (scale * probs.astype(F32) * (d_probs - delta)).astype(BF16)
             dq_s[head, :, columns] += dot(k_s[head, :, columns], d_scores)
-            dk_s[head, :, columns] += dot(q_s[head, :, columns], d_scores, NT)
-            dv_s[head, :, columns] += dot(d, probs, NT)
+            dk_s[head, columns, :] += dot(d_scores, qt_s[head, columns, :])
+            dv_s[head, columns, :] += dot(probs, dt_s[head, columns, :])
 
     each_image(len_s, tok, shards, work)
 
     stores = []
     for i, ref in enumerate((dq_s, dk_s, dv_s)):
-        whole = joined(ref)
+        whole = joined(ref, turned=i > 0)
         for shard in range(shards):
             out_s[shard, i * part:(i + 1) * part, :] = whole[:, shard * tok:(shard + 1) * tok]
     me = lax.axis_index("seq")
@@ -403,7 +407,7 @@
     return loads
 
 
-BACK_ORDER = (0, 5, 3, 4, 7, 6, 2, 1)
+BACK_ORDER = (0, 5, 3, 4, 2, 7, 6, 1)
 FIFTH_PARTS = 4
 INNER_SOURCES = (0, 2, 6, 4, 3, 1, 7, 5)
 OUTER_SOURCES = (0, 2, 1, 3, 4, 6, 5, 7)
@@ -475,11 +479,11 @@
     len_s = pltpu.SMEM((1, images), jnp.int32)
     early = 6
     late = len(pieces) - early
-    q_t, k_t, v_r, attended, probs, d_part, w_early, w_rows = pl.pallas_call(
+    q_r, k_t, v_r, attended, probs, d_part, w_early, w_rows = pl.pallas_call(
         functools.partial(forward_kernel, early),
-        out_shape=[shape(wide), shape(wide), shape(tall), shape(flat), shape(chance), shape(wide), shape((part, width), F32), shape((part, width))],
+        out_shape=[shape(tall), shape(wide), shape(tall), shape(flat), shape(chance), shape(wide), shape((part, width), F32), shape((part, width))],
         in_specs=[HBM, HBM, VMEM] + [HBM] * early, out_specs=[VMEM] * 8, compiler_params=PARAMS,
-        scratch_shapes=[len_s] + scratch(wide, tall) + scratch(wide, kind=F32) + scratch((tokens, width))
+        scratch_shapes=[len_s] + scratch(wide, wide, tall) + scratch(wide, kind=F32) + scratch((tokens, width))
         + [DMA, DMA, DMA((early,))],
     )(*in_hbm(lengths, out_weight), arrived, *in_hbm(*pieces[:early]))
     w_part = pl.pallas_call(
@@ -490,9 +494,9 @@
         functools.partial(backward_kernel, early),
         out_shape=[shape((3 * part, tok))] + [pltpu.HBM((3 * part, tok), BF16)] * (shards - 1),
         in_specs=[HBM] + [VMEM] * (7 + late), out_specs=[VMEM] + [HBM] * (shards - 1), compiler_params=PARAMS,
-        scratch_shapes=[len_s] + scratch(wide) + scratch(wide, wide, wide, kind=F32)
+        scratch_shapes=[len_s] + scratch(wide, tall) + scratch(wide, tall, tall, kind=F32)
         + scratch((shards, 3 * part, tok)) + [DMA, DMA((shards,))],
-    )(*in_hbm(lengths), w_rows, q_t, k_t, v_r, attended, probs, d_part, *pieces[early:])
+    )(*in_hbm(lengths), w_rows, q_r, k_t, v_r, attended, probs, d_part, *pieces[early:])
     sums = w_part.astype(F32)
     step = 1
     while step < groups:

time: 79.4 us -> 79.6 us (level)
  waiting for transfers between devices: 38.6 us -> 37.3 us
  starting transfers between devices: 22.4 us -> 23.6 us
    ppermute x7, starting transfers between devices: 6.09 us -> 7.38 us  [head_body(): lax.ppermute(block, 'seq', [(i, i ^ n) for i in range(shards)])]
    ppermute x7, waiting for transfers between devices: 11.1 us -> 10.3 us  [head_body(): lax.ppermute(block, 'seq', [(i, i ^ n) for i in range(shards)])]
where the time goes in v3:
time: 79.6 us; the launch traced here: 79.4 us
  waiting for transfers between devices  37.3 us (47%)
  starting transfers between devices  23.6 us (30%)
  Pallas kernels  16.4 us (21%)
  other arithmetic  1.11 us (1%)
    ppermute x10, waiting for transfers between devices, move(): return lax.ppermute(value, 'seq', pairs)  22.8 us
    ppermute x7, waiting for transfers between devices, head_body(): lax.ppermute(block, 'seq', [(i, i ^ n) for i in range(shards)])  10.3 us
    ppermute x10, starting transfers between devices, move(): return lax.ppermute(value, 'seq', pairs)  8.48 us
    ppermute x7, starting transfers between devices, head_body(): lax.ppermute(block, 'seq', [(i, i ^ n) for i in range(shards)])  7.38 us
    pallas_call x1, Pallas kernels, head_body(): pl.pallas_call(functools.partial(forward_kernel, early), out_shape=[shape...  6.73 us
    pallas_call x1, Pallas kernels, head_body(): pl.pallas_call(functools.partial(backward_kernel, early), out_shape=[shap...  5.74 us
    ppermute x2, waiting for transfers between devices, head_body(): lax.ppermute(w_part, 'dp', pairs)  4.23 us
    all_to_all x1, starting transfers between devices, head_body(): arrived = lax.all_to_all(after(sent, *pieces[1:3]), 'seq', 0, 0, tiled=True)  4.21 us
  transfers between devices with their start and end apart: 20, of which 10 were waited for; matrix products, arithmetic and copies ran while one was open for 1% of the time, Pallas kernels for 18%

profile of v3, /device:TPU:17, one launch (start us, length us, event | category | flops | bytes accessed | tf_op | source)
XLA Modules:
  0.0 79.4 jit_solution(11716151682592369920)
XLA Ops:
  0.6 1.4 %collective-permute-start = (bf16[128,1152]{1,0:T(8,128)(2,1)}, bf16[128,1152]{1,0:T(8,128)(2,1)S(1)}, u32[]{:S(2)}, u32[]{:S(2)}) collective-permute-start(bf16[128,1152]{1,0:T(8,128)(2,1)} %bitcast.7), channel_id=1, source_target_pairs={{0,2},{1,3},{2,0},{3,1},{4,6},{5,7},{6,4},{7,5},{8,10},{9,11},{10,... | collective-permute-start | bytes 884744 | tf_op jit(solution)/shard_map/ppermute | solution.py:429
  2.0 0.0 collective-permute-start.1
  2.0 2.2 %shard_map.93 = bf16[8,432,128]{2,1,0:T(8,128)(2,1)} custom-call(bf16[128,1152]{1,0:T(8,128)(2,1)} %bitcast.10, bf16[128,1152]{1,0:T(8,128)(2,1)} %bitcast.11, bf16[128,1152]{1,0:T(8,128)(2,1)} %bitcast.12), custom_call_target="tpu_custom_call" | custom-call | tf_op jit(solution)/shard_map/pallas_call | solution.py:463
  4.2 4.6 %collective-permute-done.refs_1_ = bf16[128,1152]{1,0:T(8,128)(2,1)S(1)} collective-permute-done((bf16[128,1152]{1,0:T(8,128)(2,1)}, bf16[128,1152]{1,0:T(8,128)(2,1)S(1)}, u32[]{:S(2)}, u32[]{:S(2)}) %collective-permute-start) | collective-permute-done | bytes 294944 | tf_op jit(solution)/shard_map/ppermute | solution.py:429
  8.8 0.0 copy-start.4
  8.8 0.2 collective-permute-start.2
  9.0 0.8 %collective-permute-done.1.refs_2_ = bf16[128,1152]{1,0:T(8,128)(2,1)S(1)} collective-permute-done((bf16[128,1152]{1,0:T(8,128)(2,1)}, bf16[128,1152]{1,0:T(8,128)(2,1)S(1)}, u32[]{:S(2)}, u32[]{:S(2)}) %collective-permute-start.1) | collective-permute-done | bytes 294944 | tf_op jit(solution)/shard_map/ppermute | solution.py:429
  9.8 0.0 copy-start.2
  9.8 1.5 %collective-permute-start.3 = (bf16[128,1152]{1,0:T(8,128)(2,1)S(1)}, bf16[128,1152]{1,0:T(8,128)(2,1)S(1)}, u32[]{:S(2)}, u32[]{:S(2)}) collective-permute-start(bf16[128,1152]{1,0:T(8,128)(2,1)S(1)} %collective-permute-done.1.refs_2_), channel_id=1, source_target_pairs={{0,2},{1,3},{2,0},{3,1},{4,6},{5,7},{6,4},{7,5},{8,10},{9,11},{10,... | collective-permute-start | bytes 884744 | tf_op jit(solution)/shard_map/ppermute | solution.py:429
  11.3 4.2 %all-to-all-start = ((bf16[8,432,128]{2,1,0:T(8,128)(2,1)}), bf16[8,432,128]{2,1,0:T(8,128)(2,1)S(1)}, u32[]{:S(2)}, u32[]{:S(2)}) async-start(bf16[8,432,128]{2,1,0:T(8,128)(2,1)} %shard_map.93), calls=%async_computation | async-start | bytes 1769472 | tf_op jit(solution)/shard_map/all_to_all | solution.py:469
  15.5 0.2 collective-permute-done.2.refs_3_
  15.7 0.0 copy-start
  15.8 1.4 %collective-permute-start.4 = (bf16[32,1152]{1,0:T(8,128)(2,1)S(1)}, bf16[32,1152]{1,0:T(8,128)(2,1)S(1)}, u32[]{:S(2)}, u32[]{:S(2)}) collective-permute-start(bf16[32,1152]{1,0:T(8,128)(2,1)S(1)} %get-tuple-element.57), channel_id=1, source_target_pairs={{0,2},{1,3},{2,0},{3,1},{4,6},{5,7},{6,4},{7,5},{8,10},{9,11},{10,... | collective-permute-start | bytes 221192 | tf_op jit(solution)/shard_map/ppermute | solution.py:429
  17.1 0.2 collective-permute-start.5
  17.3 1.3 %collective-permute-start.6 = (bf16[32,1152]{1,0:T(8,128)(2,1)S(1)}, bf16[32,1152]{1,0:T(8,128)(2,1)S(1)}, u32[]{:S(2)}, u32[]{:S(2)}) collective-permute-start(bf16[32,1152]{1,0:T(8,128)(2,1)S(1)} %get-tuple-element.55), channel_id=1, source_target_pairs={{0,2},{1,3},{2,0},{3,1},{4,6},{5,7},{6,4},{7,5},{8,10},{9,11},{10,... | collective-permute-start | bytes 221192 | tf_op jit(solution)/shard_map/ppermute | solution.py:429
  18.6 0.2 collective-permute-start.7
  18.8 0.0 collective-permute-done.3.refs_4_
  18.8 0.0 copy-start.3
  18.8 1.3 %collective-permute-start.8 = (bf16[128,1152]{1,0:T(8,128)(2,1)S(1)}, bf16[128,1152]{1,0:T(8,128)(2,1)S(1)}, u32[]{:S(2)}, u32[]{:S(2)}) collective-permute-start(bf16[128,1152]{1,0:T(8,128)(2,1)S(1)} %broadcast_select_fusion.1), channel_id=1, source_target_pairs={{0,1},{1,0},{2,3},{3,2},{4,5},{5,4},{6,7},{7,6},{8,9},{9,8},{10,11... | collective-permute-start | bytes 884744 | tf_op jit(solution)/shard_map/ppermute | solution.py:429
  20.1 12.5 %collective-permute-done.4 = bf16[32,1152]{1,0:T(8,128)(2,1)S(1)} collective-permute-done((bf16[32,1152]{1,0:T(8,128)(2,1)S(1)}, bf16[32,1152]{1,0:T(8,128)(2,1)S(1)}, u32[]{:S(2)}, u32[]{:S(2)}) %collective-permute-start.4) | collective-permute-done | bytes 73760 | tf_op jit(solution)/shard_map/ppermute | solution.py:429
  32.5 1.6 %collective-permute-done.5 = bf16[32,1152]{1,0:T(8,128)(2,1)S(1)} collective-permute-done((bf16[32,1152]{1,0:T(8,128)(2,1)S(1)}, bf16[32,1152]{1,0:T(8,128)(2,1)S(1)}, u32[]{:S(2)}, u32[]{:S(2)}) %collective-permute-start.5) | collective-permute-done | bytes 73760 | tf_op jit(solution)/shard_map/ppermute | solution.py:429
  34.1 1.6 %collective-permute-done.6 = bf16[32,1152]{1,0:T(8,128)(2,1)S(1)} collective-permute-done((bf16[32,1152]{1,0:T(8,128)(2,1)S(1)}, bf16[32,1152]{1,0:T(8,128)(2,1)S(1)}, u32[]{:S(2)}, u32[]{:S(2)}) %collective-permute-start.6) | collective-permute-done | bytes 73760 | tf_op jit(solution)/shard_map/ppermute | solution.py:429
  35.7 1.6 %collective-permute-done.7 = bf16[32,1152]{1,0:T(8,128)(2,1)S(1)} collective-permute-done((bf16[32,1152]{1,0:T(8,128)(2,1)S(1)}, bf16[32,1152]{1,0:T(8,128)(2,1)S(1)}, u32[]{:S(2)}, u32[]{:S(2)}) %collective-permute-start.7) | collective-permute-done | bytes 73760 | tf_op jit(solution)/shard_map/ppermute | solution.py:429
  37.3 0.0 copy-start.1
  37.4 1.1 %collective-permute-start.9 = (bf16[128,1152]{1,0:T(8,128)(2,1)S(1)}, bf16[128,1152]{1,0:T(8,128)(2,1)S(1)}, u32[]{:S(2)}, u32[]{:S(2)}) collective-permute-start(bf16[128,1152]{1,0:T(8,128)(2,1)S(1)} %broadcast_select_fusion), channel_id=1, source_target_pairs={{0,1},{1,0},{2,3},{3,2},{4,5},{5,4},{6,7},{7,6},{8,9},{9,8},{10,11... | collective-permute-start | bytes 884744 | tf_op jit(solution)/shard_map/ppermute | solution.py:429
  38.5 0.0 all-to-all-done.in_ref
  38.5 0.0 copy-done.4
  38.5 0.0 copy-done.2
  38.5 0.0 copy-done
  38.5 0.0 copy-done.3
  38.5 0.0 copy-done.1
  38.5 6.7 %shard_map.94 = (bf16[2,1024,80]{2,1,0:T(8,128)(2,1)S(1)}, bf16[2,80,1024]{2,1,0:T(8,128)(2,1)S(1)}, bf16[2,1024,80]{2,1,0:T(8,128)(2,1)S(1)}, bf16[144,1024]{1,...) custom-call(s32[1,4]{1,0:T(1,128)} %len_ref.3, ...), custom_call_target="tpu_custom_call" | custom-call | tf_op jit(solution)/shard_map/pallas_call | solution.py:482
  45.3 0.0 collective-permute-done.8.refs_0_
  45.3 0.0 collective-permute-done.9.refs_1_
  45.3 0.3 shard_map.96
  45.6 3.0 %collective-permute-start.16 = (bf16[144,1152]{1,0:T(8,128)(2,1)S(1)}, bf16[144,1152]{1,0:T(8,128)(2,1)S(1)}, u32[]{:S(2)}, u32[]{:S(2)}) collective-permute-start(bf16[144,1152]{1,0:T(8,128)(2,1)S(1)} %shard_map.96), channel_id=1, source_target_pairs={{0,8},{8,0},{16,24},{24,16},{1,9},{9,1},{17,25},{25,17},{2,10},{10... | collective-permute-start | bytes 995336 | tf_op jit(solution)/shard_map/ppermute | solution.py:504
  48.7 5.7 %shard_map.95 = (bf16[432,128]{1,0:T(8,128)(2,1)S(1)}, bf16[432,128]{1,0:T(8,128)(2,1)}, bf16[432,128]{1,0:T(8,128)(2,1)}, bf16[432,128]{1,0:T(8,128)(2,1)}, bf1...) custom-call(s32[1,4]{1,0:T(1,128)} %len_ref.3, ...), custom_call_target="tpu_custom_call" | custom-call | tf_op jit(solution)/shard_map/pallas_call | solution.py:493
  54.4 0.0 collective-permute-done.16
  54.4 0.1 reduce-precision_convert_fusion
  54.5 0.5 collective-permute-start.17
  55.0 0.2 collective-permute-start.10
  55.2 2.4 %collective-permute-start.11 = (bf16[432,128]{1,0:T(8,128)(2,1)}, bf16[432,128]{1,0:T(8,128)(2,1)S(1)}, u32[]{:S(2)}, u32[]{:S(2)}) collective-permute-start(bf16[432,128]{1,0:T(8,128)(2,1)} %get-tuple-element.41), channel_id=1, source_target_pairs={{0,3},{1,2},{2,1},{3,0},{4,7},{5,6},{6,5},{7,4},{8,11},{9,10},{10,... | collective-permute-start | bytes 331784 | tf_op jit(solution)/shard_map/ppermute | solution.py:512
  57.6 1.3 %collective-permute-start.12 = (bf16[432,128]{1,0:T(8,128)(2,1)}, bf16[432,128]{1,0:T(8,128)(2,1)S(1)}, u32[]{:S(2)}, u32[]{:S(2)}) collective-permute-start(bf16[432,128]{1,0:T(8,128)(2,1)} %get-tuple-element.42), channel_id=1, source_target_pairs={{0,4},{1,5},{2,6},{3,7},{4,0},{5,1},{6,2},{7,3},{8,12},{9,13},{10,... | collective-permute-start | bytes 331784 | tf_op jit(solution)/shard_map/ppermute | solution.py:512
  58.9 0.9 %collective-permute-start.13 = (bf16[432,128]{1,0:T(8,128)(2,1)}, bf16[432,128]{1,0:T(8,128)(2,1)S(1)}, u32[]{:S(2)}, u32[]{:S(2)}) collective-permute-start(bf16[432,128]{1,0:T(8,128)(2,1)} %get-tuple-element.43), channel_id=1, source_target_pairs={{0,2},{1,3},{2,0},{3,1},{4,6},{5,7},{6,4},{7,5},{8,10},{9,11},{10,... | collective-permute-start | bytes 331784 | tf_op jit(solution)/shard_map/ppermute | solution.py:512
  59.8 4.2 %collective-permute-done.17 = bf16[144,1152]{1,0:T(8,128)(2,1)S(1)} collective-permute-done((bf16[144,1152]{1,0:T(8,128)(2,1)S(1)}, bf16[144,1152]{1,0:T(8,128)(2,1)S(1)}, u32[]{:S(2)}, u32[]{:S(2)}) %collective-permute-start.17) | collective-permute-done | bytes 331808 | tf_op jit(solution)/shard_map/ppermute | solution.py:504
  64.0 0.5 collective-permute-start.14
  64.5 0.9 %add_multiply_fusion = f32[144,1152]{1,0:T(8,128)} fusion(bf16[144,1152]{1,0:T(8,128)(2,1)S(1)} %collective-permute-done.17, bf16[144,1152]{1,0:T(8,128)(2,1)S(1)} %reduce-precision_convert_fusion), kind=kLoop, calls=%fused_computation | loop fusion | flops 663552 | bytes 1327104 | tf_op jit(solution)/shard_map/mul | solution.py:507
  65.4 0.0 collective-permute-done.10.refs_1_
  65.4 1.0 %collective-permute-start.15 = (bf16[432,128]{1,0:T(8,128)(2,1)}, bf16[432,128]{1,0:T(8,128)(2,1)S(1)}, u32[]{:S(2)}, u32[]{:S(2)}) collective-permute-start(bf16[432,128]{1,0:T(8,128)(2,1)} %get-tuple-element.45), channel_id=1, source_target_pairs={{0,6},{1,7},{2,4},{3,5},{4,2},{5,3},{6,0},{7,1},{8,14},{9,15},{10,... | collective-permute-start | bytes 331784 | tf_op jit(solution)/shard_map/ppermute | solution.py:512
  66.5 0.0 collective-permute-done.11.refs_2_
  66.5 1.1 %collective-permute-start.18 = (bf16[432,128]{1,0:T(8,128)(2,1)}, bf16[432,128]{1,0:T(8,128)(2,1)S(1)}, u32[]{:S(2)}, u32[]{:S(2)}) collective-permute-start(bf16[432,128]{1,0:T(8,128)(2,1)} %get-tuple-element.50), channel_id=1, source_target_pairs={{0,1},{1,0},{2,3},{3,2},{4,5},{5,4},{6,7},{7,6},{8,9},{9,8},{10,11... | collective-permute-start | bytes 331784 | tf_op jit(solution)/shard_map/ppermute | solution.py:512
  67.6 0.0 collective-permute-done.12.refs_3_
  67.6 0.0 collective-permute-done.13.refs_4_
  67.6 7.6 %collective-permute-done.14.refs_5_ = bf16[432,128]{1,0:T(8,128)(2,1)S(1)} collective-permute-done((bf16[432,128]{1,0:T(8,128)(2,1)}, bf16[432,128]{1,0:T(8,128)(2,1)S(1)}, u32[]{:S(2)}, u32[]{:S(2)}) %collective-permute-start.14) | collective-permute-done | bytes 110624 | tf_op jit(solution)/shard_map/ppermute | solution.py:512
  75.2 2.7 %collective-permute-done.15.refs_6_ = bf16[432,128]{1,0:T(8,128)(2,1)S(1)} collective-permute-done((bf16[432,128]{1,0:T(8,128)(2,1)}, bf16[432,128]{1,0:T(8,128)(2,1)S(1)}, u32[]{:S(2)}, u32[]{:S(2)}) %collective-permute-start.15) | collective-permute-done | bytes 110624 | tf_op jit(solution)/shard_map/ppermute | solution.py:512
  77.9 0.0 collective-permute-done.18.refs_7_
  77.9 1.5 %shard_map.97 = (f32[128,1152]{1,0:T(8,128)}, f32[128,1152]{1,0:T(8,128)}, f32[128,1152]{1,0:T(8,128)}) custom-call(bf16[432,128]{1,0:T(8,128)(2,1)S(1)} %get-tuple-element.39.refs_0_, bf16[432,128]{1,0:T(8,128)(2,1)S(1)} %collective-permute-done.10.refs_1_, bf16[432,128]{1,0:T(8,128)(2,1)S(1)} %collective-permute-done.11.refs_2_, ...), custom_call_target="tpu_custom_call" | custom-call | tf_op jit(solution)/shard_map/pallas_call | solution.py:514
  (7 shorter events, 0.1 us)
Async XLA Ops:
  0.6 8.2 %collective-permute-start = (bf16[128,1152]{1,0:T(8,128)(2,1)}, bf16[128,1152]{1,0:T(8,128)(2,1)S(1)}, u32[]{:S(2)}, u32[]{:S(2)}) collective-permute-start(bf16[128,1152]{1,0:T(8,128)(2,1)} %bitcast.7), channel_id=1, source_target_pairs={{0,2},{1,3},{2,0},{3,1},{4,6},{5,7},{6,4},{7,5},{8,10},{9,11},{10,... | collective-permute-start | bytes 884744 | tf_op jit(solution)/shard_map/ppermute | solution.py:429
  2.0 7.8 %collective-permute-start.1 = (bf16[128,1152]{1,0:T(8,128)(2,1)}, bf16[128,1152]{1,0:T(8,128)(2,1)S(1)}, u32[]{:S(2)}, u32[]{:S(2)}) collective-permute-start(bf16[128,1152]{1,0:T(8,128)(2,1)} %bitcast.8), channel_id=1, source_target_pairs={{0,1},{1,0},{2,4},{3,5},{4,2},{5,3},{6,7},{7,6},{8,9},{9,8},{10,12... | collective-permute-start | bytes 884744 | tf_op jit(solution)/shard_map/ppermute | solution.py:429
  8.8 29.7 %copy-start.4 = (bf16[128,1152]{1,0:T(8,128)(2,1)}, bf16[128,1152]{1,0:T(8,128)(2,1)S(1)}, u32[]{:S(2)}) copy-start(bf16[128,1152]{1,0:T(8,128)(2,1)S(1)} %collective-permute-done.refs_1_) | copy-start | bytes 884740
  8.8 7.0 %collective-permute-start.2 = (bf16[128,1152]{1,0:T(8,128)(2,1)S(1)}, bf16[128,1152]{1,0:T(8,128)(2,1)S(1)}, u32[]{:S(2)}, u32[]{:S(2)}) collective-permute-start(bf16[128,1152]{1,0:T(8,128)(2,1)S(1)} %collective-permute-done.refs_1_), channel_id=1, source_target_pairs={{0,1},{1,0},{2,4},{3,5},{4,2},{5,3},{6,7},{7,6},{8,9},{9,8},{10,12... | collective-permute-start | bytes 884744 | tf_op jit(solution)/shard_map/ppermute | solution.py:429
  9.8 28.7 %copy-start.2 = (bf16[128,1152]{1,0:T(8,128)(2,1)}, bf16[128,1152]{1,0:T(8,128)(2,1)S(1)}, u32[]{:S(2)}) copy-start(bf16[128,1152]{1,0:T(8,128)(2,1)S(1)} %collective-permute-done.1.refs_2_) | copy-start | bytes 884740
  9.8 9.0 %collective-permute-start.3 = (bf16[128,1152]{1,0:T(8,128)(2,1)S(1)}, bf16[128,1152]{1,0:T(8,128)(2,1)S(1)}, u32[]{:S(2)}, u32[]{:S(2)}) collective-permute-start(bf16[128,1152]{1,0:T(8,128)(2,1)S(1)} %collective-permute-done.1.refs_2_), channel_id=1, source_target_pairs={{0,2},{1,3},{2,0},{3,1},{4,6},{5,7},{6,4},{7,5},{8,10},{9,11},{10,... | collective-permute-start | bytes 884744 | tf_op jit(solution)/shard_map/ppermute | solution.py:429
  11.3 27.2 %all-to-all-start = ((bf16[8,432,128]{2,1,0:T(8,128)(2,1)}), bf16[8,432,128]{2,1,0:T(8,128)(2,1)S(1)}, u32[]{:S(2)}, u32[]{:S(2)}) async-start(bf16[8,432,128]{2,1,0:T(8,128)(2,1)} %shard_map.93), calls=%async_computation | async-start | bytes 1769472 | tf_op jit(solution)/shard_map/all_to_all | solution.py:469
  15.7 22.8 %copy-start = (bf16[128,1152]{1,0:T(8,128)(2,1)}, bf16[128,1152]{1,0:T(8,128)(2,1)S(1)}, u32[]{:S(2)}) copy-start(bf16[128,1152]{1,0:T(8,128)(2,1)S(1)} %collective-permute-done.2.refs_3_) | copy-start | bytes 884740
  15.8 16.8 %collective-permute-start.4 = (bf16[32,1152]{1,0:T(8,128)(2,1)S(1)}, bf16[32,1152]{1,0:T(8,128)(2,1)S(1)}, u32[]{:S(2)}, u32[]{:S(2)}) collective-permute-start(bf16[32,1152]{1,0:T(8,128)(2,1)S(1)} %get-tuple-element.57), channel_id=1, source_target_pairs={{0,2},{1,3},{2,0},{3,1},{4,6},{5,7},{6,4},{7,5},{8,10},{9,11},{10,... | collective-permute-start | bytes 221192 | tf_op jit(solution)/shard_map/ppermute | solution.py:429
  17.1 17.0 %collective-permute-start.5 = (bf16[32,1152]{1,0:T(8,128)(2,1)S(1)}, bf16[32,1152]{1,0:T(8,128)(2,1)S(1)}, u32[]{:S(2)}, u32[]{:S(2)}) collective-permute-start(bf16[32,1152]{1,0:T(8,128)(2,1)S(1)} %get-tuple-element.56), channel_id=1, source_target_pairs={{0,2},{1,3},{2,0},{3,1},{4,6},{5,7},{6,4},{7,5},{8,10},{9,11},{10,... | collective-permute-start | bytes 221192 | tf_op jit(solution)/shard_map/ppermute | solution.py:429
  17.3 18.4 %collective-permute-start.6 = (bf16[32,1152]{1,0:T(8,128)(2,1)S(1)}, bf16[32,1152]{1,0:T(8,128)(2,1)S(1)}, u32[]{:S(2)}, u32[]{:S(2)}) collective-permute-start(bf16[32,1152]{1,0:T(8,128)(2,1)S(1)} %get-tuple-element.55), channel_id=1, source_target_pairs={{0,2},{1,3},{2,0},{3,1},{4,6},{5,7},{6,4},{7,5},{8,10},{9,11},{10,... | collective-permute-start | bytes 221192 | tf_op jit(solution)/shard_map/ppermute | solution.py:429
  18.6 18.7 %collective-permute-start.7 = (bf16[32,1152]{1,0:T(8,128)(2,1)S(1)}, bf16[32,1152]{1,0:T(8,128)(2,1)S(1)}, u32[]{:S(2)}, u32[]{:S(2)}) collective-permute-start(bf16[32,1152]{1,0:T(8,128)(2,1)S(1)} %get-tuple-element.54), channel_id=1, source_target_pairs={{0,2},{1,3},{2,0},{3,1},{4,6},{5,7},{6,4},{7,5},{8,10},{9,11},{10,... | collective-permute-start | bytes 221192 | tf_op jit(solution)/shard_map/ppermute | solution.py:429
  18.8 19.7 %copy-start.3 = (bf16[128,1152]{1,0:T(8,128)(2,1)}, bf16[128,1152]{1,0:T(8,128)(2,1)S(1)}, u32[]{:S(2)}) copy-start(bf16[128,1152]{1,0:T(8,128)(2,1)S(1)} %collective-permute-done.3.refs_4_) | copy-start | bytes 884740
  18.8 26.5 %collective-permute-start.8 = (bf16[128,1152]{1,0:T(8,128)(2,1)S(1)}, bf16[128,1152]{1,0:T(8,128)(2,1)S(1)}, u32[]{:S(2)}, u32[]{:S(2)}) collective-permute-start(bf16[128,1152]{1,0:T(8,128)(2,1)S(1)} %broadcast_select_fusion.1), channel_id=1, source_target_pairs={{0,1},{1,0},{2,3},{3,2},{4,5},{5,4},{6,7},{7,6},{8,9},{9,8},{10,11... | collective-permute-start | bytes 884744 | tf_op jit(solution)/shard_map/ppermute | solution.py:429
  37.3 1.2 %copy-start.1 = (bf16[128,1152]{1,0:T(8,128)(2,1)}, bf16[128,1152]{1,0:T(8,128)(2,1)S(1)}, u32[]{:S(2)}) copy-start(bf16[128,1152]{1,0:T(8,128)(2,1)S(1)} %constant_dynamic-update-slice_fusion.refs_5_) | copy-start | bytes 884740
  37.4 7.9 %collective-permute-start.9 = (bf16[128,1152]{1,0:T(8,128)(2,1)S(1)}, bf16[128,1152]{1,0:T(8,128)(2,1)S(1)}, u32[]{:S(2)}, u32[]{:S(2)}) collective-permute-start(bf16[128,1152]{1,0:T(8,128)(2,1)S(1)} %broadcast_select_fusion), channel_id=1, source_target_pairs={{0,1},{1,0},{2,3},{3,2},{4,5},{5,4},{6,7},{7,6},{8,9},{9,8},{10,11... | collective-permute-start | bytes 884744 | tf_op jit(solution)/shard_map/ppermute | solution.py:429
  45.6 8.8 %collective-permute-start.16 = (bf16[144,1152]{1,0:T(8,128)(2,1)S(1)}, bf16[144,1152]{1,0:T(8,128)(2,1)S(1)}, u32[]{:S(2)}, u32[]{:S(2)}) collective-permute-start(bf16[144,1152]{1,0:T(8,128)(2,1)S(1)} %shard_map.96), channel_id=1, source_target_pairs={{0,8},{8,0},{16,24},{24,16},{1,9},{9,1},{17,25},{25,17},{2,10},{10... | collective-permute-start | bytes 995336 | tf_op jit(solution)/shard_map/ppermute | solution.py:504
  54.5 9.5 %collective-permute-start.17 = (bf16[144,1152]{1,0:T(8,128)(2,1)S(1)}, bf16[144,1152]{1,0:T(8,128)(2,1)S(1)}, u32[]{:S(2)}, u32[]{:S(2)}) collective-permute-start(bf16[144,1152]{1,0:T(8,128)(2,1)S(1)} %reduce-precision_convert_fusion), channel_id=1, source_target_pairs={{0,16},{8,24},{16,0},{24,8},{1,17},{9,25},{17,1},{25,9},{2,18},{10... | collective-permute-start | bytes 995336 | tf_op jit(solution)/shard_map/ppermute | solution.py:504
  55.0 10.4 %collective-permute-start.10 = (bf16[432,128]{1,0:T(8,128)(2,1)}, bf16[432,128]{1,0:T(8,128)(2,1)S(1)}, u32[]{:S(2)}, u32[]{:S(2)}) collective-permute-start(bf16[432,128]{1,0:T(8,128)(2,1)} %get-tuple-element.40), channel_id=1, source_target_pairs={{0,5},{1,4},{2,7},{3,6},{4,1},{5,0},{6,3},{7,2},{8,13},{9,12},{10,... | collective-permute-start | bytes 331784 | tf_op jit(solution)/shard_map/ppermute | solution.py:512
  55.2 11.2 %collective-permute-start.11 = (bf16[432,128]{1,0:T(8,128)(2,1)}, bf16[432,128]{1,0:T(8,128)(2,1)S(1)}, u32[]{:S(2)}, u32[]{:S(2)}) collective-permute-start(bf16[432,128]{1,0:T(8,128)(2,1)} %get-tuple-element.41), channel_id=1, source_target_pairs={{0,3},{1,2},{2,1},{3,0},{4,7},{5,6},{6,5},{7,4},{8,11},{9,10},{10,... | collective-permute-start | bytes 331784 | tf_op jit(solution)/shard_map/ppermute | solution.py:512
  57.6 10.0 %collective-permute-start.12 = (bf16[432,128]{1,0:T(8,128)(2,1)}, bf16[432,128]{1,0:T(8,128)(2,1)S(1)}, u32[]{:S(2)}, u32[]{:S(2)}) collective-permute-start(bf16[432,128]{1,0:T(8,128)(2,1)} %get-tuple-element.42), channel_id=1, source_target_pairs={{0,4},{1,5},{2,6},{3,7},{4,0},{5,1},{6,2},{7,3},{8,12},{9,13},{10,... | collective-permute-start | bytes 331784 | tf_op jit(solution)/shard_map/ppermute | solution.py:512
  58.9 8.7 %collective-permute-start.13 = (bf16[432,128]{1,0:T(8,128)(2,1)}, bf16[432,128]{1,0:T(8,128)(2,1)S(1)}, u32[]{:S(2)}, u32[]{:S(2)}) collective-permute-start(bf16[432,128]{1,0:T(8,128)(2,1)} %get-tuple-element.43), channel_id=1, source_target_pairs={{0,2},{1,3},{2,0},{3,1},{4,6},{5,7},{6,4},{7,5},{8,10},{9,11},{10,... | collective-permute-start | bytes 331784 | tf_op jit(solution)/shard_map/ppermute | solution.py:512
  64.0 11.2 %collective-permute-start.14 = (bf16[432,128]{1,0:T(8,128)(2,1)}, bf16[432,128]{1,0:T(8,128)(2,1)S(1)}, u32[]{:S(2)}, u32[]{:S(2)}) collective-permute-start(bf16[432,128]{1,0:T(8,128)(2,1)} %get-tuple-element.44), channel_id=1, source_target_pairs={{0,7},{1,6},{2,5},{3,4},{4,3},{5,2},{6,1},{7,0},{8,15},{9,14},{10,... | collective-permute-start | bytes 331784 | tf_op jit(solution)/shard_map/ppermute | solution.py:512
  65.4 12.5 %collective-permute-start.15 = (bf16[432,128]{1,0:T(8,128)(2,1)}, bf16[432,128]{1,0:T(8,128)(2,1)S(1)}, u32[]{:S(2)}, u32[]{:S(2)}) collective-permute-start(bf16[432,128]{1,0:T(8,128)(2,1)} %get-tuple-element.45), channel_id=1, source_target_pairs={{0,6},{1,7},{2,4},{3,5},{4,2},{5,3},{6,0},{7,1},{8,14},{9,15},{10,... | collective-permute-start | bytes 331784 | tf_op jit(solution)/shard_map/ppermute | solution.py:512
  66.5 11.4 %collective-permute-start.18 = (bf16[432,128]{1,0:T(8,128)(2,1)}, bf16[432,128]{1,0:T(8,128)(2,1)S(1)}, u32[]{:S(2)}, u32[]{:S(2)}) collective-permute-start(bf16[432,128]{1,0:T(8,128)(2,1)} %get-tuple-element.50), channel_id=1, source_target_pairs={{0,1},{1,0},{2,3},{3,2},{4,5},{5,4},{6,7},{7,6},{8,9},{9,8},{10,11... | collective-permute-start | bytes 331784 | tf_op jit(solution)/shard_map/ppermute | solution.py:512

commit v4 on v2

--- a/solution.py
+++ b/solution.py
@@ -271,9 +271,20 @@
     return jnp.concatenate([ref[head, 0:HEAD_DIM, :] for head in range(ref.shape[0])], axis=0).astype(BF16)
 
 
-def forward_kernel(early, len_ref, w_ref, in_ref, *refs):
-    pieces = refs[:early]
-    (q_s, k_s, vt_s, att_s, probs_s, d_s, wg_s, w_s, len_s, v_s, kt_s, sum_s, dy_s, len_sem, w_sem, dy_sem) = refs[early:]
+def project_kernel(w_ref, *refs):
+    pieces, (dy_s, d_s, w_s, w_sem, dy_sem) = refs[:-5], refs[-5:]
+    load_w = load_w_rows(w_ref, w_s, w_sem)
+    loads = load_rows(pieces, dy_s, dy_sem)
+    load_w.wait()
+    for load in loads:
+        load.wait()
+    step = 2 * pieces[0].shape[0]
+    for start in range(0, dy_s.shape[0], step):
+        columns = slice(start, start + step)
+        store_heads(d_s, dot(w_s[...], dy_s[columns, :], NT), columns)
+
+
+def forward_kernel(len_ref, in_ref, dy_ref, q_s, k_s, vt_s, att_s, probs_s, wg_s, len_s, v_s, kt_s, sum_s, len_sem):
     shards, height, tok = in_ref.shape
     part = height // 3
     heads = q_s.shape[0]
@@ -281,8 +292,6 @@
 
     load_len = pltpu.make_async_copy(len_ref, len_s, len_sem)
     load_len.start()
-    load_w = load_w_rows(w_ref, w_s, w_sem)
-    loads = load_rows(pieces, dy_s, dy_sem)
     sum_s[...] = jnp.zeros_like(sum_s)
     for shard in range(shards):
         columns = slice(shard * tok, (shard + 1) * tok)
@@ -312,32 +321,19 @@
 
     each_image(len_s, tok, shards, work)
     att_s[...] = joined(sum_s)
-    for n in range(early, shards):
-        dy_s[piece_columns(n, tok), :] = jnp.zeros((tok, dy_s.shape[1]), BF16)
-    load_w.wait()
-    for load in loads:
-        load.wait()
-    for shard in range(0, shards, 2):
-        d_block = dot(w_s[...], dy_s[shard * tok:(shard + 2) * tok, :], NT)
-        store_heads(d_s, d_block, slice(shard * tok, (shard + 2) * tok))
-    wg_s[...] = dot(att_s[...], dy_s[...])
-
-
-def backward_kernel(early, len_ref, w_s, q_s, k_s, vt_s, att_s, probs_s, d_ref, *refs):
-    late = refs[:8 - early]
-    outs = refs[8 - early:16 - early]
-    (len_s, d_s, dq_s, dk_s, dv_s, out_s, len_sem, out_sem) = refs[16 - early:]
+    wg_s[...] = dot(att_s[...], dy_ref[...]).astype(BF16)
+
+
+def backward_kernel(len_ref, q_s, k_s, vt_s, att_s, probs_s, d_s, *refs):
+    outs, (len_s, dq_s, dk_s, dv_s, out_s, len_sem, out_sem) = refs[:-7], refs[-7:]
     shards, height, tok = out_s.shape
     part = height // 3
     heads = d_s.shape[0]
     scale = HEAD_DIM ** (-0.5)
     load_len = pltpu.make_async_copy(len_ref, len_s, len_sem)
     load_len.start()
-    d_s[...] = d_ref[...]
     for ref in (dq_s, dk_s, dv_s):
         ref[...] = jnp.zeros_like(ref)
-    for n, piece in enumerate(late):
-        store_heads(d_s, dot(w_s[...], piece[...], NT), piece_columns(early + n, tok))
     load_len.wait()
 
     def work(image, count, first, start, end):
@@ -357,12 +353,12 @@
 
     each_image(len_s, tok, shards, work)
 
-    stores = []
     for i, ref in enumerate((dq_s, dk_s, dv_s)):
         whole = joined(ref)
         for shard in range(shards):
             out_s[shard, i * part:(i + 1) * part, :] = whole[:, shard * tok:(shard + 1) * tok]
     me = lax.axis_index("seq")
+    stores = []
     for n in range(shards - 1, 0, -1):
         store = pltpu.make_async_copy(out_s.at[me ^ n], outs[n], out_sem.at[n])
         store.start()
@@ -372,14 +368,6 @@
         store.wait()
 
 
-def weight_kernel(early, att_ref, wg_ref, *refs):
-    late, out_ref = refs[:-1], refs[-1]
-    total = wg_ref[...]
-    for n, piece in enumerate(late):
-        total = total + dot(att_ref[:, piece_columns(early + n, piece.shape[0])], piece[...])
-    out_ref[...] = total.astype(BF16)
-
-
 def load_w_rows(w_ref, w_s, sem):
     part = w_s.shape[0]
     row = pl.multiple_of(lax.axis_index("seq") * part, part)
@@ -404,7 +392,7 @@
 
 
 BACK_ORDER = (0, 5, 3, 4, 7, 6, 2, 1)
-FIFTH_PARTS = 4
+PARTS = 2
 INNER_SOURCES = (0, 2, 6, 4, 3, 1, 7, 5)
 OUTER_SOURCES = (0, 2, 1, 3, 4, 6, 5, 7)
 
@@ -424,16 +412,16 @@
     def move(value, pairs):
         return lax.ppermute(value, "seq", pairs)
 
-    one = move(block, along)
-    two = move(block, middle)
-    one, two = after(one, event), after(two, event)
-    three = move(one, middle)
+    rows = block.shape[0] // PARTS
+    one = [move(block[n * rows:(n + 1) * rows], along) for n in range(PARTS)]
+    two = after(move(block, middle), event)
+    three = [move(after(part, event), middle) for part in one]
     four = move(two, along)
-    rows = block.shape[0] // FIFTH_PARTS
-    five = jnp.concatenate([move(three[n * rows:(n + 1) * rows], along) for n in range(FIFTH_PARTS)])
+    five = [move(part, along) for part in three]
     six = move(jnp.where(inner, two, four), across)
-    seven = move(jnp.where(inner, three, five), across)
-    return (block, one, two, three, four, five, six, seven)
+    seven = [move(jnp.where(inner, ready, came), across) for ready, came in zip(three, five)]
+    whole = [jnp.concatenate(parts) for parts in (one, three, five, seven)]
+    return (block, whole[0], two, whole[1], four, whole[2], six, whole[3]), three
 
 
 def after(value, *events):
@@ -461,8 +449,8 @@
         in_specs=[HBM] * 3, out_specs=HBM, compiler_params=PARAMS,
         scratch_shapes=[pltpu.VMEM((3, tok, width), BF16), pltpu.VMEM((3, shards, part, tok), BF16), DMA((3,)), DMA((3,))],
     )(*in_hbm(queries[0], keys[0], values[0]))
-    pieces = gather_steps(out_grad[0], sent)
-    arrived = lax.all_to_all(after(sent, *pieces[1:3]), "seq", 0, 0, tiled=True)
+    pieces, crossed = gather_steps(out_grad[0], sent)
+    arrived = lax.all_to_all(after(sent, *crossed, pieces[4]), "seq", 0, 0, tiled=True)
 
     images = lengths.shape[1]
     window = window_sizes(tok, shards)[1] * tok
@@ -473,26 +461,24 @@
         return [pltpu.VMEM(d, kind) for d in dims]
 
     len_s = pltpu.SMEM((1, images), jnp.int32)
-    early = 6
-    late = len(pieces) - early
-    q_t, k_t, v_r, attended, probs, d_part, w_early, w_rows = pl.pallas_call(
-        functools.partial(forward_kernel, early),
-        out_shape=[shape(wide), shape(wide), shape(tall), shape(flat), shape(chance), shape(wide), shape((part, width), F32), shape((part, width))],
-        in_specs=[HBM, HBM, VMEM] + [HBM] * early, out_specs=[VMEM] * 8, compiler_params=PARAMS,
-        scratch_shapes=[len_s] + scratch(wide, tall) + scratch(wide, kind=F32) + scratch((tokens, width))
-        + [DMA, DMA, DMA((early,))],
-    )(*in_hbm(lengths, out_weight), arrived, *in_hbm(*pieces[:early]))
-    w_part = pl.pallas_call(
-        functools.partial(weight_kernel, early), out_shape=shape((part, width)),
-        in_specs=[VMEM] * (2 + late), out_specs=VMEM, compiler_params=PARAMS,
-    )(attended, w_early, *pieces[early:])
+    dy_all, d_heads = pl.pallas_call(
+        project_kernel, out_shape=[shape((tokens, width)), shape(wide)],
+        in_specs=[HBM] * (1 + len(pieces)), out_specs=[VMEM] * 2, compiler_params=PARAMS,
+        scratch_shapes=scratch((part, width)) + [DMA, DMA((len(pieces),))],
+    )(*in_hbm(out_weight, *pieces))
+    *kept, w_part = pl.pallas_call(
+        forward_kernel,
+        out_shape=[shape(wide), shape(wide), shape(tall), shape(flat), shape(chance), shape((part, width))],
+        in_specs=[HBM, VMEM, VMEM], out_specs=[VMEM] * 6, compiler_params=PARAMS,
+        scratch_shapes=[len_s] + scratch(wide, tall) + scratch(wide, kind=F32) + [DMA],
+    )(*in_hbm(lengths), arrived, dy_all)
     grads = pl.pallas_call(
-        functools.partial(backward_kernel, early),
+        backward_kernel,
         out_shape=[shape((3 * part, tok))] + [pltpu.HBM((3 * part, tok), BF16)] * (shards - 1),
-        in_specs=[HBM] + [VMEM] * (7 + late), out_specs=[VMEM] + [HBM] * (shards - 1), compiler_params=PARAMS,
-        scratch_shapes=[len_s] + scratch(wide) + scratch(wide, wide, wide, kind=F32)
+        in_specs=[HBM] + [VMEM] * 6, out_specs=[VMEM] + [HBM] * (shards - 1), compiler_params=PARAMS,
+        scratch_shapes=[len_s] + scratch(wide, wide, wide, kind=F32)
         + scratch((shards, 3 * part, tok)) + [DMA, DMA((shards,))],
-    )(*in_hbm(lengths), w_rows, q_t, k_t, v_r, attended, probs, d_part, *pieces[early:])
+    )(*in_hbm(lengths), *kept, d_heads)
     sums = w_part.astype(F32)
     step = 1
     while step < groups:

time: 79.4 us -> 89 us (1.12)
  other arithmetic: 1.11 us -> 4.06 us
  starting transfers between devices: 22.4 us -> 24.9 us
  local copies, waits for them, and re-layouts: 0.09 us -> 2.44 us
  Pallas kernels: 16 us -> 17.3 us
    concatenate x0 -> x4, other arithmetic: none -> 2.95 us  [gather_steps(): whole = [jnp.concatenate(parts) for parts in (one, three, five, seven)]]
    ppermute x10 -> x11, starting transfers between devices: 8.48 us -> 10.1 us  [move(): return lax.ppermute(value, 'seq', pairs)]
    unnamed x13 -> x10, local copies, waits for them, and re-layouts: 0.05 us -> 1.43 us
    pallas_call x3, Pallas kernels: 12.4 us -> 13.7 us  [the longest x1 5.54 us: head_body(): pl.pallas_call(forward_kernel, out_shape=[shape(wide), shape(wide), shape...]
    ppermute x2, starting transfers between devices: 3.62 us -> 4.74 us  [head_body(): lax.ppermute(w_part, 'dp', pairs)]
    slice x1, local copies, waits for them, and re-layouts: 0.02 us -> 1.01 us  [gather_steps(): one = [move(block[n * rows:(n + 1) * rows], along) for n in range(PARTS)]]
    ppermute x10 -> x11, waiting for transfers between devices: 22.8 us -> 23.2 us  [move(): return lax.ppermute(value, 'seq', pairs)]
  transfers between devices with their start and end apart: 20 -> 21, of which waited for: 10 -> 11; matrix products, arithmetic and copies ran while one was open for 1% -> 6% of each run, Pallas kernels for 18% -> 12%
where the time goes in v4:
time: 89 us; the launch traced here: 88.3 us
  waiting for transfers between devices  38.8 us (44%)
  starting transfers between devices  24.9 us (28%)
  Pallas kernels  17.3 us (19%)
  other arithmetic  4.06 us (5%)
  local copies, waits for them, and re-layouts  2.44 us (3%)
    ppermute x11, waiting for transfers between devices, move(): return lax.ppermute(value, 'seq', pairs)  23.2 us
    ppermute x7, waiting for transfers between devices, head_body(): lax.ppermute(block, 'seq', [(i, i ^ n) for i in range(shards)])  11.1 us
    ppermute x11, starting transfers between devices, move(): return lax.ppermute(value, 'seq', pairs)  10.1 us
    ppermute x7, starting transfers between devices, head_body(): lax.ppermute(block, 'seq', [(i, i ^ n) for i in range(shards)])  6 us
    pallas_call x1, Pallas kernels, head_body(): pl.pallas_call(forward_kernel, out_shape=[shape(wide), shape(wide), shape...  5.54 us
    pallas_call x1, Pallas kernels, head_body(): pl.pallas_call(backward_kernel, out_shape=[shape((3 * part, tok))] + [plt...  5.5 us
    ppermute x2, starting transfers between devices, head_body(): lax.ppermute(w_part, 'dp', pairs)  4.74 us
    ppermute x2, waiting for transfers between devices, head_body(): lax.ppermute(w_part, 'dp', pairs)  4.44 us
  transfers between devices with their start and end apart: 21, of which 11 were waited for; matrix products, arithmetic and copies ran while one was open for 6% of the time, Pallas kernels for 12%

profile of v4, /device:TPU:17, one launch (start us, length us, event | category | flops | bytes accessed | tf_op | source)
XLA Modules:
  0.0 88.3 jit_solution(6669868193648583201)
XLA Ops:
  0.6 0.2 collective-permute-start.4
  0.9 1.0 %slice_bitcast_fusion = (bf16[64,1152]{1,0:T(8,128)(2,1)S(1)}, bf16[64,1152]{1,0:T(8,128)(2,1)S(1)}) fusion(bf16[1,128,1152]{2,1,0:T(8,128)(2,1)} %param.10), kind=kLoop, calls=%fused_computation.7 | loop fusion | bytes 589824 | tf_op jit(solution)/shard_map/slice | solution.py:416
  1.9 2.4 %collective-permute-start.2 = (bf16[64,1152]{1,0:T(8,128)(2,1)S(1)}, bf16[64,1152]{1,0:T(8,128)(2,1)S(1)}, u32[]{:S(2)}, u32[]{:S(2)}) collective-permute-start(bf16[64,1152]{1,0:T(8,128)(2,1)S(1)} %get-tuple-element.56), channel_id=1, source_target_pairs={{0,2},{1,3},{2,0},{3,1},{4,6},{5,7},{6,4},{7,5},{8,10},{9,11},{10,... | collective-permute-start | bytes 442376 | tf_op jit(solution)/shard_map/ppermute | solution.py:413
  4.3 0.1 collective-permute-start
  4.4 2.2 %shard_map.93 = bf16[8,432,128]{2,1,0:T(8,128)(2,1)} custom-call(bf16[128,1152]{1,0:T(8,128)(2,1)} %bitcast.13, bf16[128,1152]{1,0:T(8,128)(2,1)} %bitcast.14, bf16[128,1152]{1,0:T(8,128)(2,1)} %bitcast.15), custom_call_target="tpu_custom_call" | custom-call | tf_op jit(solution)/shard_map/pallas_call | solution.py:447
  6.5 1.0 %collective-permute-done.2 = bf16[64,1152]{1,0:T(8,128)(2,1)S(1)} collective-permute-done((bf16[64,1152]{1,0:T(8,128)(2,1)S(1)}, bf16[64,1152]{1,0:T(8,128)(2,1)S(1)}, u32[]{:S(2)}, u32[]{:S(2)}) %collective-permute-start.2) | collective-permute-done | bytes 147488 | tf_op jit(solution)/shard_map/ppermute | solution.py:413
  7.5 3.2 %collective-permute-done = bf16[64,1152]{1,0:T(8,128)(2,1)S(1)} collective-permute-done((bf16[64,1152]{1,0:T(8,128)(2,1)S(1)}, bf16[64,1152]{1,0:T(8,128)(2,1)S(1)}, u32[]{:S(2)}, u32[]{:S(2)}) %collective-permute-start) | collective-permute-done | bytes 147488 | tf_op jit(solution)/shard_map/ppermute | solution.py:413
  10.7 0.1 collective-permute-start.1
  10.8 1.4 %collective-permute-start.3 = (bf16[64,1152]{1,0:T(8,128)(2,1)S(1)}, bf16[64,1152]{1,0:T(8,128)(2,1)S(1)}, u32[]{:S(2)}, u32[]{:S(2)}) collective-permute-start(bf16[64,1152]{1,0:T(8,128)(2,1)S(1)} %collective-permute-done.2), channel_id=1, source_target_pairs={{0,1},{1,0},{2,4},{3,5},{4,2},{5,3},{6,7},{7,6},{8,9},{9,8},{10,12... | collective-permute-start | bytes 442376 | tf_op jit(solution)/shard_map/ppermute | solution.py:413
  12.2 0.0 collective-permute-done.4.refs_2_
  12.2 0.0 copy-start.2
  12.2 1.1 %collective-permute-start.5 = (bf16[128,1152]{1,0:T(8,128)(2,1)S(1)}, bf16[128,1152]{1,0:T(8,128)(2,1)S(1)}, u32[]{:S(2)}, u32[]{:S(2)}) collective-permute-start(bf16[128,1152]{1,0:T(8,128)(2,1)S(1)} %collective-permute-done.4.refs_2_), channel_id=1, source_target_pairs={{0,2},{1,3},{2,0},{3,1},{4,6},{5,7},{6,4},{7,5},{8,10},{9,11},{10,... | collective-permute-start | bytes 884744 | tf_op jit(solution)/shard_map/ppermute | solution.py:413
  13.3 0.7 pad_maximum_fusion.refs_1_
  14.0 0.6 collective-permute-done.1
  14.7 1.1 %collective-permute-start.6 = (bf16[64,1152]{1,0:T(8,128)(2,1)S(1)}, bf16[64,1152]{1,0:T(8,128)(2,1)S(1)}, u32[]{:S(2)}, u32[]{:S(2)}) collective-permute-start(bf16[64,1152]{1,0:T(8,128)(2,1)S(1)} %collective-permute-done.1), channel_id=1, source_target_pairs={{0,2},{1,3},{2,0},{3,1},{4,6},{5,7},{6,4},{7,5},{8,10},{9,11},{10,... | collective-permute-start | bytes 442376 | tf_op jit(solution)/shard_map/ppermute | solution.py:413
  15.8 1.8 %collective-permute-done.3 = bf16[64,1152]{1,0:T(8,128)(2,1)S(1)} collective-permute-done((bf16[64,1152]{1,0:T(8,128)(2,1)S(1)}, bf16[64,1152]{1,0:T(8,128)(2,1)S(1)}, u32[]{:S(2)}, u32[]{:S(2)}) %collective-permute-start.3) | collective-permute-done | bytes 147488 | tf_op jit(solution)/shard_map/ppermute | solution.py:413
  17.6 0.8 collective-permute-start.7
  18.5 0.7 pad_maximum_fusion.1.refs_3_
  19.2 0.0 collective-permute-done.5.refs_4_
  19.2 0.0 copy-start.3
  19.2 4.0 %all-to-all-start = ((bf16[8,432,128]{2,1,0:T(8,128)(2,1)}), bf16[8,432,128]{2,1,0:T(8,128)(2,1)S(1)}, u32[]{:S(2)}, u32[]{:S(2)}) async-start(bf16[8,432,128]{2,1,0:T(8,128)(2,1)} %shard_map.93), calls=%async_computation | async-start | bytes 1769472 | tf_op jit(solution)/shard_map/all_to_all | solution.py:453
  23.2 0.0 collective-permute-done.6
  23.2 1.2 %collective-permute-start.9 = (bf16[64,1152]{1,0:T(8,128)(2,1)S(1)}, bf16[64,1152]{1,0:T(8,128)(2,1)S(1)}, u32[]{:S(2)}, u32[]{:S(2)}) collective-permute-start(bf16[64,1152]{1,0:T(8,128)(2,1)S(1)} %broadcast_select_fusion.2), channel_id=1, source_target_pairs={{0,1},{1,0},{2,3},{3,2},{4,5},{5,4},{6,7},{7,6},{8,9},{9,8},{10,11... | collective-permute-start | bytes 442376 | tf_op jit(solution)/shard_map/ppermute | solution.py:413
  24.5 0.4 collective-permute-done.7
  24.9 0.1 collective-permute-start.10
  25.0 1.5 %collective-permute-start.8 = (bf16[128,1152]{1,0:T(8,128)(2,1)S(1)}, bf16[128,1152]{1,0:T(8,128)(2,1)S(1)}, u32[]{:S(2)}, u32[]{:S(2)}) collective-permute-start(bf16[128,1152]{1,0:T(8,128)(2,1)S(1)} %broadcast_select_fusion), channel_id=1, source_target_pairs={{0,1},{1,0},{2,3},{3,2},{4,5},{5,4},{6,7},{7,6},{8,9},{9,8},{10,11... | collective-permute-start | bytes 884744 | tf_op jit(solution)/shard_map/ppermute | solution.py:413
  26.5 0.7 pad_maximum_fusion.2.refs_5_
  27.3 0.0 copy-done.2
  27.3 2.2 %collective-permute-done.9 = bf16[64,1152]{1,0:T(8,128)(2,1)S(1)} collective-permute-done((bf16[64,1152]{1,0:T(8,128)(2,1)S(1)}, bf16[64,1152]{1,0:T(8,128)(2,1)S(1)}, u32[]{:S(2)}, u32[]{:S(2)}) %collective-permute-start.9) | collective-permute-done | bytes 147488 | tf_op jit(solution)/shard_map/ppermute | solution.py:413
  29.5 6.1 %collective-permute-done.10 = bf16[64,1152]{1,0:T(8,128)(2,1)S(1)} collective-permute-done((bf16[64,1152]{1,0:T(8,128)(2,1)S(1)}, bf16[64,1152]{1,0:T(8,128)(2,1)S(1)}, u32[]{:S(2)}, u32[]{:S(2)}) %collective-permute-start.10) | collective-permute-done | bytes 147488 | tf_op jit(solution)/shard_map/ppermute | solution.py:413
  35.6 0.7 pad_maximum_fusion.3.refs_7_
  36.3 0.0 copy-done.3
  36.3 7.9 %collective-permute-done.8.refs_6_ = bf16[128,1152]{1,0:T(8,128)(2,1)S(1)} collective-permute-done((bf16[128,1152]{1,0:T(8,128)(2,1)S(1)}, bf16[128,1152]{1,0:T(8,128)(2,1)S(1)}, u32[]{:S(2)}, u32[]{:S(2)}) %collective-permute-start.8) | collective-permute-done | bytes 294944 | tf_op jit(solution)/shard_map/ppermute | solution.py:413
  44.3 0.0 copy-start.4
  44.3 0.7 copy-done.4
  45.0 2.7 %shard_map.94 = (bf16[1024,1152]{1,0:T(8,128)(2,1)S(1)}, bf16[2,80,1024]{2,1,0:T(8,128)(2,1)S(1)}) custom-call(bf16[1152,1152]{1,0:T(8,128)(2,1)} %w_ref.1, bf16[128,1152]{1,0:T(8,128)(2,1)} %bitcast.12, bf16[128,1152]{1,0:T(8,128)(2,1)} %pad_maximum_fusion.refs_1_, bf16[128,1152]{1,0:T(8,128)(2,1)} %copy-done.2, ...), custom_call_target="tpu_custom_call" | custom-call | tf_op jit(solution)/shard_map/pallas_call | solution.py:464
  47.6 0.0 copy-start
  47.6 0.7 copy-done
  48.4 0.0 all-to-all-done.in_ref
  48.4 0.0 copy-start.1
  48.4 5.5 %shard_map.95 = (bf16[2,80,1024]{2,1,0:T(8,128)(2,1)S(1)}, bf16[2,80,1024]{2,1,0:T(8,128)(2,1)S(1)}, bf16[2,1024,80]{2,1,0:T(8,128)(2,1)S(1)}, bf16[144,1024]{1,...) custom-call(s32[1,4]{1,0:T(1,128)} %len_ref.3, ...), custom_call_target="tpu_custom_call" | custom-call | tf_op jit(solution)/shard_map/pallas_call | solution.py:469
  53.9 4.2 %collective-permute-start.17 = (bf16[144,1152]{1,0:T(8,128)(2,1)S(1)}, bf16[144,1152]{1,0:T(8,128)(2,1)S(1)}, u32[]{:S(2)}, u32[]{:S(2)}) collective-permute-start(bf16[144,1152]{1,0:T(8,128)(2,1)S(1)} %get-tuple-element.49), channel_id=1, source_target_pairs={{0,8},{8,0},{16,24},{24,16},{1,9},{9,1},{17,25},{25,17},{2,10},{10... | collective-permute-start | bytes 995336 | tf_op jit(solution)/shard_map/ppermute | solution.py:486
  58.1 0.0 copy-done.1
  58.1 5.5 %shard_map.96 = (bf16[432,128]{1,0:T(8,128)(2,1)S(1)}, bf16[432,128]{1,0:T(8,128)(2,1)}, bf16[432,128]{1,0:T(8,128)(2,1)}, bf16[432,128]{1,0:T(8,128)(2,1)}, bf1...) custom-call(s32[1,4]{1,0:T(1,128)} %len_ref.3, ...), custom_call_target="tpu_custom_call" | custom-call | tf_op jit(solution)/shard_map/pallas_call | solution.py:475
  63.6 0.0 collective-permute-done.17
  63.6 0.1 reduce-precision_convert_fusion
  63.7 0.6 collective-permute-start.18
  64.3 0.1 collective-permute-start.11
  64.4 2.2 %collective-permute-start.12 = (bf16[432,128]{1,0:T(8,128)(2,1)}, bf16[432,128]{1,0:T(8,128)(2,1)S(1)}, u32[]{:S(2)}, u32[]{:S(2)}) collective-permute-start(bf16[432,128]{1,0:T(8,128)(2,1)} %get-tuple-element.43), channel_id=1, source_target_pairs={{0,3},{1,2},{2,1},{3,0},{4,7},{5,6},{6,5},{7,4},{8,11},{9,10},{10,... | collective-permute-start | bytes 331784 | tf_op jit(solution)/shard_map/ppermute | solution.py:494
  66.6 2.1 %collective-permute-start.13 = (bf16[432,128]{1,0:T(8,128)(2,1)}, bf16[432,128]{1,0:T(8,128)(2,1)S(1)}, u32[]{:S(2)}, u32[]{:S(2)}) collective-permute-start(bf16[432,128]{1,0:T(8,128)(2,1)} %get-tuple-element.44), channel_id=1, source_target_pairs={{0,4},{1,5},{2,6},{3,7},{4,0},{5,1},{6,2},{7,3},{8,12},{9,13},{10,... | collective-permute-start | bytes 331784 | tf_op jit(solution)/shard_map/ppermute | solution.py:494
  68.7 0.0 collective-permute-start.14
  68.7 4.4 %collective-permute-done.18 = bf16[144,1152]{1,0:T(8,128)(2,1)S(1)} collective-permute-done((bf16[144,1152]{1,0:T(8,128)(2,1)S(1)}, bf16[144,1152]{1,0:T(8,128)(2,1)S(1)}, u32[]{:S(2)}, u32[]{:S(2)}) %collective-permute-start.18) | collective-permute-done | bytes 331808 | tf_op jit(solution)/shard_map/ppermute | solution.py:486
  73.2 0.3 collective-permute-start.15
  73.4 0.9 %add_multiply_fusion = f32[144,1152]{1,0:T(8,128)} fusion(bf16[144,1152]{1,0:T(8,128)(2,1)S(1)} %collective-permute-done.18, bf16[144,1152]{1,0:T(8,128)(2,1)S(1)} %reduce-precision_convert_fusion), kind=kLoop, calls=%fused_computation | loop fusion | flops 663552 | bytes 1327104 | tf_op jit(solution)/shard_map/mul | solution.py:489
  74.4 0.0 collective-permute-done.11.refs_1_
  74.4 1.2 %collective-permute-start.16 = (bf16[432,128]{1,0:T(8,128)(2,1)}, bf16[432,128]{1,0:T(8,128)(2,1)S(1)}, u32[]{:S(2)}, u32[]{:S(2)}) collective-permute-start(bf16[432,128]{1,0:T(8,128)(2,1)} %get-tuple-element.47), channel_id=1, source_target_pairs={{0,2},{1,3},{2,0},{3,1},{4,6},{5,7},{6,4},{7,5},{8,10},{9,11},{10,... | collective-permute-start | bytes 331784 | tf_op jit(solution)/shard_map/ppermute | solution.py:494
  75.6 0.0 collective-permute-done.12.refs_2_
  75.6 0.1 collective-permute-start.19
  75.7 0.0 collective-permute-done.13.refs_3_
  75.7 9.8 %collective-permute-done.14.refs_4_ = bf16[432,128]{1,0:T(8,128)(2,1)S(1)} collective-permute-done((bf16[432,128]{1,0:T(8,128)(2,1)}, bf16[432,128]{1,0:T(8,128)(2,1)S(1)}, u32[]{:S(2)}, u32[]{:S(2)}) %collective-permute-start.14) | collective-permute-done | bytes 110624 | tf_op jit(solution)/shard_map/ppermute | solution.py:494
  85.5 1.3 %collective-permute-done.15.refs_5_ = bf16[432,128]{1,0:T(8,128)(2,1)S(1)} collective-permute-done((bf16[432,128]{1,0:T(8,128)(2,1)}, bf16[432,128]{1,0:T(8,128)(2,1)S(1)}, u32[]{:S(2)}, u32[]{:S(2)}) %collective-permute-start.15) | collective-permute-done | bytes 110624 | tf_op jit(solution)/shard_map/ppermute | solution.py:494
  86.8 0.0 collective-permute-done.16.refs_6_
  86.8 0.0 collective-permute-done.19.refs_7_
  86.8 1.5 %shard_map.97 = (f32[128,1152]{1,0:T(8,128)}, f32[128,1152]{1,0:T(8,128)}, f32[128,1152]{1,0:T(8,128)}) custom-call(bf16[432,128]{1,0:T(8,128)(2,1)S(1)} %get-tuple-element.41.refs_0_, bf16[432,128]{1,0:T(8,128)(2,1)S(1)} %collective-permute-done.11.refs_1_, bf16[432,128]{1,0:T(8,128)(2,1)S(1)} %collective-permute-done.12.refs_2_, ...), custom_call_target="tpu_custom_call" | custom-call | tf_op jit(solution)/shard_map/pallas_call | solution.py:496
  (3 shorter events, 0.1 us)
Async XLA Ops:
  0.6 11.5 %collective-permute-start.4 = (bf16[128,1152]{1,0:T(8,128)(2,1)}, bf16[128,1152]{1,0:T(8,128)(2,1)S(1)}, u32[]{:S(2)}, u32[]{:S(2)}) collective-permute-start(bf16[128,1152]{1,0:T(8,128)(2,1)} %bitcast.11), channel_id=1, source_target_pairs={{0,1},{1,0},{2,4},{3,5},{4,2},{5,3},{6,7},{7,6},{8,9},{9,8},{10,12... | collective-permute-start | bytes 884744 | tf_op jit(solution)/shard_map/ppermute | solution.py:413
  1.9 5.7 %collective-permute-start.2 = (bf16[64,1152]{1,0:T(8,128)(2,1)S(1)}, bf16[64,1152]{1,0:T(8,128)(2,1)S(1)}, u32[]{:S(2)}, u32[]{:S(2)}) collective-permute-start(bf16[64,1152]{1,0:T(8,128)(2,1)S(1)} %get-tuple-element.56), channel_id=1, source_target_pairs={{0,2},{1,3},{2,0},{3,1},{4,6},{5,7},{6,4},{7,5},{8,10},{9,11},{10,... | collective-permute-start | bytes 442376 | tf_op jit(solution)/shard_map/ppermute | solution.py:413
  4.3 6.4 %collective-permute-start = (bf16[64,1152]{1,0:T(8,128)(2,1)S(1)}, bf16[64,1152]{1,0:T(8,128)(2,1)S(1)}, u32[]{:S(2)}, u32[]{:S(2)}) collective-permute-start(bf16[64,1152]{1,0:T(8,128)(2,1)S(1)} %get-tuple-element.57), channel_id=1, source_target_pairs={{0,2},{1,3},{2,0},{3,1},{4,6},{5,7},{6,4},{7,5},{8,10},{9,11},{10,... | collective-permute-start | bytes 442376 | tf_op jit(solution)/shard_map/ppermute | solution.py:413
  10.7 4.0 %collective-permute-start.1 = (bf16[64,1152]{1,0:T(8,128)(2,1)S(1)}, bf16[64,1152]{1,0:T(8,128)(2,1)S(1)}, u32[]{:S(2)}, u32[]{:S(2)}) collective-permute-start(bf16[64,1152]{1,0:T(8,128)(2,1)S(1)} %collective-permute-done), channel_id=1, source_target_pairs={{0,1},{1,0},{2,4},{3,5},{4,2},{5,3},{6,7},{7,6},{8,9},{9,8},{10,12... | collective-permute-start | bytes 442376 | tf_op jit(solution)/shard_map/ppermute | solution.py:413
  10.8 6.9 %collective-permute-start.3 = (bf16[64,1152]{1,0:T(8,128)(2,1)S(1)}, bf16[64,1152]{1,0:T(8,128)(2,1)S(1)}, u32[]{:S(2)}, u32[]{:S(2)}) collective-permute-start(bf16[64,1152]{1,0:T(8,128)(2,1)S(1)} %collective-permute-done.2), channel_id=1, source_target_pairs={{0,1},{1,0},{2,4},{3,5},{4,2},{5,3},{6,7},{7,6},{8,9},{9,8},{10,12... | collective-permute-start | bytes 442376 | tf_op jit(solution)/shard_map/ppermute | solution.py:413
  12.2 15.1 %copy-start.2 = (bf16[128,1152]{1,0:T(8,128)(2,1)}, bf16[128,1152]{1,0:T(8,128)(2,1)S(1)}, u32[]{:S(2)}) copy-start(bf16[128,1152]{1,0:T(8,128)(2,1)S(1)} %collective-permute-done.4.refs_2_) | copy-start | bytes 884740
  12.2 7.0 %collective-permute-start.5 = (bf16[128,1152]{1,0:T(8,128)(2,1)S(1)}, bf16[128,1152]{1,0:T(8,128)(2,1)S(1)}, u32[]{:S(2)}, u32[]{:S(2)}) collective-permute-start(bf16[128,1152]{1,0:T(8,128)(2,1)S(1)} %collective-permute-done.4.refs_2_), channel_id=1, source_target_pairs={{0,2},{1,3},{2,0},{3,1},{4,6},{5,7},{6,4},{7,5},{8,10},{9,11},{10,... | collective-permute-start | bytes 884744 | tf_op jit(solution)/shard_map/ppermute | solution.py:413
  14.7 8.5 %collective-permute-start.6 = (bf16[64,1152]{1,0:T(8,128)(2,1)S(1)}, bf16[64,1152]{1,0:T(8,128)(2,1)S(1)}, u32[]{:S(2)}, u32[]{:S(2)}) collective-permute-start(bf16[64,1152]{1,0:T(8,128)(2,1)S(1)} %collective-permute-done.1), channel_id=1, source_target_pairs={{0,2},{1,3},{2,0},{3,1},{4,6},{5,7},{6,4},{7,5},{8,10},{9,11},{10,... | collective-permute-start | bytes 442376 | tf_op jit(solution)/shard_map/ppermute | solution.py:413
  17.6 7.2 %collective-permute-start.7 = (bf16[64,1152]{1,0:T(8,128)(2,1)S(1)}, bf16[64,1152]{1,0:T(8,128)(2,1)S(1)}, u32[]{:S(2)}, u32[]{:S(2)}) collective-permute-start(bf16[64,1152]{1,0:T(8,128)(2,1)S(1)} %collective-permute-done.3), channel_id=1, source_target_pairs={{0,2},{1,3},{2,0},{3,1},{4,6},{5,7},{6,4},{7,5},{8,10},{9,11},{10,... | collective-permute-start | bytes 442376 | tf_op jit(solution)/shard_map/ppermute | solution.py:413
  19.2 17.1 %copy-start.3 = (bf16[128,1152]{1,0:T(8,128)(2,1)}, bf16[128,1152]{1,0:T(8,128)(2,1)S(1)}, u32[]{:S(2)}) copy-start(bf16[128,1152]{1,0:T(8,128)(2,1)S(1)} %collective-permute-done.5.refs_4_) | copy-start | bytes 884740
  19.2 29.2 %all-to-all-start = ((bf16[8,432,128]{2,1,0:T(8,128)(2,1)}), bf16[8,432,128]{2,1,0:T(8,128)(2,1)S(1)}, u32[]{:S(2)}, u32[]{:S(2)}) async-start(bf16[8,432,128]{2,1,0:T(8,128)(2,1)} %shard_map.93), calls=%async_computation | async-start | bytes 1769472 | tf_op jit(solution)/shard_map/all_to_all | solution.py:453
  23.2 6.3 %collective-permute-start.9 = (bf16[64,1152]{1,0:T(8,128)(2,1)S(1)}, bf16[64,1152]{1,0:T(8,128)(2,1)S(1)}, u32[]{:S(2)}, u32[]{:S(2)}) collective-permute-start(bf16[64,1152]{1,0:T(8,128)(2,1)S(1)} %broadcast_select_fusion.2), channel_id=1, source_target_pairs={{0,1},{1,0},{2,3},{3,2},{4,5},{5,4},{6,7},{7,6},{8,9},{9,8},{10,11... | collective-permute-start | bytes 442376 | tf_op jit(solution)/shard_map/ppermute | solution.py:413
  24.9 10.7 %collective-permute-start.10 = (bf16[64,1152]{1,0:T(8,128)(2,1)S(1)}, bf16[64,1152]{1,0:T(8,128)(2,1)S(1)}, u32[]{:S(2)}, u32[]{:S(2)}) collective-permute-start(bf16[64,1152]{1,0:T(8,128)(2,1)S(1)} %broadcast_select_fusion.1), channel_id=1, source_target_pairs={{0,1},{1,0},{2,3},{3,2},{4,5},{5,4},{6,7},{7,6},{8,9},{9,8},{10,11... | collective-permute-start | bytes 442376 | tf_op jit(solution)/shard_map/ppermute | solution.py:413
  25.0 19.2 %collective-permute-start.8 = (bf16[128,1152]{1,0:T(8,128)(2,1)S(1)}, bf16[128,1152]{1,0:T(8,128)(2,1)S(1)}, u32[]{:S(2)}, u32[]{:S(2)}) collective-permute-start(bf16[128,1152]{1,0:T(8,128)(2,1)S(1)} %broadcast_select_fusion), channel_id=1, source_target_pairs={{0,1},{1,0},{2,3},{3,2},{4,5},{5,4},{6,7},{7,6},{8,9},{9,8},{10,11... | collective-permute-start | bytes 884744 | tf_op jit(solution)/shard_map/ppermute | solution.py:413
  44.3 0.7 copy-start.4
  47.6 0.7 copy-start
  48.4 9.7 %copy-start.1 = (bf16[2,80,1024]{2,1,0:T(8,128)(2,1)S(1)}, bf16[2,80,1024]{2,1,0:T(8,128)(2,1)}, u32[]{:S(2)}) copy-start(bf16[2,80,1024]{2,1,0:T(8,128)(2,1)} %copy-done) | copy-start | bytes 983044
  53.9 9.7 %collective-permute-start.17 = (bf16[144,1152]{1,0:T(8,128)(2,1)S(1)}, bf16[144,1152]{1,0:T(8,128)(2,1)S(1)}, u32[]{:S(2)}, u32[]{:S(2)}) collective-permute-start(bf16[144,1152]{1,0:T(8,128)(2,1)S(1)} %get-tuple-element.49), channel_id=1, source_target_pairs={{0,8},{8,0},{16,24},{24,16},{1,9},{9,1},{17,25},{25,17},{2,10},{10... | collective-permute-start | bytes 995336 | tf_op jit(solution)/shard_map/ppermute | solution.py:486
  63.7 9.5 %collective-permute-start.18 = (bf16[144,1152]{1,0:T(8,128)(2,1)S(1)}, bf16[144,1152]{1,0:T(8,128)(2,1)S(1)}, u32[]{:S(2)}, u32[]{:S(2)}) collective-permute-start(bf16[144,1152]{1,0:T(8,128)(2,1)S(1)} %reduce-precision_convert_fusion), channel_id=1, source_target_pairs={{0,16},{8,24},{16,0},{24,8},{1,17},{9,25},{17,1},{25,9},{2,18},{10... | collective-permute-start | bytes 995336 | tf_op jit(solution)/shard_map/ppermute | solution.py:486
  64.3 10.1 %collective-permute-start.11 = (bf16[432,128]{1,0:T(8,128)(2,1)}, bf16[432,128]{1,0:T(8,128)(2,1)S(1)}, u32[]{:S(2)}, u32[]{:S(2)}) collective-permute-start(bf16[432,128]{1,0:T(8,128)(2,1)} %get-tuple-element.42), channel_id=1, source_target_pairs={{0,5},{1,4},{2,7},{3,6},{4,1},{5,0},{6,3},{7,2},{8,13},{9,12},{10,... | collective-permute-start | bytes 331784 | tf_op jit(solution)/shard_map/ppermute | solution.py:494
  64.4 11.2 %collective-permute-start.12 = (bf16[432,128]{1,0:T(8,128)(2,1)}, bf16[432,128]{1,0:T(8,128)(2,1)S(1)}, u32[]{:S(2)}, u32[]{:S(2)}) collective-permute-start(bf16[432,128]{1,0:T(8,128)(2,1)} %get-tuple-element.43), channel_id=1, source_target_pairs={{0,3},{1,2},{2,1},{3,0},{4,7},{5,6},{6,5},{7,4},{8,11},{9,10},{10,... | collective-permute-start | bytes 331784 | tf_op jit(solution)/shard_map/ppermute | solution.py:494
  66.6 9.0 %collective-permute-start.13 = (bf16[432,128]{1,0:T(8,128)(2,1)}, bf16[432,128]{1,0:T(8,128)(2,1)S(1)}, u32[]{:S(2)}, u32[]{:S(2)}) collective-permute-start(bf16[432,128]{1,0:T(8,128)(2,1)} %get-tuple-element.44), channel_id=1, source_target_pairs={{0,4},{1,5},{2,6},{3,7},{4,0},{5,1},{6,2},{7,3},{8,12},{9,13},{10,... | collective-permute-start | bytes 331784 | tf_op jit(solution)/shard_map/ppermute | solution.py:494
  68.7 16.8 %collective-permute-start.14 = (bf16[432,128]{1,0:T(8,128)(2,1)}, bf16[432,128]{1,0:T(8,128)(2,1)S(1)}, u32[]{:S(2)}, u32[]{:S(2)}) collective-permute-start(bf16[432,128]{1,0:T(8,128)(2,1)} %get-tuple-element.45), channel_id=1, source_target_pairs={{0,7},{1,6},{2,5},{3,4},{4,3},{5,2},{6,1},{7,0},{8,15},{9,14},{10,... | collective-permute-start | bytes 331784 | tf_op jit(solution)/shard_map/ppermute | solution.py:494
  73.2 13.6 %collective-permute-start.15 = (bf16[432,128]{1,0:T(8,128)(2,1)}, bf16[432,128]{1,0:T(8,128)(2,1)S(1)}, u32[]{:S(2)}, u32[]{:S(2)}) collective-permute-start(bf16[432,128]{1,0:T(8,128)(2,1)} %get-tuple-element.46), channel_id=1, source_target_pairs={{0,6},{1,7},{2,4},{3,5},{4,2},{5,3},{6,0},{7,1},{8,14},{9,15},{10,... | collective-permute-start | bytes 331784 | tf_op jit(solution)/shard_map/ppermute | solution.py:494
  74.4 12.4 %collective-permute-start.16 = (bf16[432,128]{1,0:T(8,128)(2,1)}, bf16[432,128]{1,0:T(8,128)(2,1)S(1)}, u32[]{:S(2)}, u32[]{:S(2)}) collective-permute-start(bf16[432,128]{1,0:T(8,128)(2,1)} %get-tuple-element.47), channel_id=1, source_target_pairs={{0,2},{1,3},{2,0},{3,1},{4,6},{5,7},{6,4},{7,5},{8,10},{9,11},{10,... | collective-permute-start | bytes 331784 | tf_op jit(solution)/shard_map/ppermute | solution.py:494
  75.6 11.2 %collective-permute-start.19 = (bf16[432,128]{1,0:T(8,128)(2,1)}, bf16[432,128]{1,0:T(8,128)(2,1)S(1)}, u32[]{:S(2)}, u32[]{:S(2)}) collective-permute-start(bf16[432,128]{1,0:T(8,128)(2,1)} %get-tuple-element.52), channel_id=1, source_target_pairs={{0,1},{1,0},{2,3},{3,2},{4,5},{5,4},{6,7},{7,6},{8,9},{9,8},{10,11... | collective-permute-start | bytes 331784 | tf_op jit(solution)/shard_map/ppermute | solution.py:494

commit v5 on v2

--- a/solution.py
+++ b/solution.py
@@ -348,7 +348,7 @@
             d = d_s[head, :, columns]
             probs = probs_s[image, head, 0:width, 0:width]
             att = att_all[head * HEAD_DIM:(head + 1) * HEAD_DIM, :]
-            delta = jnp.sum(d[0:HEAD_DIM, :].astype(F32) * att, axis=0, keepdims=True)
+            delta = jnp.sum(d.astype(F32)[0:HEAD_DIM, :] * att, axis=0, keepdims=True)
             d_probs = dot(vt_s[head, columns, :], d)
             d_scores = (scale * probs.astype(F32) * (d_probs - delta)).astype(BF16)
             dq_s[head, :, columns] += dot(k_s[head, :, columns], d_scores)
@@ -357,16 +357,17 @@
 
     each_image(len_s, tok, shards, work)
 
+    me = lax.axis_index("seq")
     stores = []
     for i, ref in enumerate((dq_s, dk_s, dv_s)):
         whole = joined(ref)
+        rows = pl.ds(i * part, part)
         for shard in range(shards):
             out_s[shard, i * part:(i + 1) * part, :] = whole[:, shard * tok:(shard + 1) * tok]
-    me = lax.axis_index("seq")
-    for n in range(shards - 1, 0, -1):
-        store = pltpu.make_async_copy(out_s.at[me ^ n], outs[n], out_sem.at[n])
-        store.start()
-        stores.append(store)
+        for n in BACK_ORDER[1:]:
+            store = pltpu.make_async_copy(out_s.at[me ^ n, rows], outs[n].at[rows], out_sem.at[i, n])
+            store.start()
+            stores.append(store)
     outs[0][...] = out_s[me]
     for store in stores:
         store.wait()
@@ -491,7 +492,7 @@
         out_shape=[shape((3 * part, tok))] + [pltpu.HBM((3 * part, tok), BF16)] * (shards - 1),
         in_specs=[HBM] + [VMEM] * (7 + late), out_specs=[VMEM] + [HBM] * (shards - 1), compiler_params=PARAMS,
         scratch_shapes=[len_s] + scratch(wide) + scratch(wide, wide, wide, kind=F32)
-        + scratch((shards, 3 * part, tok)) + [DMA, DMA((shards,))],
+        + scratch((shards, 3 * part, tok)) + [DMA, DMA((3, shards))],
     )(*in_hbm(lengths), w_rows, q_t, k_t, v_r, attended, probs, d_part, *pieces[early:])
     sums = w_part.astype(F32)
     step = 1

time: 79.4 us -> 79.5 us (level)
  starting transfers between devices: 22.4 us -> 23.5 us
    ppermute x2, starting transfers between devices: 3.62 us -> 4.66 us  [head_body(): lax.ppermute(w_part, 'dp', pairs)]
  transfers between devices with their start and end apart: 20 -> 20, of which waited for: 10 -> 11; matrix products, arithmetic and copies ran while one was open for 1% -> 1% of each run, Pallas kernels for 18% -> 17%
where the time goes in v5:
time: 79.5 us
  waiting for transfers between devices  38.7 us (49%)
  starting transfers between devices  23.5 us (30%)
  Pallas kernels  15.4 us (19%)
  other arithmetic  1.11 us (1%)
    ppermute x10, waiting for transfers between devices, move(): return lax.ppermute(value, 'seq', pairs)  22.8 us
    ppermute x7, waiting for transfers between devices, head_body(): lax.ppermute(block, 'seq', [(i, i ^ n) for i in range(shards)])  11.8 us
    ppermute x10, starting transfers between devices, move(): return lax.ppermute(value, 'seq', pairs)  8.48 us
    pallas_call x1, Pallas kernels, head_body(): pl.pallas_call(functools.partial(forward_kernel, early), out_shape=[shape...  6.16 us
    ppermute x7, starting transfers between devices, head_body(): lax.ppermute(block, 'seq', [(i, i ^ n) for i in range(shards)])  6.11 us
    pallas_call x1, Pallas kernels, head_body(): pl.pallas_call(functools.partial(backward_kernel, early), out_shape=[shap...  5.26 us
    ppermute x2, starting transfers between devices, head_body(): lax.ppermute(w_part, 'dp', pairs)  4.66 us
    all_to_all x1, starting transfers between devices, head_body(): arrived = lax.all_to_all(after(sent, *pieces[1:3]), 'seq', 0, 0, tiled=True)  4.21 us
  transfers between devices with their start and end apart: 20, of which 11 were waited for; matrix products, arithmetic and copies ran while one was open for 1% of the time, Pallas kernels for 17%

profile of v5, /device:TPU:17, one launch (start us, length us, event | category | flops | bytes accessed | tf_op | source)
XLA Modules:
  0.0 79.5 jit_solution(12091845032192869773)
XLA Ops:
  0.6 1.4 %collective-permute-start = (bf16[128,1152]{1,0:T(8,128)(2,1)}, bf16[128,1152]{1,0:T(8,128)(2,1)S(1)}, u32[]{:S(2)}, u32[]{:S(2)}) collective-permute-start(bf16[128,1152]{1,0:T(8,128)(2,1)} %bitcast.7), channel_id=1, source_target_pairs={{0,2},{1,3},{2,0},{3,1},{4,6},{5,7},{6,4},{7,5},{8,10},{9,11},{10,... | collective-permute-start | bytes 884744 | tf_op jit(solution)/shard_map/ppermute | solution.py:426
  2.0 0.0 collective-permute-start.1
  2.0 2.2 %shard_map.93 = bf16[8,432,128]{2,1,0:T(8,128)(2,1)} custom-call(bf16[128,1152]{1,0:T(8,128)(2,1)} %bitcast.10, bf16[128,1152]{1,0:T(8,128)(2,1)} %bitcast.11, bf16[128,1152]{1,0:T(8,128)(2,1)} %bitcast.12), custom_call_target="tpu_custom_call" | custom-call | tf_op jit(solution)/shard_map/pallas_call | solution.py:460
  4.2 4.6 %collective-permute-done.refs_1_ = bf16[128,1152]{1,0:T(8,128)(2,1)S(1)} collective-permute-done((bf16[128,1152]{1,0:T(8,128)(2,1)}, bf16[128,1152]{1,0:T(8,128)(2,1)S(1)}, u32[]{:S(2)}, u32[]{:S(2)}) %collective-permute-start) | collective-permute-done | bytes 294944 | tf_op jit(solution)/shard_map/ppermute | solution.py:426
  8.8 0.0 copy-start.4
  8.8 0.2 collective-permute-start.2
  9.0 0.8 %collective-permute-done.1.refs_2_ = bf16[128,1152]{1,0:T(8,128)(2,1)S(1)} collective-permute-done((bf16[128,1152]{1,0:T(8,128)(2,1)}, bf16[128,1152]{1,0:T(8,128)(2,1)S(1)}, u32[]{:S(2)}, u32[]{:S(2)}) %collective-permute-start.1) | collective-permute-done | bytes 294944 | tf_op jit(solution)/shard_map/ppermute | solution.py:426
  9.8 0.0 copy-start.2
  9.8 1.5 %collective-permute-start.3 = (bf16[128,1152]{1,0:T(8,128)(2,1)S(1)}, bf16[128,1152]{1,0:T(8,128)(2,1)S(1)}, u32[]{:S(2)}, u32[]{:S(2)}) collective-permute-start(bf16[128,1152]{1,0:T(8,128)(2,1)S(1)} %collective-permute-done.1.refs_2_), channel_id=1, source_target_pairs={{0,2},{1,3},{2,0},{3,1},{4,6},{5,7},{6,4},{7,5},{8,10},{9,11},{10,... | collective-permute-start | bytes 884744 | tf_op jit(solution)/shard_map/ppermute | solution.py:426
  11.3 4.2 %all-to-all-start = ((bf16[8,432,128]{2,1,0:T(8,128)(2,1)}), bf16[8,432,128]{2,1,0:T(8,128)(2,1)S(1)}, u32[]{:S(2)}, u32[]{:S(2)}) async-start(bf16[8,432,128]{2,1,0:T(8,128)(2,1)} %shard_map.93), calls=%async_computation | async-start | bytes 1769472 | tf_op jit(solution)/shard_map/all_to_all | solution.py:466
  15.5 0.2 collective-permute-done.2.refs_3_
  15.7 0.0 copy-start
  15.8 1.4 %collective-permute-start.4 = (bf16[32,1152]{1,0:T(8,128)(2,1)S(1)}, bf16[32,1152]{1,0:T(8,128)(2,1)S(1)}, u32[]{:S(2)}, u32[]{:S(2)}) collective-permute-start(bf16[32,1152]{1,0:T(8,128)(2,1)S(1)} %get-tuple-element.57), channel_id=1, source_target_pairs={{0,2},{1,3},{2,0},{3,1},{4,6},{5,7},{6,4},{7,5},{8,10},{9,11},{10,... | collective-permute-start | bytes 221192 | tf_op jit(solution)/shard_map/ppermute | solution.py:426
  17.1 0.2 collective-permute-start.5
  17.3 1.3 %collective-permute-start.6 = (bf16[32,1152]{1,0:T(8,128)(2,1)S(1)}, bf16[32,1152]{1,0:T(8,128)(2,1)S(1)}, u32[]{:S(2)}, u32[]{:S(2)}) collective-permute-start(bf16[32,1152]{1,0:T(8,128)(2,1)S(1)} %get-tuple-element.55), channel_id=1, source_target_pairs={{0,2},{1,3},{2,0},{3,1},{4,6},{5,7},{6,4},{7,5},{8,10},{9,11},{10,... | collective-permute-start | bytes 221192 | tf_op jit(solution)/shard_map/ppermute | solution.py:426
  18.6 0.2 collective-permute-start.7
  18.8 0.0 collective-permute-done.3.refs_4_
  18.8 0.0 copy-start.3
  18.8 1.3 %collective-permute-start.8 = (bf16[128,1152]{1,0:T(8,128)(2,1)S(1)}, bf16[128,1152]{1,0:T(8,128)(2,1)S(1)}, u32[]{:S(2)}, u32[]{:S(2)}) collective-permute-start(bf16[128,1152]{1,0:T(8,128)(2,1)S(1)} %broadcast_select_fusion.1), channel_id=1, source_target_pairs={{0,1},{1,0},{2,3},{3,2},{4,5},{5,4},{6,7},{7,6},{8,9},{9,8},{10,11... | collective-permute-start | bytes 884744 | tf_op jit(solution)/shard_map/ppermute | solution.py:426
  20.1 12.5 %collective-permute-done.4 = bf16[32,1152]{1,0:T(8,128)(2,1)S(1)} collective-permute-done((bf16[32,1152]{1,0:T(8,128)(2,1)S(1)}, bf16[32,1152]{1,0:T(8,128)(2,1)S(1)}, u32[]{:S(2)}, u32[]{:S(2)}) %collective-permute-start.4) | collective-permute-done | bytes 73760 | tf_op jit(solution)/shard_map/ppermute | solution.py:426
  32.5 1.6 %collective-permute-done.5 = bf16[32,1152]{1,0:T(8,128)(2,1)S(1)} collective-permute-done((bf16[32,1152]{1,0:T(8,128)(2,1)S(1)}, bf16[32,1152]{1,0:T(8,128)(2,1)S(1)}, u32[]{:S(2)}, u32[]{:S(2)}) %collective-permute-start.5) | collective-permute-done | bytes 73760 | tf_op jit(solution)/shard_map/ppermute | solution.py:426
  34.1 1.6 %collective-permute-done.6 = bf16[32,1152]{1,0:T(8,128)(2,1)S(1)} collective-permute-done((bf16[32,1152]{1,0:T(8,128)(2,1)S(1)}, bf16[32,1152]{1,0:T(8,128)(2,1)S(1)}, u32[]{:S(2)}, u32[]{:S(2)}) %collective-permute-start.6) | collective-permute-done | bytes 73760 | tf_op jit(solution)/shard_map/ppermute | solution.py:426
  35.7 1.6 %collective-permute-done.7 = bf16[32,1152]{1,0:T(8,128)(2,1)S(1)} collective-permute-done((bf16[32,1152]{1,0:T(8,128)(2,1)S(1)}, bf16[32,1152]{1,0:T(8,128)(2,1)S(1)}, u32[]{:S(2)}, u32[]{:S(2)}) %collective-permute-start.7) | collective-permute-done | bytes 73760 | tf_op jit(solution)/shard_map/ppermute | solution.py:426
  37.3 0.0 copy-start.1
  37.4 1.1 %collective-permute-start.9 = (bf16[128,1152]{1,0:T(8,128)(2,1)S(1)}, bf16[128,1152]{1,0:T(8,128)(2,1)S(1)}, u32[]{:S(2)}, u32[]{:S(2)}) collective-permute-start(bf16[128,1152]{1,0:T(8,128)(2,1)S(1)} %broadcast_select_fusion), channel_id=1, source_target_pairs={{0,1},{1,0},{2,3},{3,2},{4,5},{5,4},{6,7},{7,6},{8,9},{9,8},{10,11... | collective-permute-start | bytes 884744 | tf_op jit(solution)/shard_map/ppermute | solution.py:426
  38.5 0.0 all-to-all-done.in_ref
  38.5 0.0 copy-done.4
  38.5 0.0 copy-done.2
  38.5 0.0 copy-done
  38.5 0.0 copy-done.3
  38.5 0.0 copy-done.1
  38.5 6.2 %shard_map.94 = (bf16[2,80,1024]{2,1,0:T(8,128)(2,1)S(1)}, bf16[2,80,1024]{2,1,0:T(8,128)(2,1)S(1)}, bf16[2,1024,80]{2,1,0:T(8,128)(2,1)S(1)}, bf16[144,1024]{1,...) custom-call(s32[1,4]{1,0:T(1,128)} %len_ref.3, ...), custom_call_target="tpu_custom_call" | custom-call | tf_op jit(solution)/shard_map/pallas_call | solution.py:479
  44.7 0.0 collective-permute-done.8.refs_0_
  44.7 0.0 collective-permute-done.9.refs_1_
  44.7 0.3 shard_map.96
  45.1 3.0 %collective-permute-start.16 = (bf16[144,1152]{1,0:T(8,128)(2,1)S(1)}, bf16[144,1152]{1,0:T(8,128)(2,1)S(1)}, u32[]{:S(2)}, u32[]{:S(2)}) collective-permute-start(bf16[144,1152]{1,0:T(8,128)(2,1)S(1)} %shard_map.96), channel_id=1, source_target_pairs={{0,8},{8,0},{16,24},{24,16},{1,9},{9,1},{17,25},{25,17},{2,10},{10... | collective-permute-start | bytes 995336 | tf_op jit(solution)/shard_map/ppermute | solution.py:501
  48.1 5.3 %shard_map.95 = (bf16[432,128]{1,0:T(8,128)(2,1)S(1)}, bf16[432,128]{1,0:T(8,128)(2,1)}, bf16[432,128]{1,0:T(8,128)(2,1)}, bf16[432,128]{1,0:T(8,128)(2,1)}, bf1...) custom-call(s32[1,4]{1,0:T(1,128)} %len_ref.3, ...), custom_call_target="tpu_custom_call" | custom-call | tf_op jit(solution)/shard_map/pallas_call | solution.py:490
  53.4 0.0 collective-permute-done.16
  53.4 0.1 reduce-precision_convert_fusion
  53.5 1.6 %collective-permute-start.17 = (bf16[144,1152]{1,0:T(8,128)(2,1)S(1)}, bf16[144,1152]{1,0:T(8,128)(2,1)S(1)}, u32[]{:S(2)}, u32[]{:S(2)}) collective-permute-start(bf16[144,1152]{1,0:T(8,128)(2,1)S(1)} %reduce-precision_convert_fusion), channel_id=1, source_target_pairs={{0,16},{8,24},{16,0},{24,8},{1,17},{9,25},{17,1},{25,9},{2,18},{10... | collective-permute-start | bytes 995336 | tf_op jit(solution)/shard_map/ppermute | solution.py:501
  55.1 0.4 collective-permute-start.10
  55.5 2.2 %collective-permute-start.11 = (bf16[432,128]{1,0:T(8,128)(2,1)}, bf16[432,128]{1,0:T(8,128)(2,1)S(1)}, u32[]{:S(2)}, u32[]{:S(2)}) collective-permute-start(bf16[432,128]{1,0:T(8,128)(2,1)} %get-tuple-element.41), channel_id=1, source_target_pairs={{0,3},{1,2},{2,1},{3,0},{4,7},{5,6},{6,5},{7,4},{8,11},{9,10},{10,... | collective-permute-start | bytes 331784 | tf_op jit(solution)/shard_map/ppermute | solution.py:509
  57.7 1.5 %collective-permute-start.12 = (bf16[432,128]{1,0:T(8,128)(2,1)}, bf16[432,128]{1,0:T(8,128)(2,1)S(1)}, u32[]{:S(2)}, u32[]{:S(2)}) collective-permute-start(bf16[432,128]{1,0:T(8,128)(2,1)} %get-tuple-element.42), channel_id=1, source_target_pairs={{0,4},{1,5},{2,6},{3,7},{4,0},{5,1},{6,2},{7,3},{8,12},{9,13},{10,... | collective-permute-start | bytes 331784 | tf_op jit(solution)/shard_map/ppermute | solution.py:509
  59.2 0.0 collective-permute-start.13
  59.2 4.0 %collective-permute-done.17 = bf16[144,1152]{1,0:T(8,128)(2,1)S(1)} collective-permute-done((bf16[144,1152]{1,0:T(8,128)(2,1)S(1)}, bf16[144,1152]{1,0:T(8,128)(2,1)S(1)}, u32[]{:S(2)}, u32[]{:S(2)}) %collective-permute-start.17) | collective-permute-done | bytes 331808 | tf_op jit(solution)/shard_map/ppermute | solution.py:501
  63.2 0.5 collective-permute-start.14
  63.7 0.9 %add_multiply_fusion = f32[144,1152]{1,0:T(8,128)} fusion(bf16[144,1152]{1,0:T(8,128)(2,1)S(1)} %collective-permute-done.17, bf16[144,1152]{1,0:T(8,128)(2,1)S(1)} %reduce-precision_convert_fusion), kind=kLoop, calls=%fused_computation | loop fusion | flops 663552 | bytes 1327104 | tf_op jit(solution)/shard_map/mul | solution.py:504
  64.6 0.0 collective-permute-done.10.refs_1_
  64.6 0.8 %collective-permute-start.15 = (bf16[432,128]{1,0:T(8,128)(2,1)}, bf16[432,128]{1,0:T(8,128)(2,1)S(1)}, u32[]{:S(2)}, u32[]{:S(2)}) collective-permute-start(bf16[432,128]{1,0:T(8,128)(2,1)} %get-tuple-element.45), channel_id=1, source_target_pairs={{0,2},{1,3},{2,0},{3,1},{4,6},{5,7},{6,4},{7,5},{8,10},{9,11},{10,... | collective-permute-start | bytes 331784 | tf_op jit(solution)/shard_map/ppermute | solution.py:509
  65.5 0.0 collective-permute-done.11.refs_2_
  65.5 0.7 collective-permute-start.18
  66.2 0.3 collective-permute-done.12.refs_3_
  66.5 9.3 %collective-permute-done.13.refs_4_ = bf16[432,128]{1,0:T(8,128)(2,1)S(1)} collective-permute-done((bf16[432,128]{1,0:T(8,128)(2,1)}, bf16[432,128]{1,0:T(8,128)(2,1)S(1)}, u32[]{:S(2)}, u32[]{:S(2)}) %collective-permute-start.13) | collective-permute-done | bytes 110624 | tf_op jit(solution)/shard_map/ppermute | solution.py:509
  75.8 2.2 %collective-permute-done.14.refs_5_ = bf16[432,128]{1,0:T(8,128)(2,1)S(1)} collective-permute-done((bf16[432,128]{1,0:T(8,128)(2,1)}, bf16[432,128]{1,0:T(8,128)(2,1)S(1)}, u32[]{:S(2)}, u32[]{:S(2)}) %collective-permute-start.14) | collective-permute-done | bytes 110624 | tf_op jit(solution)/shard_map/ppermute | solution.py:509
  78.0 0.0 collective-permute-done.15.refs_6_
  78.0 0.0 collective-permute-done.18.refs_7_
  78.0 1.5 %shard_map.97 = (f32[128,1152]{1,0:T(8,128)}, f32[128,1152]{1,0:T(8,128)}, f32[128,1152]{1,0:T(8,128)}) custom-call(bf16[432,128]{1,0:T(8,128)(2,1)S(1)} %get-tuple-element.39.refs_0_, bf16[432,128]{1,0:T(8,128)(2,1)S(1)} %collective-permute-done.10.refs_1_, bf16[432,128]{1,0:T(8,128)(2,1)S(1)} %collective-permute-done.11.refs_2_, ...), custom_call_target="tpu_custom_call" | custom-call | tf_op jit(solution)/shard_map/pallas_call | solution.py:511
  (7 shorter events, 0.1 us)
Async XLA Ops:
  0.6 8.2 %collective-permute-start = (bf16[128,1152]{1,0:T(8,128)(2,1)}, bf16[128,1152]{1,0:T(8,128)(2,1)S(1)}, u32[]{:S(2)}, u32[]{:S(2)}) collective-permute-start(bf16[128,1152]{1,0:T(8,128)(2,1)} %bitcast.7), channel_id=1, source_target_pairs={{0,2},{1,3},{2,0},{3,1},{4,6},{5,7},{6,4},{7,5},{8,10},{9,11},{10,... | collective-permute-start | bytes 884744 | tf_op jit(solution)/shard_map/ppermute | solution.py:426
  2.0 7.8 %collective-permute-start.1 = (bf16[128,1152]{1,0:T(8,128)(2,1)}, bf16[128,1152]{1,0:T(8,128)(2,1)S(1)}, u32[]{:S(2)}, u32[]{:S(2)}) collective-permute-start(bf16[128,1152]{1,0:T(8,128)(2,1)} %bitcast.8), channel_id=1, source_target_pairs={{0,1},{1,0},{2,4},{3,5},{4,2},{5,3},{6,7},{7,6},{8,9},{9,8},{10,12... | collective-permute-start | bytes 884744 | tf_op jit(solution)/shard_map/ppermute | solution.py:426
  8.8 29.7 %copy-start.4 = (bf16[128,1152]{1,0:T(8,128)(2,1)}, bf16[128,1152]{1,0:T(8,128)(2,1)S(1)}, u32[]{:S(2)}) copy-start(bf16[128,1152]{1,0:T(8,128)(2,1)S(1)} %collective-permute-done.refs_1_) | copy-start | bytes 884740
  8.8 7.0 %collective-permute-start.2 = (bf16[128,1152]{1,0:T(8,128)(2,1)S(1)}, bf16[128,1152]{1,0:T(8,128)(2,1)S(1)}, u32[]{:S(2)}, u32[]{:S(2)}) collective-permute-start(bf16[128,1152]{1,0:T(8,128)(2,1)S(1)} %collective-permute-done.refs_1_), channel_id=1, source_target_pairs={{0,1},{1,0},{2,4},{3,5},{4,2},{5,3},{6,7},{7,6},{8,9},{9,8},{10,12... | collective-permute-start | bytes 884744 | tf_op jit(solution)/shard_map/ppermute | solution.py:426
  9.8 28.7 %copy-start.2 = (bf16[128,1152]{1,0:T(8,128)(2,1)}, bf16[128,1152]{1,0:T(8,128)(2,1)S(1)}, u32[]{:S(2)}) copy-start(bf16[128,1152]{1,0:T(8,128)(2,1)S(1)} %collective-permute-done.1.refs_2_) | copy-start | bytes 884740
  9.8 9.0 %collective-permute-start.3 = (bf16[128,1152]{1,0:T(8,128)(2,1)S(1)}, bf16[128,1152]{1,0:T(8,128)(2,1)S(1)}, u32[]{:S(2)}, u32[]{:S(2)}) collective-permute-start(bf16[128,1152]{1,0:T(8,128)(2,1)S(1)} %collective-permute-done.1.refs_2_), channel_id=1, source_target_pairs={{0,2},{1,3},{2,0},{3,1},{4,6},{5,7},{6,4},{7,5},{8,10},{9,11},{10,... | collective-permute-start | bytes 884744 | tf_op jit(solution)/shard_map/ppermute | solution.py:426
  11.3 27.2 %all-to-all-start = ((bf16[8,432,128]{2,1,0:T(8,128)(2,1)}), bf16[8,432,128]{2,1,0:T(8,128)(2,1)S(1)}, u32[]{:S(2)}, u32[]{:S(2)}) async-start(bf16[8,432,128]{2,1,0:T(8,128)(2,1)} %shard_map.93), calls=%async_computation | async-start | bytes 1769472 | tf_op jit(solution)/shard_map/all_to_all | solution.py:466
  15.7 22.8 %copy-start = (bf16[128,1152]{1,0:T(8,128)(2,1)}, bf16[128,1152]{1,0:T(8,128)(2,1)S(1)}, u32[]{:S(2)}) copy-start(bf16[128,1152]{1,0:T(8,128)(2,1)S(1)} %collective-permute-done.2.refs_3_) | copy-start | bytes 884740
  15.8 16.8 %collective-permute-start.4 = (bf16[32,1152]{1,0:T(8,128)(2,1)S(1)}, bf16[32,1152]{1,0:T(8,128)(2,1)S(1)}, u32[]{:S(2)}, u32[]{:S(2)}) collective-permute-start(bf16[32,1152]{1,0:T(8,128)(2,1)S(1)} %get-tuple-element.57), channel_id=1, source_target_pairs={{0,2},{1,3},{2,0},{3,1},{4,6},{5,7},{6,4},{7,5},{8,10},{9,11},{10,... | collective-permute-start | bytes 221192 | tf_op jit(solution)/shard_map/ppermute | solution.py:426
  17.1 17.0 %collective-permute-start.5 = (bf16[32,1152]{1,0:T(8,128)(2,1)S(1)}, bf16[32,1152]{1,0:T(8,128)(2,1)S(1)}, u32[]{:S(2)}, u32[]{:S(2)}) collective-permute-start(bf16[32,1152]{1,0:T(8,128)(2,1)S(1)} %get-tuple-element.56), channel_id=1, source_target_pairs={{0,2},{1,3},{2,0},{3,1},{4,6},{5,7},{6,4},{7,5},{8,10},{9,11},{10,... | collective-permute-start | bytes 221192 | tf_op jit(solution)/shard_map/ppermute | solution.py:426
  17.3 18.4 %collective-permute-start.6 = (bf16[32,1152]{1,0:T(8,128)(2,1)S(1)}, bf16[32,1152]{1,0:T(8,128)(2,1)S(1)}, u32[]{:S(2)}, u32[]{:S(2)}) collective-permute-start(bf16[32,1152]{1,0:T(8,128)(2,1)S(1)} %get-tuple-element.55), channel_id=1, source_target_pairs={{0,2},{1,3},{2,0},{3,1},{4,6},{5,7},{6,4},{7,5},{8,10},{9,11},{10,... | collective-permute-start | bytes 221192 | tf_op jit(solution)/shard_map/ppermute | solution.py:426
  18.6 18.7 %collective-permute-start.7 = (bf16[32,1152]{1,0:T(8,128)(2,1)S(1)}, bf16[32,1152]{1,0:T(8,128)(2,1)S(1)}, u32[]{:S(2)}, u32[]{:S(2)}) collective-permute-start(bf16[32,1152]{1,0:T(8,128)(2,1)S(1)} %get-tuple-element.54), channel_id=1, source_target_pairs={{0,2},{1,3},{2,0},{3,1},{4,6},{5,7},{6,4},{7,5},{8,10},{9,11},{10,... | collective-permute-start | bytes 221192 | tf_op jit(solution)/shard_map/ppermute | solution.py:426
  18.8 19.7 %copy-start.3 = (bf16[128,1152]{1,0:T(8,128)(2,1)}, bf16[128,1152]{1,0:T(8,128)(2,1)S(1)}, u32[]{:S(2)}) copy-start(bf16[128,1152]{1,0:T(8,128)(2,1)S(1)} %collective-permute-done.3.refs_4_) | copy-start | bytes 884740
  18.8 25.9 %collective-permute-start.8 = (bf16[128,1152]{1,0:T(8,128)(2,1)S(1)}, bf16[128,1152]{1,0:T(8,128)(2,1)S(1)}, u32[]{:S(2)}, u32[]{:S(2)}) collective-permute-start(bf16[128,1152]{1,0:T(8,128)(2,1)S(1)} %broadcast_select_fusion.1), channel_id=1, source_target_pairs={{0,1},{1,0},{2,3},{3,2},{4,5},{5,4},{6,7},{7,6},{8,9},{9,8},{10,11... | collective-permute-start | bytes 884744 | tf_op jit(solution)/shard_map/ppermute | solution.py:426
  37.3 1.2 %copy-start.1 = (bf16[128,1152]{1,0:T(8,128)(2,1)}, bf16[128,1152]{1,0:T(8,128)(2,1)S(1)}, u32[]{:S(2)}) copy-start(bf16[128,1152]{1,0:T(8,128)(2,1)S(1)} %constant_dynamic-update-slice_fusion.refs_5_) | copy-start | bytes 884740
  37.4 7.4 %collective-permute-start.9 = (bf16[128,1152]{1,0:T(8,128)(2,1)S(1)}, bf16[128,1152]{1,0:T(8,128)(2,1)S(1)}, u32[]{:S(2)}, u32[]{:S(2)}) collective-permute-start(bf16[128,1152]{1,0:T(8,128)(2,1)S(1)} %broadcast_select_fusion), channel_id=1, source_target_pairs={{0,1},{1,0},{2,3},{3,2},{4,5},{5,4},{6,7},{7,6},{8,9},{9,8},{10,11... | collective-permute-start | bytes 884744 | tf_op jit(solution)/shard_map/ppermute | solution.py:426
  45.1 8.3 %collective-permute-start.16 = (bf16[144,1152]{1,0:T(8,128)(2,1)S(1)}, bf16[144,1152]{1,0:T(8,128)(2,1)S(1)}, u32[]{:S(2)}, u32[]{:S(2)}) collective-permute-start(bf16[144,1152]{1,0:T(8,128)(2,1)S(1)} %shard_map.96), channel_id=1, source_target_pairs={{0,8},{8,0},{16,24},{24,16},{1,9},{9,1},{17,25},{25,17},{2,10},{10... | collective-permute-start | bytes 995336 | tf_op jit(solution)/shard_map/ppermute | solution.py:501
  53.5 9.7 %collective-permute-start.17 = (bf16[144,1152]{1,0:T(8,128)(2,1)S(1)}, bf16[144,1152]{1,0:T(8,128)(2,1)S(1)}, u32[]{:S(2)}, u32[]{:S(2)}) collective-permute-start(bf16[144,1152]{1,0:T(8,128)(2,1)S(1)} %reduce-precision_convert_fusion), channel_id=1, source_target_pairs={{0,16},{8,24},{16,0},{24,8},{1,17},{9,25},{17,1},{25,9},{2,18},{10... | collective-permute-start | bytes 995336 | tf_op jit(solution)/shard_map/ppermute | solution.py:501
  55.1 9.5 %collective-permute-start.10 = (bf16[432,128]{1,0:T(8,128)(2,1)}, bf16[432,128]{1,0:T(8,128)(2,1)S(1)}, u32[]{:S(2)}, u32[]{:S(2)}) collective-permute-start(bf16[432,128]{1,0:T(8,128)(2,1)} %get-tuple-element.40), channel_id=1, source_target_pairs={{0,5},{1,4},{2,7},{3,6},{4,1},{5,0},{6,3},{7,2},{8,13},{9,12},{10,... | collective-permute-start | bytes 331784 | tf_op jit(solution)/shard_map/ppermute | solution.py:509
  55.5 10.0 %collective-permute-start.11 = (bf16[432,128]{1,0:T(8,128)(2,1)}, bf16[432,128]{1,0:T(8,128)(2,1)S(1)}, u32[]{:S(2)}, u32[]{:S(2)}) collective-permute-start(bf16[432,128]{1,0:T(8,128)(2,1)} %get-tuple-element.41), channel_id=1, source_target_pairs={{0,3},{1,2},{2,1},{3,0},{4,7},{5,6},{6,5},{7,4},{8,11},{9,10},{10,... | collective-permute-start | bytes 331784 | tf_op jit(solution)/shard_map/ppermute | solution.py:509
  57.7 8.8 %collective-permute-start.12 = (bf16[432,128]{1,0:T(8,128)(2,1)}, bf16[432,128]{1,0:T(8,128)(2,1)S(1)}, u32[]{:S(2)}, u32[]{:S(2)}) collective-permute-start(bf16[432,128]{1,0:T(8,128)(2,1)} %get-tuple-element.42), channel_id=1, source_target_pairs={{0,4},{1,5},{2,6},{3,7},{4,0},{5,1},{6,2},{7,3},{8,12},{9,13},{10,... | collective-permute-start | bytes 331784 | tf_op jit(solution)/shard_map/ppermute | solution.py:509
  59.2 16.6 %collective-permute-start.13 = (bf16[432,128]{1,0:T(8,128)(2,1)}, bf16[432,128]{1,0:T(8,128)(2,1)S(1)}, u32[]{:S(2)}, u32[]{:S(2)}) collective-permute-start(bf16[432,128]{1,0:T(8,128)(2,1)} %get-tuple-element.43), channel_id=1, source_target_pairs={{0,7},{1,6},{2,5},{3,4},{4,3},{5,2},{6,1},{7,0},{8,15},{9,14},{10,... | collective-permute-start | bytes 331784 | tf_op jit(solution)/shard_map/ppermute | solution.py:509
  63.2 14.8 %collective-permute-start.14 = (bf16[432,128]{1,0:T(8,128)(2,1)}, bf16[432,128]{1,0:T(8,128)(2,1)S(1)}, u32[]{:S(2)}, u32[]{:S(2)}) collective-permute-start(bf16[432,128]{1,0:T(8,128)(2,1)} %get-tuple-element.44), channel_id=1, source_target_pairs={{0,6},{1,7},{2,4},{3,5},{4,2},{5,3},{6,0},{7,1},{8,14},{9,15},{10,... | collective-permute-start | bytes 331784 | tf_op jit(solution)/shard_map/ppermute | solution.py:509
  64.6 13.4 %collective-permute-start.15 = (bf16[432,128]{1,0:T(8,128)(2,1)}, bf16[432,128]{1,0:T(8,128)(2,1)S(1)}, u32[]{:S(2)}, u32[]{:S(2)}) collective-permute-start(bf16[432,128]{1,0:T(8,128)(2,1)} %get-tuple-element.45), channel_id=1, source_target_pairs={{0,2},{1,3},{2,0},{3,1},{4,6},{5,7},{6,4},{7,5},{8,10},{9,11},{10,... | collective-permute-start | bytes 331784 | tf_op jit(solution)/shard_map/ppermute | solution.py:509
  65.5 12.5 %collective-permute-start.18 = (bf16[432,128]{1,0:T(8,128)(2,1)}, bf16[432,128]{1,0:T(8,128)(2,1)S(1)}, u32[]{:S(2)}, u32[]{:S(2)}) collective-permute-start(bf16[432,128]{1,0:T(8,128)(2,1)} %get-tuple-element.50), channel_id=1, source_target_pairs={{0,1},{1,0},{2,3},{3,2},{4,5},{5,4},{6,7},{7,6},{8,9},{9,8},{10,11... | collective-permute-start | bytes 331784 | tf_op jit(solution)/shard_map/ppermute | solution.py:509

commit v6 on v5

--- a/solution.py
+++ b/solution.py
@@ -404,7 +404,7 @@
     return loads
 
 
-BACK_ORDER = (0, 5, 3, 4, 7, 6, 2, 1)
+BACK_ORDER = (0, 5, 3, 4, 7, 2, 6, 1)
 FIFTH_PARTS = 4
 INNER_SOURCES = (0, 2, 6, 4, 3, 1, 7, 5)
 OUTER_SOURCES = (0, 2, 1, 3, 4, 6, 5, 7)

time: 79.5 us -> 79.7 us (level)
  transfers between devices with their start and end apart: 20 -> 20, of which waited for: 11 -> 10; matrix products, arithmetic and copies ran while one was open for 1% -> 1% of each run, Pallas kernels for 17% -> 17%
where the time goes in v6:
time: 79.7 us; the launch traced here: 79.8 us
  waiting for transfers between devices  39.2 us (49%)
  starting transfers between devices  23.3 us (29%)
  Pallas kernels  15.4 us (19%)
  other arithmetic  1.11 us (1%)
    ppermute x10, waiting for transfers between devices, move(): return lax.ppermute(value, 'seq', pairs)  22.8 us
    ppermute x7, waiting for transfers between devices, head_body(): lax.ppermute(block, 'seq', [(i, i ^ n) for i in range(shards)])  12.4 us
    ppermute x10, starting transfers between devices, move(): return lax.ppermute(value, 'seq', pairs)  8.48 us
    pallas_call x1, Pallas kernels, head_body(): pl.pallas_call(functools.partial(forward_kernel, early), out_shape=[shape...  6.16 us
    ppermute x7, starting transfers between devices, head_body(): lax.ppermute(block, 'seq', [(i, i ^ n) for i in range(shards)])  5.56 us
    pallas_call x1, Pallas kernels, head_body(): pl.pallas_call(functools.partial(backward_kernel, early), out_shape=[shap...  5.27 us
    ppermute x2, starting transfers between devices, head_body(): lax.ppermute(w_part, 'dp', pairs)  5.02 us
    all_to_all x1, starting transfers between devices, head_body(): arrived = lax.all_to_all(after(sent, *pieces[1:3]), 'seq', 0, 0, tiled=True)  4.21 us
  transfers between devices with their start and end apart: 20, of which 10 were waited for; matrix products, arithmetic and copies ran while one was open for 1% of the time, Pallas kernels for 17%

profile of v6, /device:TPU:17, one launch (start us, length us, event | category | flops | bytes accessed | tf_op | source)
XLA Modules:
  0.0 79.8 jit_solution(2103532601909004405)
XLA Ops:
  0.6 1.4 %collective-permute-start = (bf16[128,1152]{1,0:T(8,128)(2,1)}, bf16[128,1152]{1,0:T(8,128)(2,1)S(1)}, u32[]{:S(2)}, u32[]{:S(2)}) collective-permute-start(bf16[128,1152]{1,0:T(8,128)(2,1)} %bitcast.7), channel_id=1, source_target_pairs={{0,2},{1,3},{2,0},{3,1},{4,6},{5,7},{6,4},{7,5},{8,10},{9,11},{10,... | collective-permute-start | bytes 884744 | tf_op jit(solution)/shard_map/ppermute | solution.py:426
  2.0 0.0 collective-permute-start.1
  2.0 2.2 %shard_map.93 = bf16[8,432,128]{2,1,0:T(8,128)(2,1)} custom-call(bf16[128,1152]{1,0:T(8,128)(2,1)} %bitcast.10, bf16[128,1152]{1,0:T(8,128)(2,1)} %bitcast.11, bf16[128,1152]{1,0:T(8,128)(2,1)} %bitcast.12), custom_call_target="tpu_custom_call" | custom-call | tf_op jit(solution)/shard_map/pallas_call | solution.py:460
  4.2 4.6 %collective-permute-done.refs_1_ = bf16[128,1152]{1,0:T(8,128)(2,1)S(1)} collective-permute-done((bf16[128,1152]{1,0:T(8,128)(2,1)}, bf16[128,1152]{1,0:T(8,128)(2,1)S(1)}, u32[]{:S(2)}, u32[]{:S(2)}) %collective-permute-start) | collective-permute-done | bytes 294944 | tf_op jit(solution)/shard_map/ppermute | solution.py:426
  8.8 0.0 copy-start.4
  8.8 0.2 collective-permute-start.2
  9.0 0.8 %collective-permute-done.1.refs_2_ = bf16[128,1152]{1,0:T(8,128)(2,1)S(1)} collective-permute-done((bf16[128,1152]{1,0:T(8,128)(2,1)}, bf16[128,1152]{1,0:T(8,128)(2,1)S(1)}, u32[]{:S(2)}, u32[]{:S(2)}) %collective-permute-start.1) | collective-permute-done | bytes 294944 | tf_op jit(solution)/shard_map/ppermute | solution.py:426
  9.8 0.0 copy-start.2
  9.8 1.5 %collective-permute-start.3 = (bf16[128,1152]{1,0:T(8,128)(2,1)S(1)}, bf16[128,1152]{1,0:T(8,128)(2,1)S(1)}, u32[]{:S(2)}, u32[]{:S(2)}) collective-permute-start(bf16[128,1152]{1,0:T(8,128)(2,1)S(1)} %collective-permute-done.1.refs_2_), channel_id=1, source_target_pairs={{0,2},{1,3},{2,0},{3,1},{4,6},{5,7},{6,4},{7,5},{8,10},{9,11},{10,... | collective-permute-start | bytes 884744 | tf_op jit(solution)/shard_map/ppermute | solution.py:426
  11.3 4.2 %all-to-all-start = ((bf16[8,432,128]{2,1,0:T(8,128)(2,1)}), bf16[8,432,128]{2,1,0:T(8,128)(2,1)S(1)}, u32[]{:S(2)}, u32[]{:S(2)}) async-start(bf16[8,432,128]{2,1,0:T(8,128)(2,1)} %shard_map.93), calls=%async_computation | async-start | bytes 1769472 | tf_op jit(solution)/shard_map/all_to_all | solution.py:466
  15.5 0.2 collective-permute-done.2.refs_3_
  15.7 0.0 copy-start
  15.8 1.4 %collective-permute-start.4 = (bf16[32,1152]{1,0:T(8,128)(2,1)S(1)}, bf16[32,1152]{1,0:T(8,128)(2,1)S(1)}, u32[]{:S(2)}, u32[]{:S(2)}) collective-permute-start(bf16[32,1152]{1,0:T(8,128)(2,1)S(1)} %get-tuple-element.57), channel_id=1, source_target_pairs={{0,2},{1,3},{2,0},{3,1},{4,6},{5,7},{6,4},{7,5},{8,10},{9,11},{10,... | collective-permute-start | bytes 221192 | tf_op jit(solution)/shard_map/ppermute | solution.py:426
  17.1 0.2 collective-permute-start.5
  17.3 1.3 %collective-permute-start.6 = (bf16[32,1152]{1,0:T(8,128)(2,1)S(1)}, bf16[32,1152]{1,0:T(8,128)(2,1)S(1)}, u32[]{:S(2)}, u32[]{:S(2)}) collective-permute-start(bf16[32,1152]{1,0:T(8,128)(2,1)S(1)} %get-tuple-element.55), channel_id=1, source_target_pairs={{0,2},{1,3},{2,0},{3,1},{4,6},{5,7},{6,4},{7,5},{8,10},{9,11},{10,... | collective-permute-start | bytes 221192 | tf_op jit(solution)/shard_map/ppermute | solution.py:426
  18.6 0.2 collective-permute-start.7
  18.8 0.0 collective-permute-done.3.refs_4_
  18.8 0.0 copy-start.3
  18.8 1.3 %collective-permute-start.8 = (bf16[128,1152]{1,0:T(8,128)(2,1)S(1)}, bf16[128,1152]{1,0:T(8,128)(2,1)S(1)}, u32[]{:S(2)}, u32[]{:S(2)}) collective-permute-start(bf16[128,1152]{1,0:T(8,128)(2,1)S(1)} %broadcast_select_fusion.1), channel_id=1, source_target_pairs={{0,1},{1,0},{2,3},{3,2},{4,5},{5,4},{6,7},{7,6},{8,9},{9,8},{10,11... | collective-permute-start | bytes 884744 | tf_op jit(solution)/shard_map/ppermute | solution.py:426
  20.1 12.5 %collective-permute-done.4 = bf16[32,1152]{1,0:T(8,128)(2,1)S(1)} collective-permute-done((bf16[32,1152]{1,0:T(8,128)(2,1)S(1)}, bf16[32,1152]{1,0:T(8,128)(2,1)S(1)}, u32[]{:S(2)}, u32[]{:S(2)}) %collective-permute-start.4) | collective-permute-done | bytes 73760 | tf_op jit(solution)/shard_map/ppermute | solution.py:426
  32.5 1.6 %collective-permute-done.5 = bf16[32,1152]{1,0:T(8,128)(2,1)S(1)} collective-permute-done((bf16[32,1152]{1,0:T(8,128)(2,1)S(1)}, bf16[32,1152]{1,0:T(8,128)(2,1)S(1)}, u32[]{:S(2)}, u32[]{:S(2)}) %collective-permute-start.5) | collective-permute-done | bytes 73760 | tf_op jit(solution)/shard_map/ppermute | solution.py:426
  34.1 1.6 %collective-permute-done.6 = bf16[32,1152]{1,0:T(8,128)(2,1)S(1)} collective-permute-done((bf16[32,1152]{1,0:T(8,128)(2,1)S(1)}, bf16[32,1152]{1,0:T(8,128)(2,1)S(1)}, u32[]{:S(2)}, u32[]{:S(2)}) %collective-permute-start.6) | collective-permute-done | bytes 73760 | tf_op jit(solution)/shard_map/ppermute | solution.py:426
  35.7 1.6 %collective-permute-done.7 = bf16[32,1152]{1,0:T(8,128)(2,1)S(1)} collective-permute-done((bf16[32,1152]{1,0:T(8,128)(2,1)S(1)}, bf16[32,1152]{1,0:T(8,128)(2,1)S(1)}, u32[]{:S(2)}, u32[]{:S(2)}) %collective-permute-start.7) | collective-permute-done | bytes 73760 | tf_op jit(solution)/shard_map/ppermute | solution.py:426
  37.3 0.0 copy-start.1
  37.4 1.1 %collective-permute-start.9 = (bf16[128,1152]{1,0:T(8,128)(2,1)S(1)}, bf16[128,1152]{1,0:T(8,128)(2,1)S(1)}, u32[]{:S(2)}, u32[]{:S(2)}) collective-permute-start(bf16[128,1152]{1,0:T(8,128)(2,1)S(1)} %broadcast_select_fusion), channel_id=1, source_target_pairs={{0,1},{1,0},{2,3},{3,2},{4,5},{5,4},{6,7},{7,6},{8,9},{9,8},{10,11... | collective-permute-start | bytes 884744 | tf_op jit(solution)/shard_map/ppermute | solution.py:426
  38.5 0.0 all-to-all-done.in_ref
  38.5 0.0 copy-done.4
  38.5 0.0 copy-done.2
  38.5 0.0 copy-done
  38.5 0.0 copy-done.3
  38.5 0.0 copy-done.1
  38.5 6.2 %shard_map.94 = (bf16[2,80,1024]{2,1,0:T(8,128)(2,1)S(1)}, bf16[2,80,1024]{2,1,0:T(8,128)(2,1)S(1)}, bf16[2,1024,80]{2,1,0:T(8,128)(2,1)S(1)}, bf16[144,1024]{1,...) custom-call(s32[1,4]{1,0:T(1,128)} %len_ref.3, ...), custom_call_target="tpu_custom_call" | custom-call | tf_op jit(solution)/shard_map/pallas_call | solution.py:479
  44.7 0.0 collective-permute-done.8.refs_0_
  44.7 0.0 collective-permute-done.9.refs_1_
  44.7 0.3 shard_map.96
  45.1 3.4 %collective-permute-start.16 = (bf16[144,1152]{1,0:T(8,128)(2,1)S(1)}, bf16[144,1152]{1,0:T(8,128)(2,1)S(1)}, u32[]{:S(2)}, u32[]{:S(2)}) collective-permute-start(bf16[144,1152]{1,0:T(8,128)(2,1)S(1)} %shard_map.96), channel_id=1, source_target_pairs={{0,8},{8,0},{16,24},{24,16},{1,9},{9,1},{17,25},{25,17},{2,10},{10... | collective-permute-start | bytes 995336 | tf_op jit(solution)/shard_map/ppermute | solution.py:501
  48.5 5.3 %shard_map.95 = (bf16[432,128]{1,0:T(8,128)(2,1)S(1)}, bf16[432,128]{1,0:T(8,128)(2,1)}, bf16[432,128]{1,0:T(8,128)(2,1)}, bf16[432,128]{1,0:T(8,128)(2,1)}, bf1...) custom-call(s32[1,4]{1,0:T(1,128)} %len_ref.3, ...), custom_call_target="tpu_custom_call" | custom-call | tf_op jit(solution)/shard_map/pallas_call | solution.py:490
  53.7 0.0 collective-permute-done.16
  53.7 0.1 reduce-precision_convert_fusion
  53.8 1.6 %collective-permute-start.17 = (bf16[144,1152]{1,0:T(8,128)(2,1)S(1)}, bf16[144,1152]{1,0:T(8,128)(2,1)S(1)}, u32[]{:S(2)}, u32[]{:S(2)}) collective-permute-start(bf16[144,1152]{1,0:T(8,128)(2,1)S(1)} %reduce-precision_convert_fusion), channel_id=1, source_target_pairs={{0,16},{8,24},{16,0},{24,8},{1,17},{9,25},{17,1},{25,9},{2,18},{10... | collective-permute-start | bytes 995336 | tf_op jit(solution)/shard_map/ppermute | solution.py:501
  55.5 0.2 collective-permute-start.10
  55.7 2.4 %collective-permute-start.11 = (bf16[432,128]{1,0:T(8,128)(2,1)}, bf16[432,128]{1,0:T(8,128)(2,1)S(1)}, u32[]{:S(2)}, u32[]{:S(2)}) collective-permute-start(bf16[432,128]{1,0:T(8,128)(2,1)} %get-tuple-element.41), channel_id=1, source_target_pairs={{0,3},{1,2},{2,1},{3,0},{4,7},{5,6},{6,5},{7,4},{8,11},{9,10},{10,... | collective-permute-start | bytes 331784 | tf_op jit(solution)/shard_map/ppermute | solution.py:509
  58.1 1.2 %collective-permute-start.12 = (bf16[432,128]{1,0:T(8,128)(2,1)}, bf16[432,128]{1,0:T(8,128)(2,1)S(1)}, u32[]{:S(2)}, u32[]{:S(2)}) collective-permute-start(bf16[432,128]{1,0:T(8,128)(2,1)} %get-tuple-element.42), channel_id=1, source_target_pairs={{0,4},{1,5},{2,6},{3,7},{4,0},{5,1},{6,2},{7,3},{8,12},{9,13},{10,... | collective-permute-start | bytes 331784 | tf_op jit(solution)/shard_map/ppermute | solution.py:509
  59.2 0.0 collective-permute-start.13
  59.2 3.9 %collective-permute-done.17 = bf16[144,1152]{1,0:T(8,128)(2,1)S(1)} collective-permute-done((bf16[144,1152]{1,0:T(8,128)(2,1)S(1)}, bf16[144,1152]{1,0:T(8,128)(2,1)S(1)}, u32[]{:S(2)}, u32[]{:S(2)}) %collective-permute-start.17) | collective-permute-done | bytes 331808 | tf_op jit(solution)/shard_map/ppermute | solution.py:501
  63.2 0.5 collective-permute-start.14
  63.7 0.9 %add_multiply_fusion = f32[144,1152]{1,0:T(8,128)} fusion(bf16[144,1152]{1,0:T(8,128)(2,1)S(1)} %collective-permute-done.17, bf16[144,1152]{1,0:T(8,128)(2,1)S(1)} %reduce-precision_convert_fusion), kind=kLoop, calls=%fused_computation | loop fusion | flops 663552 | bytes 1327104 | tf_op jit(solution)/shard_map/mul | solution.py:504
  64.6 0.0 collective-permute-done.10.refs_1_
  64.6 0.0 collective-permute-start.15
  64.6 0.0 collective-permute-done.11.refs_2_
  64.6 1.3 %collective-permute-start.18 = (bf16[432,128]{1,0:T(8,128)(2,1)}, bf16[432,128]{1,0:T(8,128)(2,1)S(1)}, u32[]{:S(2)}, u32[]{:S(2)}) collective-permute-start(bf16[432,128]{1,0:T(8,128)(2,1)} %get-tuple-element.50), channel_id=1, source_target_pairs={{0,1},{1,0},{2,3},{3,2},{4,5},{5,4},{6,7},{7,6},{8,9},{9,8},{10,11... | collective-permute-start | bytes 331784 | tf_op jit(solution)/shard_map/ppermute | solution.py:509
  65.9 0.0 collective-permute-done.12.refs_3_
  65.9 9.5 %collective-permute-done.13.refs_4_ = bf16[432,128]{1,0:T(8,128)(2,1)S(1)} collective-permute-done((bf16[432,128]{1,0:T(8,128)(2,1)}, bf16[432,128]{1,0:T(8,128)(2,1)S(1)}, u32[]{:S(2)}, u32[]{:S(2)}) %collective-permute-start.13) | collective-permute-done | bytes 110624 | tf_op jit(solution)/shard_map/ppermute | solution.py:509
  75.4 0.0 collective-permute-done.14.refs_5_
  75.4 2.9 %collective-permute-done.15.refs_6_ = bf16[432,128]{1,0:T(8,128)(2,1)S(1)} collective-permute-done((bf16[432,128]{1,0:T(8,128)(2,1)}, bf16[432,128]{1,0:T(8,128)(2,1)S(1)}, u32[]{:S(2)}, u32[]{:S(2)}) %collective-permute-start.15) | collective-permute-done | bytes 110624 | tf_op jit(solution)/shard_map/ppermute | solution.py:509
  78.3 0.0 collective-permute-done.18.refs_7_
  78.3 1.5 %shard_map.97 = (f32[128,1152]{1,0:T(8,128)}, f32[128,1152]{1,0:T(8,128)}, f32[128,1152]{1,0:T(8,128)}) custom-call(bf16[432,128]{1,0:T(8,128)(2,1)S(1)} %get-tuple-element.39.refs_0_, bf16[432,128]{1,0:T(8,128)(2,1)S(1)} %collective-permute-done.10.refs_1_, bf16[432,128]{1,0:T(8,128)(2,1)S(1)} %collective-permute-done.11.refs_2_, ...), custom_call_target="tpu_custom_call" | custom-call | tf_op jit(solution)/shard_map/pallas_call | solution.py:511
  (7 shorter events, 0.1 us)
Async XLA Ops:
  0.6 8.2 %collective-permute-start = (bf16[128,1152]{1,0:T(8,128)(2,1)}, bf16[128,1152]{1,0:T(8,128)(2,1)S(1)}, u32[]{:S(2)}, u32[]{:S(2)}) collective-permute-start(bf16[128,1152]{1,0:T(8,128)(2,1)} %bitcast.7), channel_id=1, source_target_pairs={{0,2},{1,3},{2,0},{3,1},{4,6},{5,7},{6,4},{7,5},{8,10},{9,11},{10,... | collective-permute-start | bytes 884744 | tf_op jit(solution)/shard_map/ppermute | solution.py:426
  2.0 7.8 %collective-permute-start.1 = (bf16[128,1152]{1,0:T(8,128)(2,1)}, bf16[128,1152]{1,0:T(8,128)(2,1)S(1)}, u32[]{:S(2)}, u32[]{:S(2)}) collective-permute-start(bf16[128,1152]{1,0:T(8,128)(2,1)} %bitcast.8), channel_id=1, source_target_pairs={{0,1},{1,0},{2,4},{3,5},{4,2},{5,3},{6,7},{7,6},{8,9},{9,8},{10,12... | collective-permute-start | bytes 884744 | tf_op jit(solution)/shard_map/ppermute | solution.py:426
  8.8 29.7 %copy-start.4 = (bf16[128,1152]{1,0:T(8,128)(2,1)}, bf16[128,1152]{1,0:T(8,128)(2,1)S(1)}, u32[]{:S(2)}) copy-start(bf16[128,1152]{1,0:T(8,128)(2,1)S(1)} %collective-permute-done.refs_1_) | copy-start | bytes 884740
  8.8 7.0 %collective-permute-start.2 = (bf16[128,1152]{1,0:T(8,128)(2,1)S(1)}, bf16[128,1152]{1,0:T(8,128)(2,1)S(1)}, u32[]{:S(2)}, u32[]{:S(2)}) collective-permute-start(bf16[128,1152]{1,0:T(8,128)(2,1)S(1)} %collective-permute-done.refs_1_), channel_id=1, source_target_pairs={{0,1},{1,0},{2,4},{3,5},{4,2},{5,3},{6,7},{7,6},{8,9},{9,8},{10,12... | collective-permute-start | bytes 884744 | tf_op jit(solution)/shard_map/ppermute | solution.py:426
  9.8 28.7 %copy-start.2 = (bf16[128,1152]{1,0:T(8,128)(2,1)}, bf16[128,1152]{1,0:T(8,128)(2,1)S(1)}, u32[]{:S(2)}) copy-start(bf16[128,1152]{1,0:T(8,128)(2,1)S(1)} %collective-permute-done.1.refs_2_) | copy-start | bytes 884740
  9.8 9.0 %collective-permute-start.3 = (bf16[128,1152]{1,0:T(8,128)(2,1)S(1)}, bf16[128,1152]{1,0:T(8,128)(2,1)S(1)}, u32[]{:S(2)}, u32[]{:S(2)}) collective-permute-start(bf16[128,1152]{1,0:T(8,128)(2,1)S(1)} %collective-permute-done.1.refs_2_), channel_id=1, source_target_pairs={{0,2},{1,3},{2,0},{3,1},{4,6},{5,7},{6,4},{7,5},{8,10},{9,11},{10,... | collective-permute-start | bytes 884744 | tf_op jit(solution)/shard_map/ppermute | solution.py:426
  11.3 27.2 %all-to-all-start = ((bf16[8,432,128]{2,1,0:T(8,128)(2,1)}), bf16[8,432,128]{2,1,0:T(8,128)(2,1)S(1)}, u32[]{:S(2)}, u32[]{:S(2)}) async-start(bf16[8,432,128]{2,1,0:T(8,128)(2,1)} %shard_map.93), calls=%async_computation | async-start | bytes 1769472 | tf_op jit(solution)/shard_map/all_to_all | solution.py:466
  15.7 22.8 %copy-start = (bf16[128,1152]{1,0:T(8,128)(2,1)}, bf16[128,1152]{1,0:T(8,128)(2,1)S(1)}, u32[]{:S(2)}) copy-start(bf16[128,1152]{1,0:T(8,128)(2,1)S(1)} %collective-permute-done.2.refs_3_) | copy-start | bytes 884740
  15.8 16.8 %collective-permute-start.4 = (bf16[32,1152]{1,0:T(8,128)(2,1)S(1)}, bf16[32,1152]{1,0:T(8,128)(2,1)S(1)}, u32[]{:S(2)}, u32[]{:S(2)}) collective-permute-start(bf16[32,1152]{1,0:T(8,128)(2,1)S(1)} %get-tuple-element.57), channel_id=1, source_target_pairs={{0,2},{1,3},{2,0},{3,1},{4,6},{5,7},{6,4},{7,5},{8,10},{9,11},{10,... | collective-permute-start | bytes 221192 | tf_op jit(solution)/shard_map/ppermute | solution.py:426
  17.1 17.0 %collective-permute-start.5 = (bf16[32,1152]{1,0:T(8,128)(2,1)S(1)}, bf16[32,1152]{1,0:T(8,128)(2,1)S(1)}, u32[]{:S(2)}, u32[]{:S(2)}) collective-permute-start(bf16[32,1152]{1,0:T(8,128)(2,1)S(1)} %get-tuple-element.56), channel_id=1, source_target_pairs={{0,2},{1,3},{2,0},{3,1},{4,6},{5,7},{6,4},{7,5},{8,10},{9,11},{10,... | collective-permute-start | bytes 221192 | tf_op jit(solution)/shard_map/ppermute | solution.py:426
  17.3 18.4 %collective-permute-start.6 = (bf16[32,1152]{1,0:T(8,128)(2,1)S(1)}, bf16[32,1152]{1,0:T(8,128)(2,1)S(1)}, u32[]{:S(2)}, u32[]{:S(2)}) collective-permute-start(bf16[32,1152]{1,0:T(8,128)(2,1)S(1)} %get-tuple-element.55), channel_id=1, source_target_pairs={{0,2},{1,3},{2,0},{3,1},{4,6},{5,7},{6,4},{7,5},{8,10},{9,11},{10,... | collective-permute-start | bytes 221192 | tf_op jit(solution)/shard_map/ppermute | solution.py:426
  18.6 18.7 %collective-permute-start.7 = (bf16[32,1152]{1,0:T(8,128)(2,1)S(1)}, bf16[32,1152]{1,0:T(8,128)(2,1)S(1)}, u32[]{:S(2)}, u32[]{:S(2)}) collective-permute-start(bf16[32,1152]{1,0:T(8,128)(2,1)S(1)} %get-tuple-element.54), channel_id=1, source_target_pairs={{0,2},{1,3},{2,0},{3,1},{4,6},{5,7},{6,4},{7,5},{8,10},{9,11},{10,... | collective-permute-start | bytes 221192 | tf_op jit(solution)/shard_map/ppermute | solution.py:426
  18.8 19.7 %copy-start.3 = (bf16[128,1152]{1,0:T(8,128)(2,1)}, bf16[128,1152]{1,0:T(8,128)(2,1)S(1)}, u32[]{:S(2)}) copy-start(bf16[128,1152]{1,0:T(8,128)(2,1)S(1)} %collective-permute-done.3.refs_4_) | copy-start | bytes 884740
  18.8 25.9 %collective-permute-start.8 = (bf16[128,1152]{1,0:T(8,128)(2,1)S(1)}, bf16[128,1152]{1,0:T(8,128)(2,1)S(1)}, u32[]{:S(2)}, u32[]{:S(2)}) collective-permute-start(bf16[128,1152]{1,0:T(8,128)(2,1)S(1)} %broadcast_select_fusion.1), channel_id=1, source_target_pairs={{0,1},{1,0},{2,3},{3,2},{4,5},{5,4},{6,7},{7,6},{8,9},{9,8},{10,11... | collective-permute-start | bytes 884744 | tf_op jit(solution)/shard_map/ppermute | solution.py:426
  37.3 1.2 %copy-start.1 = (bf16[128,1152]{1,0:T(8,128)(2,1)}, bf16[128,1152]{1,0:T(8,128)(2,1)S(1)}, u32[]{:S(2)}) copy-start(bf16[128,1152]{1,0:T(8,128)(2,1)S(1)} %constant_dynamic-update-slice_fusion.refs_5_) | copy-start | bytes 884740
  37.4 7.4 %collective-permute-start.9 = (bf16[128,1152]{1,0:T(8,128)(2,1)S(1)}, bf16[128,1152]{1,0:T(8,128)(2,1)S(1)}, u32[]{:S(2)}, u32[]{:S(2)}) collective-permute-start(bf16[128,1152]{1,0:T(8,128)(2,1)S(1)} %broadcast_select_fusion), channel_id=1, source_target_pairs={{0,1},{1,0},{2,3},{3,2},{4,5},{5,4},{6,7},{7,6},{8,9},{9,8},{10,11... | collective-permute-start | bytes 884744 | tf_op jit(solution)/shard_map/ppermute | solution.py:426
  45.1 8.7 %collective-permute-start.16 = (bf16[144,1152]{1,0:T(8,128)(2,1)S(1)}, bf16[144,1152]{1,0:T(8,128)(2,1)S(1)}, u32[]{:S(2)}, u32[]{:S(2)}) collective-permute-start(bf16[144,1152]{1,0:T(8,128)(2,1)S(1)} %shard_map.96), channel_id=1, source_target_pairs={{0,8},{8,0},{16,24},{24,16},{1,9},{9,1},{17,25},{25,17},{2,10},{10... | collective-permute-start | bytes 995336 | tf_op jit(solution)/shard_map/ppermute | solution.py:501
  53.8 9.3 %collective-permute-start.17 = (bf16[144,1152]{1,0:T(8,128)(2,1)S(1)}, bf16[144,1152]{1,0:T(8,128)(2,1)S(1)}, u32[]{:S(2)}, u32[]{:S(2)}) collective-permute-start(bf16[144,1152]{1,0:T(8,128)(2,1)S(1)} %reduce-precision_convert_fusion), channel_id=1, source_target_pairs={{0,16},{8,24},{16,0},{24,8},{1,17},{9,25},{17,1},{25,9},{2,18},{10... | collective-permute-start | bytes 995336 | tf_op jit(solution)/shard_map/ppermute | solution.py:501
  55.5 9.1 %collective-permute-start.10 = (bf16[432,128]{1,0:T(8,128)(2,1)}, bf16[432,128]{1,0:T(8,128)(2,1)S(1)}, u32[]{:S(2)}, u32[]{:S(2)}) collective-permute-start(bf16[432,128]{1,0:T(8,128)(2,1)} %get-tuple-element.40), channel_id=1, source_target_pairs={{0,5},{1,4},{2,7},{3,6},{4,1},{5,0},{6,3},{7,2},{8,13},{9,12},{10,... | collective-permute-start | bytes 331784 | tf_op jit(solution)/shard_map/ppermute | solution.py:509
  55.7 9.0 %collective-permute-start.11 = (bf16[432,128]{1,0:T(8,128)(2,1)}, bf16[432,128]{1,0:T(8,128)(2,1)S(1)}, u32[]{:S(2)}, u32[]{:S(2)}) collective-permute-start(bf16[432,128]{1,0:T(8,128)(2,1)} %get-tuple-element.41), channel_id=1, source_target_pairs={{0,3},{1,2},{2,1},{3,0},{4,7},{5,6},{6,5},{7,4},{8,11},{9,10},{10,... | collective-permute-start | bytes 331784 | tf_op jit(solution)/shard_map/ppermute | solution.py:509
  58.1 7.9 %collective-permute-start.12 = (bf16[432,128]{1,0:T(8,128)(2,1)}, bf16[432,128]{1,0:T(8,128)(2,1)S(1)}, u32[]{:S(2)}, u32[]{:S(2)}) collective-permute-start(bf16[432,128]{1,0:T(8,128)(2,1)} %get-tuple-element.42), channel_id=1, source_target_pairs={{0,4},{1,5},{2,6},{3,7},{4,0},{5,1},{6,2},{7,3},{8,12},{9,13},{10,... | collective-permute-start | bytes 331784 | tf_op jit(solution)/shard_map/ppermute | solution.py:509
  59.2 16.2 %collective-permute-start.13 = (bf16[432,128]{1,0:T(8,128)(2,1)}, bf16[432,128]{1,0:T(8,128)(2,1)S(1)}, u32[]{:S(2)}, u32[]{:S(2)}) collective-permute-start(bf16[432,128]{1,0:T(8,128)(2,1)} %get-tuple-element.43), channel_id=1, source_target_pairs={{0,7},{1,6},{2,5},{3,4},{4,3},{5,2},{6,1},{7,0},{8,15},{9,14},{10,... | collective-permute-start | bytes 331784 | tf_op jit(solution)/shard_map/ppermute | solution.py:509
  63.2 12.3 %collective-permute-start.14 = (bf16[432,128]{1,0:T(8,128)(2,1)}, bf16[432,128]{1,0:T(8,128)(2,1)S(1)}, u32[]{:S(2)}, u32[]{:S(2)}) collective-permute-start(bf16[432,128]{1,0:T(8,128)(2,1)} %get-tuple-element.44), channel_id=1, source_target_pairs={{0,2},{1,3},{2,0},{3,1},{4,6},{5,7},{6,4},{7,5},{8,10},{9,11},{10,... | collective-permute-start | bytes 331784 | tf_op jit(solution)/shard_map/ppermute | solution.py:509
  64.6 13.7 %collective-permute-start.15 = (bf16[432,128]{1,0:T(8,128)(2,1)}, bf16[432,128]{1,0:T(8,128)(2,1)S(1)}, u32[]{:S(2)}, u32[]{:S(2)}) collective-permute-start(bf16[432,128]{1,0:T(8,128)(2,1)} %get-tuple-element.45), channel_id=1, source_target_pairs={{0,6},{1,7},{2,4},{3,5},{4,2},{5,3},{6,0},{7,1},{8,14},{9,15},{10,... | collective-permute-start | bytes 331784 | tf_op jit(solution)/shard_map/ppermute | solution.py:509
  64.6 13.7 %collective-permute-start.18 = (bf16[432,128]{1,0:T(8,128)(2,1)}, bf16[432,128]{1,0:T(8,128)(2,1)S(1)}, u32[]{:S(2)}, u32[]{:S(2)}) collective-permute-start(bf16[432,128]{1,0:T(8,128)(2,1)} %get-tuple-element.50), channel_id=1, source_target_pairs={{0,1},{1,0},{2,3},{3,2},{4,5},{5,4},{6,7},{7,6},{8,9},{9,8},{10,11... | collective-permute-start | bytes 331784 | tf_op jit(solution)/shard_map/ppermute | solution.py:509

commit v7 on v5

--- a/solution.py
+++ b/solution.py
@@ -498,7 +498,7 @@
     step = 1
     while step < groups:
         pairs = [(i, i ^ step) for i in range(groups)]
-        sums = w_part.astype(F32) + after(lax.ppermute(w_part, "dp", pairs), grads[0]).astype(F32)
+        sums = w_part.astype(F32) + lax.ppermute(w_part, "dp", pairs).astype(F32)
         w_part = lax.reduce_precision(sums, 8, 7).astype(BF16)
         step *= 2
     weight_grad = sums * (1.0 / math.sqrt(tokens * groups))

time: 79.5 us -> 80.9 us (1.018)
  starting transfers between devices: 23.5 us -> 27.1 us
  waiting for transfers between devices: 38.7 us -> 35.6 us
    ppermute x7, starting transfers between devices: 6.11 us -> 10.5 us  [head_body(): lax.ppermute(block, 'seq', [(i, i ^ n) for i in range(shards)])]
    ppermute x2, waiting for transfers between devices: 4.01 us -> 1.26 us  [head_body(): sums = w_part.astype(F32) + lax.ppermute(w_part, 'dp', pairs).astype(F32)]
  transfers between devices with their start and end apart: 20 -> 20, of which waited for: 11 -> 10; matrix products, arithmetic and copies ran while one was open for 1% -> 1% of each run, Pallas kernels for 17% -> 18%
where the time goes in v7:
time: 80.9 us; the launch traced here: 80.7 us
  waiting for transfers between devices  35.6 us (44%)
  starting transfers between devices  27.1 us (33%)
  Pallas kernels  16.1 us (20%)
  other arithmetic  1.09 us (1%)
    ppermute x10, waiting for transfers between devices, move(): return lax.ppermute(value, 'seq', pairs)  22.8 us
    ppermute x7, waiting for transfers between devices, head_body(): lax.ppermute(block, 'seq', [(i, i ^ n) for i in range(shards)])  11.5 us
    ppermute x7, starting transfers between devices, head_body(): lax.ppermute(block, 'seq', [(i, i ^ n) for i in range(shards)])  10.5 us
    ppermute x10, starting transfers between devices, move(): return lax.ppermute(value, 'seq', pairs)  8.48 us
    pallas_call x1, Pallas kernels, head_body(): pl.pallas_call(functools.partial(forward_kernel, early), out_shape=[shape...  6.55 us
    pallas_call x1, Pallas kernels, head_body(): pl.pallas_call(functools.partial(backward_kernel, early), out_shape=[shap...  5.6 us
    all_to_all x1, starting transfers between devices, head_body(): arrived = lax.all_to_all(after(sent, *pieces[1:3]), 'seq', 0, 0, tiled=True)  4.21 us
    ppermute x2, starting transfers between devices, head_body(): sums = w_part.astype(F32) + lax.ppermute(w_part, 'dp', pairs).astype(F32)  3.93 us
  transfers between devices with their start and end apart: 20, of which 10 were waited for; matrix products, arithmetic and copies ran while one was open for 1% of the time, Pallas kernels for 18%

profile of v7, /device:TPU:17, one launch (start us, length us, event | category | flops | bytes accessed | tf_op | source)
XLA Modules:
  0.0 80.7 jit_solution(10822532117020840136)
XLA Ops:
  0.6 1.4 %collective-permute-start = (bf16[128,1152]{1,0:T(8,128)(2,1)}, bf16[128,1152]{1,0:T(8,128)(2,1)S(1)}, u32[]{:S(2)}, u32[]{:S(2)}) collective-permute-start(bf16[128,1152]{1,0:T(8,128)(2,1)} %bitcast.7), channel_id=1, source_target_pairs={{0,2},{1,3},{2,0},{3,1},{4,6},{5,7},{6,4},{7,5},{8,10},{9,11},{10,... | collective-permute-start | bytes 884744 | tf_op jit(solution)/shard_map/ppermute | solution.py:426
  2.0 0.0 collective-permute-start.1
  2.0 2.2 %shard_map.93 = bf16[8,432,128]{2,1,0:T(8,128)(2,1)} custom-call(bf16[128,1152]{1,0:T(8,128)(2,1)} %bitcast.10, bf16[128,1152]{1,0:T(8,128)(2,1)} %bitcast.11, bf16[128,1152]{1,0:T(8,128)(2,1)} %bitcast.12), custom_call_target="tpu_custom_call" | custom-call | tf_op jit(solution)/shard_map/pallas_call | solution.py:460
  4.2 4.6 %collective-permute-done.refs_1_ = bf16[128,1152]{1,0:T(8,128)(2,1)S(1)} collective-permute-done((bf16[128,1152]{1,0:T(8,128)(2,1)}, bf16[128,1152]{1,0:T(8,128)(2,1)S(1)}, u32[]{:S(2)}, u32[]{:S(2)}) %collective-permute-start) | collective-permute-done | bytes 294944 | tf_op jit(solution)/shard_map/ppermute | solution.py:426
  8.8 0.0 copy-start.4
  8.8 0.2 collective-permute-start.2
  9.0 0.8 collective-permute-done.1.refs_2_
  9.8 0.0 copy-start.2
  9.8 1.5 %collective-permute-start.3 = (bf16[128,1152]{1,0:T(8,128)(2,1)S(1)}, bf16[128,1152]{1,0:T(8,128)(2,1)S(1)}, u32[]{:S(2)}, u32[]{:S(2)}) collective-permute-start(bf16[128,1152]{1,0:T(8,128)(2,1)S(1)} %collective-permute-done.1.refs_2_), channel_id=1, source_target_pairs={{0,2},{1,3},{2,0},{3,1},{4,6},{5,7},{6,4},{7,5},{8,10},{9,11},{10,... | collective-permute-start | bytes 884744 | tf_op jit(solution)/shard_map/ppermute | solution.py:426
  11.3 4.2 %all-to-all-start = ((bf16[8,432,128]{2,1,0:T(8,128)(2,1)}), bf16[8,432,128]{2,1,0:T(8,128)(2,1)S(1)}, u32[]{:S(2)}, u32[]{:S(2)}) async-start(bf16[8,432,128]{2,1,0:T(8,128)(2,1)} %shard_map.93), calls=%async_computation | async-start | bytes 1769472 | tf_op jit(solution)/shard_map/all_to_all | solution.py:466
  15.5 0.2 collective-permute-done.2.refs_3_
  15.7 0.0 copy-start
  15.8 1.4 %collective-permute-start.4 = (bf16[32,1152]{1,0:T(8,128)(2,1)S(1)}, bf16[32,1152]{1,0:T(8,128)(2,1)S(1)}, u32[]{:S(2)}, u32[]{:S(2)}) collective-permute-start(bf16[32,1152]{1,0:T(8,128)(2,1)S(1)} %get-tuple-element.53), channel_id=1, source_target_pairs={{0,2},{1,3},{2,0},{3,1},{4,6},{5,7},{6,4},{7,5},{8,10},{9,11},{10,... | collective-permute-start | bytes 221192 | tf_op jit(solution)/shard_map/ppermute | solution.py:426
  17.1 0.2 collective-permute-start.5
  17.3 1.3 %collective-permute-start.6 = (bf16[32,1152]{1,0:T(8,128)(2,1)S(1)}, bf16[32,1152]{1,0:T(8,128)(2,1)S(1)}, u32[]{:S(2)}, u32[]{:S(2)}) collective-permute-start(bf16[32,1152]{1,0:T(8,128)(2,1)S(1)} %get-tuple-element.51), channel_id=1, source_target_pairs={{0,2},{1,3},{2,0},{3,1},{4,6},{5,7},{6,4},{7,5},{8,10},{9,11},{10,... | collective-permute-start | bytes 221192 | tf_op jit(solution)/shard_map/ppermute | solution.py:426
  18.6 0.2 collective-permute-start.7
  18.8 0.0 collective-permute-done.3.refs_4_
  18.8 0.0 copy-start.3
  18.8 1.3 %collective-permute-start.8 = (bf16[128,1152]{1,0:T(8,128)(2,1)S(1)}, bf16[128,1152]{1,0:T(8,128)(2,1)S(1)}, u32[]{:S(2)}, u32[]{:S(2)}) collective-permute-start(bf16[128,1152]{1,0:T(8,128)(2,1)S(1)} %broadcast_select_fusion.1), channel_id=1, source_target_pairs={{0,1},{1,0},{2,3},{3,2},{4,5},{5,4},{6,7},{7,6},{8,9},{9,8},{10,11... | collective-permute-start | bytes 884744 | tf_op jit(solution)/shard_map/ppermute | solution.py:426
  20.1 12.5 %collective-permute-done.4 = bf16[32,1152]{1,0:T(8,128)(2,1)S(1)} collective-permute-done((bf16[32,1152]{1,0:T(8,128)(2,1)S(1)}, bf16[32,1152]{1,0:T(8,128)(2,1)S(1)}, u32[]{:S(2)}, u32[]{:S(2)}) %collective-permute-start.4) | collective-permute-done | bytes 73760 | tf_op jit(solution)/shard_map/ppermute | solution.py:426
  32.5 1.6 %collective-permute-done.5 = bf16[32,1152]{1,0:T(8,128)(2,1)S(1)} collective-permute-done((bf16[32,1152]{1,0:T(8,128)(2,1)S(1)}, bf16[32,1152]{1,0:T(8,128)(2,1)S(1)}, u32[]{:S(2)}, u32[]{:S(2)}) %collective-permute-start.5) | collective-permute-done | bytes 73760 | tf_op jit(solution)/shard_map/ppermute | solution.py:426
  34.1 1.6 %collective-permute-done.6 = bf16[32,1152]{1,0:T(8,128)(2,1)S(1)} collective-permute-done((bf16[32,1152]{1,0:T(8,128)(2,1)S(1)}, bf16[32,1152]{1,0:T(8,128)(2,1)S(1)}, u32[]{:S(2)}, u32[]{:S(2)}) %collective-permute-start.6) | collective-permute-done | bytes 73760 | tf_op jit(solution)/shard_map/ppermute | solution.py:426
  35.7 1.6 %collective-permute-done.7 = bf16[32,1152]{1,0:T(8,128)(2,1)S(1)} collective-permute-done((bf16[32,1152]{1,0:T(8,128)(2,1)S(1)}, bf16[32,1152]{1,0:T(8,128)(2,1)S(1)}, u32[]{:S(2)}, u32[]{:S(2)}) %collective-permute-start.7) | collective-permute-done | bytes 73760 | tf_op jit(solution)/shard_map/ppermute | solution.py:426
  37.3 0.0 copy-start.1
  37.4 1.1 %collective-permute-start.9 = (bf16[128,1152]{1,0:T(8,128)(2,1)S(1)}, bf16[128,1152]{1,0:T(8,128)(2,1)S(1)}, u32[]{:S(2)}, u32[]{:S(2)}) collective-permute-start(bf16[128,1152]{1,0:T(8,128)(2,1)S(1)} %broadcast_select_fusion), channel_id=1, source_target_pairs={{0,1},{1,0},{2,3},{3,2},{4,5},{5,4},{6,7},{7,6},{8,9},{9,8},{10,11... | collective-permute-start | bytes 884744 | tf_op jit(solution)/shard_map/ppermute | solution.py:426
  38.5 0.0 all-to-all-done.in_ref
  38.5 0.0 copy-done.4
  38.5 0.0 copy-done.2
  38.5 0.0 copy-done
  38.5 0.0 copy-done.3
  38.5 0.0 copy-done.1
  38.5 6.5 %shard_map.94 = (bf16[2,80,1024]{2,1,0:T(8,128)(2,1)S(1)}, bf16[2,80,1024]{2,1,0:T(8,128)(2,1)S(1)}, bf16[2,1024,80]{2,1,0:T(8,128)(2,1)S(1)}, bf16[144,1024]{1,...) custom-call(s32[1,4]{1,0:T(1,128)} %len_ref.3, ...), custom_call_target="tpu_custom_call" | custom-call | tf_op jit(solution)/shard_map/pallas_call | solution.py:479
  45.1 0.0 collective-permute-done.8.refs_0_
  45.1 0.0 collective-permute-done.9.refs_1_
  45.1 0.3 shard_map.96
  45.5 2.6 %collective-permute-start.16 = (bf16[144,1152]{1,0:T(8,128)(2,1)S(1)}, bf16[144,1152]{1,0:T(8,128)(2,1)S(1)}, u32[]{:S(2)}, u32[]{:S(2)}) collective-permute-start(bf16[144,1152]{1,0:T(8,128)(2,1)S(1)} %shard_map.96), channel_id=1, source_target_pairs={{0,8},{8,0},{16,24},{24,16},{1,9},{9,1},{17,25},{25,17},{2,10},{10... | collective-permute-start | bytes 995336 | tf_op jit(solution)/shard_map/ppermute | solution.py:501
  48.1 1.3 %collective-permute-done.16 = bf16[144,1152]{1,0:T(8,128)(2,1)S(1)} collective-permute-done((bf16[144,1152]{1,0:T(8,128)(2,1)S(1)}, bf16[144,1152]{1,0:T(8,128)(2,1)S(1)}, u32[]{:S(2)}, u32[]{:S(2)}) %collective-permute-start.16) | collective-permute-done | bytes 331808 | tf_op jit(solution)/shard_map/ppermute | solution.py:501
  49.3 0.1 reduce-precision_convert_fusion
  49.4 1.3 %collective-permute-start.17 = (bf16[144,1152]{1,0:T(8,128)(2,1)S(1)}, bf16[144,1152]{1,0:T(8,128)(2,1)S(1)}, u32[]{:S(2)}, u32[]{:S(2)}) collective-permute-start(bf16[144,1152]{1,0:T(8,128)(2,1)S(1)} %reduce-precision_convert_fusion), channel_id=1, source_target_pairs={{0,16},{8,24},{16,0},{24,8},{1,17},{9,25},{17,1},{25,9},{2,18},{10... | collective-permute-start | bytes 995336 | tf_op jit(solution)/shard_map/ppermute | solution.py:501
  50.7 5.6 %shard_map.95 = (bf16[432,128]{1,0:T(8,128)(2,1)S(1)}, bf16[432,128]{1,0:T(8,128)(2,1)}, bf16[432,128]{1,0:T(8,128)(2,1)}, bf16[432,128]{1,0:T(8,128)(2,1)}, bf1...) custom-call(s32[1,4]{1,0:T(1,128)} %len_ref.3, ...), custom_call_target="tpu_custom_call" | custom-call | tf_op jit(solution)/shard_map/pallas_call | solution.py:490
  56.4 0.4 collective-permute-start.10
  56.8 2.2 %collective-permute-start.11 = (bf16[432,128]{1,0:T(8,128)(2,1)}, bf16[432,128]{1,0:T(8,128)(2,1)S(1)}, u32[]{:S(2)}, u32[]{:S(2)}) collective-permute-start(bf16[432,128]{1,0:T(8,128)(2,1)} %get-tuple-element.39), channel_id=1, source_target_pairs={{0,3},{1,2},{2,1},{3,0},{4,7},{5,6},{6,5},{7,4},{8,11},{9,10},{10,... | collective-permute-start | bytes 331784 | tf_op jit(solution)/shard_map/ppermute | solution.py:509
  59.0 1.5 %collective-permute-start.12 = (bf16[432,128]{1,0:T(8,128)(2,1)}, bf16[432,128]{1,0:T(8,128)(2,1)S(1)}, u32[]{:S(2)}, u32[]{:S(2)}) collective-permute-start(bf16[432,128]{1,0:T(8,128)(2,1)} %get-tuple-element.40), channel_id=1, source_target_pairs={{0,4},{1,5},{2,6},{3,7},{4,0},{5,1},{6,2},{7,3},{8,12},{9,13},{10,... | collective-permute-start | bytes 331784 | tf_op jit(solution)/shard_map/ppermute | solution.py:509
  60.5 0.0 collective-permute-start.13
  60.5 0.0 collective-permute-done.17
  60.5 2.4 %collective-permute-start.14 = (bf16[432,128]{1,0:T(8,128)(2,1)}, bf16[432,128]{1,0:T(8,128)(2,1)S(1)}, u32[]{:S(2)}, u32[]{:S(2)}) collective-permute-start(bf16[432,128]{1,0:T(8,128)(2,1)} %get-tuple-element.42), channel_id=1, source_target_pairs={{0,6},{1,7},{2,4},{3,5},{4,2},{5,3},{6,0},{7,1},{8,14},{9,15},{10,... | collective-permute-start | bytes 331784 | tf_op jit(solution)/shard_map/ppermute | solution.py:509
  62.9 0.9 %add_multiply_fusion = f32[144,1152]{1,0:T(8,128)} fusion(bf16[144,1152]{1,0:T(8,128)(2,1)S(1)} %collective-permute-done.17, bf16[144,1152]{1,0:T(8,128)(2,1)S(1)} %reduce-precision_convert_fusion), kind=kLoop, calls=%fused_computation | loop fusion | flops 663552 | bytes 1327104 | tf_op jit(solution)/shard_map/mul | solution.py:504
  63.8 0.0 collective-permute-done.10.refs_1_
  63.8 2.4 %collective-permute-start.15 = (bf16[432,128]{1,0:T(8,128)(2,1)}, bf16[432,128]{1,0:T(8,128)(2,1)S(1)}, u32[]{:S(2)}, u32[]{:S(2)}) collective-permute-start(bf16[432,128]{1,0:T(8,128)(2,1)} %get-tuple-element.43), channel_id=1, source_target_pairs={{0,2},{1,3},{2,0},{3,1},{4,6},{5,7},{6,4},{7,5},{8,10},{9,11},{10,... | collective-permute-start | bytes 331784 | tf_op jit(solution)/shard_map/ppermute | solution.py:509
  66.2 0.0 collective-permute-done.11.refs_2_
  66.2 1.5 %collective-permute-start.18 = (bf16[432,128]{1,0:T(8,128)(2,1)}, bf16[432,128]{1,0:T(8,128)(2,1)S(1)}, u32[]{:S(2)}, u32[]{:S(2)}) collective-permute-start(bf16[432,128]{1,0:T(8,128)(2,1)} %get-tuple-element.46), channel_id=1, source_target_pairs={{0,1},{1,0},{2,3},{3,2},{4,5},{5,4},{6,7},{7,6},{8,9},{9,8},{10,11... | collective-permute-start | bytes 331784 | tf_op jit(solution)/shard_map/ppermute | solution.py:509
  67.8 0.0 collective-permute-done.12.refs_3_
  67.8 9.2 %collective-permute-done.13.refs_4_ = bf16[432,128]{1,0:T(8,128)(2,1)S(1)} collective-permute-done((bf16[432,128]{1,0:T(8,128)(2,1)}, bf16[432,128]{1,0:T(8,128)(2,1)S(1)}, u32[]{:S(2)}, u32[]{:S(2)}) %collective-permute-start.13) | collective-permute-done | bytes 110624 | tf_op jit(solution)/shard_map/ppermute | solution.py:509
  77.0 2.3 %collective-permute-done.14.refs_5_ = bf16[432,128]{1,0:T(8,128)(2,1)S(1)} collective-permute-done((bf16[432,128]{1,0:T(8,128)(2,1)}, bf16[432,128]{1,0:T(8,128)(2,1)S(1)}, u32[]{:S(2)}, u32[]{:S(2)}) %collective-permute-start.14) | collective-permute-done | bytes 110624 | tf_op jit(solution)/shard_map/ppermute | solution.py:509
  79.3 0.0 collective-permute-done.15.refs_6_
  79.3 0.0 collective-permute-done.18.refs_7_
  79.3 1.5 %shard_map.97 = (f32[128,1152]{1,0:T(8,128)}, f32[128,1152]{1,0:T(8,128)}, f32[128,1152]{1,0:T(8,128)}) custom-call(bf16[432,128]{1,0:T(8,128)(2,1)S(1)} %get-tuple-element.37.refs_0_, bf16[432,128]{1,0:T(8,128)(2,1)S(1)} %collective-permute-done.10.refs_1_, bf16[432,128]{1,0:T(8,128)(2,1)S(1)} %collective-permute-done.11.refs_2_, ...), custom_call_target="tpu_custom_call" | custom-call | tf_op jit(solution)/shard_map/pallas_call | solution.py:511
  (7 shorter events, 0.1 us)
Async XLA Ops:
  0.6 8.2 %collective-permute-start = (bf16[128,1152]{1,0:T(8,128)(2,1)}, bf16[128,1152]{1,0:T(8,128)(2,1)S(1)}, u32[]{:S(2)}, u32[]{:S(2)}) collective-permute-start(bf16[128,1152]{1,0:T(8,128)(2,1)} %bitcast.7), channel_id=1, source_target_pairs={{0,2},{1,3},{2,0},{3,1},{4,6},{5,7},{6,4},{7,5},{8,10},{9,11},{10,... | collective-permute-start | bytes 884744 | tf_op jit(solution)/shard_map/ppermute | solution.py:426
  2.0 7.8 %collective-permute-start.1 = (bf16[128,1152]{1,0:T(8,128)(2,1)}, bf16[128,1152]{1,0:T(8,128)(2,1)S(1)}, u32[]{:S(2)}, u32[]{:S(2)}) collective-permute-start(bf16[128,1152]{1,0:T(8,128)(2,1)} %bitcast.8), channel_id=1, source_target_pairs={{0,1},{1,0},{2,4},{3,5},{4,2},{5,3},{6,7},{7,6},{8,9},{9,8},{10,12... | collective-permute-start | bytes 884744 | tf_op jit(solution)/shard_map/ppermute | solution.py:426
  8.8 29.7 %copy-start.4 = (bf16[128,1152]{1,0:T(8,128)(2,1)}, bf16[128,1152]{1,0:T(8,128)(2,1)S(1)}, u32[]{:S(2)}) copy-start(bf16[128,1152]{1,0:T(8,128)(2,1)S(1)} %collective-permute-done.refs_1_) | copy-start | bytes 884740
  8.8 7.0 %collective-permute-start.2 = (bf16[128,1152]{1,0:T(8,128)(2,1)S(1)}, bf16[128,1152]{1,0:T(8,128)(2,1)S(1)}, u32[]{:S(2)}, u32[]{:S(2)}) collective-permute-start(bf16[128,1152]{1,0:T(8,128)(2,1)S(1)} %collective-permute-done.refs_1_), channel_id=1, source_target_pairs={{0,1},{1,0},{2,4},{3,5},{4,2},{5,3},{6,7},{7,6},{8,9},{9,8},{10,12... | collective-permute-start | bytes 884744 | tf_op jit(solution)/shard_map/ppermute | solution.py:426
  9.8 28.7 %copy-start.2 = (bf16[128,1152]{1,0:T(8,128)(2,1)}, bf16[128,1152]{1,0:T(8,128)(2,1)S(1)}, u32[]{:S(2)}) copy-start(bf16[128,1152]{1,0:T(8,128)(2,1)S(1)} %collective-permute-done.1.refs_2_) | copy-start | bytes 884740
  9.8 9.0 %collective-permute-start.3 = (bf16[128,1152]{1,0:T(8,128)(2,1)S(1)}, bf16[128,1152]{1,0:T(8,128)(2,1)S(1)}, u32[]{:S(2)}, u32[]{:S(2)}) collective-permute-start(bf16[128,1152]{1,0:T(8,128)(2,1)S(1)} %collective-permute-done.1.refs_2_), channel_id=1, source_target_pairs={{0,2},{1,3},{2,0},{3,1},{4,6},{5,7},{6,4},{7,5},{8,10},{9,11},{10,... | collective-permute-start | bytes 884744 | tf_op jit(solution)/shard_map/ppermute | solution.py:426
  11.3 27.2 %all-to-all-start = ((bf16[8,432,128]{2,1,0:T(8,128)(2,1)}), bf16[8,432,128]{2,1,0:T(8,128)(2,1)S(1)}, u32[]{:S(2)}, u32[]{:S(2)}) async-start(bf16[8,432,128]{2,1,0:T(8,128)(2,1)} %shard_map.93), calls=%async_computation | async-start | bytes 1769472 | tf_op jit(solution)/shard_map/all_to_all | solution.py:466
  15.7 22.8 %copy-start = (bf16[128,1152]{1,0:T(8,128)(2,1)}, bf16[128,1152]{1,0:T(8,128)(2,1)S(1)}, u32[]{:S(2)}) copy-start(bf16[128,1152]{1,0:T(8,128)(2,1)S(1)} %collective-permute-done.2.refs_3_) | copy-start | bytes 884740
  15.8 16.8 %collective-permute-start.4 = (bf16[32,1152]{1,0:T(8,128)(2,1)S(1)}, bf16[32,1152]{1,0:T(8,128)(2,1)S(1)}, u32[]{:S(2)}, u32[]{:S(2)}) collective-permute-start(bf16[32,1152]{1,0:T(8,128)(2,1)S(1)} %get-tuple-element.53), channel_id=1, source_target_pairs={{0,2},{1,3},{2,0},{3,1},{4,6},{5,7},{6,4},{7,5},{8,10},{9,11},{10,... | collective-permute-start | bytes 221192 | tf_op jit(solution)/shard_map/ppermute | solution.py:426
  17.1 17.0 %collective-permute-start.5 = (bf16[32,1152]{1,0:T(8,128)(2,1)S(1)}, bf16[32,1152]{1,0:T(8,128)(2,1)S(1)}, u32[]{:S(2)}, u32[]{:S(2)}) collective-permute-start(bf16[32,1152]{1,0:T(8,128)(2,1)S(1)} %get-tuple-element.52), channel_id=1, source_target_pairs={{0,2},{1,3},{2,0},{3,1},{4,6},{5,7},{6,4},{7,5},{8,10},{9,11},{10,... | collective-permute-start | bytes 221192 | tf_op jit(solution)/shard_map/ppermute | solution.py:426
  17.3 18.4 %collective-permute-start.6 = (bf16[32,1152]{1,0:T(8,128)(2,1)S(1)}, bf16[32,1152]{1,0:T(8,128)(2,1)S(1)}, u32[]{:S(2)}, u32[]{:S(2)}) collective-permute-start(bf16[32,1152]{1,0:T(8,128)(2,1)S(1)} %get-tuple-element.51), channel_id=1, source_target_pairs={{0,2},{1,3},{2,0},{3,1},{4,6},{5,7},{6,4},{7,5},{8,10},{9,11},{10,... | collective-permute-start | bytes 221192 | tf_op jit(solution)/shard_map/ppermute | solution.py:426
  18.6 18.7 %collective-permute-start.7 = (bf16[32,1152]{1,0:T(8,128)(2,1)S(1)}, bf16[32,1152]{1,0:T(8,128)(2,1)S(1)}, u32[]{:S(2)}, u32[]{:S(2)}) collective-permute-start(bf16[32,1152]{1,0:T(8,128)(2,1)S(1)} %get-tuple-element.50), channel_id=1, source_target_pairs={{0,2},{1,3},{2,0},{3,1},{4,6},{5,7},{6,4},{7,5},{8,10},{9,11},{10,... | collective-permute-start | bytes 221192 | tf_op jit(solution)/shard_map/ppermute | solution.py:426
  18.8 19.7 %copy-start.3 = (bf16[128,1152]{1,0:T(8,128)(2,1)}, bf16[128,1152]{1,0:T(8,128)(2,1)S(1)}, u32[]{:S(2)}) copy-start(bf16[128,1152]{1,0:T(8,128)(2,1)S(1)} %collective-permute-done.3.refs_4_) | copy-start | bytes 884740
  18.8 26.3 %collective-permute-start.8 = (bf16[128,1152]{1,0:T(8,128)(2,1)S(1)}, bf16[128,1152]{1,0:T(8,128)(2,1)S(1)}, u32[]{:S(2)}, u32[]{:S(2)}) collective-permute-start(bf16[128,1152]{1,0:T(8,128)(2,1)S(1)} %broadcast_select_fusion.1), channel_id=1, source_target_pairs={{0,1},{1,0},{2,3},{3,2},{4,5},{5,4},{6,7},{7,6},{8,9},{9,8},{10,11... | collective-permute-start | bytes 884744 | tf_op jit(solution)/shard_map/ppermute | solution.py:426
  37.3 1.2 %copy-start.1 = (bf16[128,1152]{1,0:T(8,128)(2,1)}, bf16[128,1152]{1,0:T(8,128)(2,1)S(1)}, u32[]{:S(2)}) copy-start(bf16[128,1152]{1,0:T(8,128)(2,1)S(1)} %constant_dynamic-update-slice_fusion.refs_5_) | copy-start | bytes 884740
  37.4 7.8 %collective-permute-start.9 = (bf16[128,1152]{1,0:T(8,128)(2,1)S(1)}, bf16[128,1152]{1,0:T(8,128)(2,1)S(1)}, u32[]{:S(2)}, u32[]{:S(2)}) collective-permute-start(bf16[128,1152]{1,0:T(8,128)(2,1)S(1)} %broadcast_select_fusion), channel_id=1, source_target_pairs={{0,1},{1,0},{2,3},{3,2},{4,5},{5,4},{6,7},{7,6},{8,9},{9,8},{10,11... | collective-permute-start | bytes 884744 | tf_op jit(solution)/shard_map/ppermute | solution.py:426
  45.5 3.9 %collective-permute-start.16 = (bf16[144,1152]{1,0:T(8,128)(2,1)S(1)}, bf16[144,1152]{1,0:T(8,128)(2,1)S(1)}, u32[]{:S(2)}, u32[]{:S(2)}) collective-permute-start(bf16[144,1152]{1,0:T(8,128)(2,1)S(1)} %shard_map.96), channel_id=1, source_target_pairs={{0,8},{8,0},{16,24},{24,16},{1,9},{9,1},{17,25},{25,17},{2,10},{10... | collective-permute-start | bytes 995336 | tf_op jit(solution)/shard_map/ppermute | solution.py:501
  49.4 11.1 %collective-permute-start.17 = (bf16[144,1152]{1,0:T(8,128)(2,1)S(1)}, bf16[144,1152]{1,0:T(8,128)(2,1)S(1)}, u32[]{:S(2)}, u32[]{:S(2)}) collective-permute-start(bf16[144,1152]{1,0:T(8,128)(2,1)S(1)} %reduce-precision_convert_fusion), channel_id=1, source_target_pairs={{0,16},{8,24},{16,0},{24,8},{1,17},{9,25},{17,1},{25,9},{2,18},{10... | collective-permute-start | bytes 995336 | tf_op jit(solution)/shard_map/ppermute | solution.py:501
  56.4 7.5 %collective-permute-start.10 = (bf16[432,128]{1,0:T(8,128)(2,1)}, bf16[432,128]{1,0:T(8,128)(2,1)S(1)}, u32[]{:S(2)}, u32[]{:S(2)}) collective-permute-start(bf16[432,128]{1,0:T(8,128)(2,1)} %get-tuple-element.38), channel_id=1, source_target_pairs={{0,5},{1,4},{2,7},{3,6},{4,1},{5,0},{6,3},{7,2},{8,13},{9,12},{10,... | collective-permute-start | bytes 331784 | tf_op jit(solution)/shard_map/ppermute | solution.py:509
  56.8 9.4 %collective-permute-start.11 = (bf16[432,128]{1,0:T(8,128)(2,1)}, bf16[432,128]{1,0:T(8,128)(2,1)S(1)}, u32[]{:S(2)}, u32[]{:S(2)}) collective-permute-start(bf16[432,128]{1,0:T(8,128)(2,1)} %get-tuple-element.39), channel_id=1, source_target_pairs={{0,3},{1,2},{2,1},{3,0},{4,7},{5,6},{6,5},{7,4},{8,11},{9,10},{10,... | collective-permute-start | bytes 331784 | tf_op jit(solution)/shard_map/ppermute | solution.py:509
  59.0 8.8 %collective-permute-start.12 = (bf16[432,128]{1,0:T(8,128)(2,1)}, bf16[432,128]{1,0:T(8,128)(2,1)S(1)}, u32[]{:S(2)}, u32[]{:S(2)}) collective-permute-start(bf16[432,128]{1,0:T(8,128)(2,1)} %get-tuple-element.40), channel_id=1, source_target_pairs={{0,4},{1,5},{2,6},{3,7},{4,0},{5,1},{6,2},{7,3},{8,12},{9,13},{10,... | collective-permute-start | bytes 331784 | tf_op jit(solution)/shard_map/ppermute | solution.py:509
  60.5 16.5 %collective-permute-start.13 = (bf16[432,128]{1,0:T(8,128)(2,1)}, bf16[432,128]{1,0:T(8,128)(2,1)S(1)}, u32[]{:S(2)}, u32[]{:S(2)}) collective-permute-start(bf16[432,128]{1,0:T(8,128)(2,1)} %get-tuple-element.41), channel_id=1, source_target_pairs={{0,7},{1,6},{2,5},{3,4},{4,3},{5,2},{6,1},{7,0},{8,15},{9,14},{10,... | collective-permute-start | bytes 331784 | tf_op jit(solution)/shard_map/ppermute | solution.py:509
  60.5 18.8 %collective-permute-start.14 = (bf16[432,128]{1,0:T(8,128)(2,1)}, bf16[432,128]{1,0:T(8,128)(2,1)S(1)}, u32[]{:S(2)}, u32[]{:S(2)}) collective-permute-start(bf16[432,128]{1,0:T(8,128)(2,1)} %get-tuple-element.42), channel_id=1, source_target_pairs={{0,6},{1,7},{2,4},{3,5},{4,2},{5,3},{6,0},{7,1},{8,14},{9,15},{10,... | collective-permute-start | bytes 331784 | tf_op jit(solution)/shard_map/ppermute | solution.py:509
  63.8 15.4 %collective-permute-start.15 = (bf16[432,128]{1,0:T(8,128)(2,1)}, bf16[432,128]{1,0:T(8,128)(2,1)S(1)}, u32[]{:S(2)}, u32[]{:S(2)}) collective-permute-start(bf16[432,128]{1,0:T(8,128)(2,1)} %get-tuple-element.43), channel_id=1, source_target_pairs={{0,2},{1,3},{2,0},{3,1},{4,6},{5,7},{6,4},{7,5},{8,10},{9,11},{10,... | collective-permute-start | bytes 331784 | tf_op jit(solution)/shard_map/ppermute | solution.py:509
  66.2 13.0 %collective-permute-start.18 = (bf16[432,128]{1,0:T(8,128)(2,1)}, bf16[432,128]{1,0:T(8,128)(2,1)S(1)}, u32[]{:S(2)}, u32[]{:S(2)}) collective-permute-start(bf16[432,128]{1,0:T(8,128)(2,1)} %get-tuple-element.46), channel_id=1, source_target_pairs={{0,1},{1,0},{2,3},{3,2},{4,5},{5,4},{6,7},{7,6},{8,9},{9,8},{10,11... | collective-permute-start | bytes 331784 | tf_op jit(solution)/shard_map/ppermute | solution.py:509
